TPU v7x, 128 devices: a whole 4x4x4 slice. The times are simulated.
128 devices in a mesh: prompt: 4 (over x), sample: 32 (over y, z, core).
Axes of the slice: x: 4, y: 4, z: 4, core: 2. Of those that a mesh axis runs over, the one named last changes fastest.
Arguments:
- embeddings: bfloat16 [128, 512, 1024], P(('prompt', 'sample')), parts along dimension 0
- lengths: int32 [128], P(('prompt', 'sample')), parts along dimension 0, may hold values from 32 to 512, as said below
Outputs:
- precision: float32 [128, 32], P(('prompt', 'sample')), parts along dimension 0
- utility: float32 [128], P(('prompt', 'sample')), parts along dimension 0
There are 4 independent parts, one for each index of `prompt`. A program takes and returns all parts, laid end to end along the dimension named above; each array names one. Nothing has to cross between parts.
Inputs may be any that keep to these rules, and one draw needn't show every extreme that they name: `lengths`: some sample of the prompt has exactly 512 tokens.
All inputs are finite; a program needn't handle non-finite values.
Results may differ from a plain program's by a relative error of at most 0.0007.
Values may be sent and summed in bfloat16 or wider, within the bound.
No kernel may reach another device: no remote copies, remote signals or barrier semaphores. Data moves between devices by JAX's collectives and lax.ppermute only.
A program may use at most 128 MiB of HBM per device.

v0:
```python
import jax
import jax.numpy as jnp
from jax import lax
from jax.sharding import PartitionSpec as P


def tile_pairs(own, own_len, other, other_len):
    similar = jnp.einsum("aie,bje->abij", own, other, preferred_element_type=jnp.float32)
    places = jnp.arange(own.shape[1], dtype=jnp.int32)
    own_ok = places[None, :] < own_len[:, None]
    other_ok = places[None, :] < other_len[:, None]
    masked = jnp.where(other_ok[None, :, None, :], similar, jnp.float32(-4.0))
    best_row = jnp.max(masked, axis=3)
    forward = jnp.sum(jnp.where(own_ok[:, None, :], best_row, jnp.float32(0.0)), axis=2)
    forward = forward / own_len[:, None].astype(jnp.float32)
    masked_col = jnp.where(own_ok[:, None, :, None], similar, jnp.float32(-4.0))
    best_col = jnp.max(masked_col, axis=2)
    backward = jnp.sum(jnp.where(other_ok[None, :, :], best_col, jnp.float32(0.0)), axis=2)
    backward = backward / other_len[None, :].astype(jnp.float32)
    return (forward, backward)


def body(embeddings, lengths):
    values = embeddings.astype(jnp.float32)
    unit = (values / jnp.sqrt(jnp.sum(values * values, axis=2, keepdims=True) + 1e-06)).astype(
        jnp.bfloat16
    )
    devices = lax.axis_size("sample")
    here = lax.axis_index("sample")
    per_dev = unit.shape[0]
    total = per_dev * devices
    base = here * per_dev
    piece = lax.all_gather(unit, "sample", axis=0, tiled=True)
    piece_len = lax.all_gather(lengths, "sample", axis=0, tiled=True)
    ahead, behind = tile_pairs(unit, lengths, piece, piece_len)
    own_index = base + jnp.arange(per_dev, dtype=jnp.int32)
    offdiag = jnp.arange(total, dtype=jnp.int32)[None, :] != own_index[:, None]
    utility = jnp.sum(jnp.where(offdiag, ahead + behind, jnp.float32(0.0)), axis=1)
    utility = utility / jnp.float32(2 * (total - 1))
    return (ahead, utility)


def solution(mesh):
    in_specs = (P(("prompt", "sample"), None, None), P(("prompt", "sample")))
    out_specs = (P(("prompt", "sample"), None), P(("prompt", "sample")))
    return jax.shard_map(body, mesh=mesh, in_specs=in_specs, out_specs=out_specs, check_vma=False)
```

profile of v0, /device:TPU:0, one launch (start us, length us, event | category | flops | bytes accessed | tf_op | source)
XLA Modules:
  0.0 162.2 jit_solution(90192062204781523)
XLA Ops:
  7.2 0.0 all-gather.2.cloned.1.call-start
  7.2 1.5 fusion.2
  8.7 2.6 %fusion.3 = bf16[1,512,1024]{2,1,0:T(8,128)(2,1)} fusion(bf16[1,512,1024]{2,1,0:T(8,128)(2,1)} %param.2, f32[512]{0:T(512)S(1)} %add_sqrt_fusion), kind=kLoop, calls=%fused_computation.7 | loop fusion | flops 1572864 | bytes 2099200 | tf_op jit(solution)/shard_map/convert_element_type | solution.py:25
  11.3 0.0 all-gather.2.cloned.1.call-update
  12.0 1.2 dynamic-slice
  13.2 0.8 dynamic-update-slice
  14.0 18.4 %all-reduce = s32[32]{0:T(128)S(1)} all-reduce(s32[32]{0:T(128)S(1)} %dynamic-update-slice), channel_id=1, replica_groups=mesh['prompt'=4,'sample'=32] {'sample'}, use_global_device_ids=true, to_apply=%add | all-reduce | flops 32 | bytes 256
  32.3 0.1 iota_compare_fusion
  32.4 95.5 %all-gather.2.cloned.1.call-done = bf16[32,512,1024]{2,1,0:T(8,128)(2,1)} async-done(((bf16[1,512,1024]{2,1,0:T(8,128)(2,1)}), bf16[32,512,1024]{2,1,0:T(8,128)(2,1)}) %all-gather.2.cloned.1.call-update) | async-done | bytes 33554448 | tf_op jit(solution)/shard_map/all_gather | solution.py:33
  127.9 24.3 %fusion.1 = (f32[32,512]{1,0:T(8,128)S(1)}, f32[32,512]{1,0:T(8,128)S(1)}) fusion(pred[512]{0:T(512)(128)(4,1)S(1)} %iota_compare_fusion.1, pred[32,512]{1,0:T(8,128)(4,1)S(1)} %iota_compare_fusion, bf16[32,512,1024]{2,1,0:T(8,128)(2,1)} %all-gather.2.cloned.1.call-done, bf16[1,512,1024]{2,1,0:T(8,128)(2,1)} %fusion.3), kind=kOutput, calls=%fused_computation.3 | convolution fusion | flops 17213390848 | bytes 34750976 | tf_op jit(solution)/shard_map/aie,bje->abij/dot_general | solution.py:8
  152.2 0.2 select_reduce_fusion
  152.4 1.1 fusion.6
  (3 shorter events, 0.0 us)
Async XLA Ops:
  7.2 120.7 %all-gather.2.cloned.1.call-start = ((), (), s32[]{:S(2)}) async-start(), calls=%async_computation | async-start | bytes 34603008 | tf_op jit(solution)/shard_map/all_gather | solution.py:33
Sparse Core Ops, SparseCore 0:
  11.4 116.4 all-gather.1
where the time goes:
time: 164 us; the launch traced here: 162 us
  waiting for transfers between devices  95.5 us (58%)
  matrix products  24.3 us (15%)
  blocking collectives  18.4 us (11%)
  between operations  16.5 us (10%)
  other arithmetic  5.47 us (3%)
  local copies, waits for them, and re-layouts  2 us (1%)
    all_gather x1, waiting for transfers between devices, body(): piece = lax.all_gather(unit, 'sample', axis=0, tiled=True)  95.5 us
    dot_general x1, matrix products, tile_pairs(): jnp.einsum('aie,bje->abij', own, other, preferred_element_type=jnp.float32)  24.3 us
    unnamed x1, blocking collectives  18.4 us
  transfers between devices with their start and end apart: 1, of which 1 were waited for; matrix products, arithmetic and copies ran while one was open for 1% of the time, Pallas kernels for 0%

commit v1 on v0

v1 whole, which is shorter than its diff:
```python
import functools

import jax
import jax.numpy as jnp
import numpy as np
from jax import lax
from jax.experimental import pallas as pl
from jax.experimental.pallas import tpu as pltpu
from jax.sharding import PartitionSpec as P

N = 4
HALF = 256
TAG = 16


def device(y, z, core):
    return ((y % N) * N + z % N) * 2 + core % 2


def moves(dy, dz, dcore=0, flip=False):
    pairs = []
    for y in range(N):
        for z in range(N):
            for core in range(2):
                change = dcore + (1 if flip and (y + dy) % N >= N // 2 else 0)
                pairs.append((device(y, z, core), device(y + dy, z + dz, core + change)))
    return pairs


def shift(x, dy, dz, dcore=0, flip=False):
    return lax.ppermute(x, "sample", moves(dy, dz, dcore, flip))


def plan(here):
    y, z, core = here // (2 * N), here // 2 % N, here % 2
    low, left = int(y >= N // 2), int(z >= N // 2)

    def at(dy, dz, flip=0):
        return device(y + dy, z + dz, core + flip)

    own, sib, up, up_o, right, right_o = at(0, 0), at(0, 0, 1), at(1, 0), at(1, 0, 1), at(0, 1), at(0, 1, 1)
    far_y, far_z = at(2, 0), at(0, 2, low)
    columns = [
        (0, 0, own, own, 1, 0, 0),
        (0, 1, own, sib, 0, 2, 0),
        (2, 0, up, own, 3, 1, 1),
        (2, 1, up, sib, 0, 2, 1),
        (5, 0, right, own, 6, 0, 1),
        (5, 1, right, sib, 0, 0, 1),
        (2, 5, up, right, 0, 0, 1),
        (2, 6, up, right_o, 0, 7, 1),
        (4, 5, at(-1, 0), right, 5, 0, 1),
        (4, 6, at(-1, 0), right_o, 0, 0, 1),
        (7, 5 + left, at(0, -1), at(0, 1, left), 8, 0, 1),
        (4, 2 + low, at(-1, 0), at(1, 0, low), 0, 4, 1),
        (0, 4, far_y, right, 1, 5, 1),
        (0, 5, far_y, right_o, 0, 6, 1),
        (1, 2, far_z, up, 2, 3, 1),
        (1, 3, far_z, up_o, 0, 4, 1),
        (0, 1, far_y, far_z, 0, 0, 1),
    ]
    return np.array(columns, np.int32).T


def unit_kernel(len_ref, emb_ref, head_ref, tail_ref):
    length = len_ref[0]
    first = None
    for start, out in ((0, head_ref), (HALF, tail_ref)):
        values = emb_ref[0, start : start + HALF, :].astype(jnp.float32)
        norm = jnp.sqrt(jnp.sum(values * values, axis=1, keepdims=True) + 1e-06)
        unit = values / norm
        if first is None:
            first = unit[0:1, :]
        places = lax.broadcasted_iota(jnp.int32, (HALF, 1), 0) + start
        out[0:HALF, :] = jnp.where(places < length, unit, first).astype(jnp.bfloat16)
    rows = lax.broadcasted_iota(jnp.int32, (TAG, head_ref.shape[1]), 0)
    tag = jnp.where(rows < TAG // 2, length // 16, length % 16)
    head_ref[HALF : HALF + TAG, :] = tag.astype(jnp.float32).astype(jnp.bfloat16)


def make_unit(lengths, embeddings):
    width = embeddings.shape[2]
    return pl.pallas_call(
        unit_kernel,
        out_shape=(
            jax.ShapeDtypeStruct((HALF + TAG, width), jnp.bfloat16),
            jax.ShapeDtypeStruct((HALF, width), jnp.bfloat16),
        ),
        in_specs=[
            pl.BlockSpec(memory_space=pltpu.SMEM),
            pl.BlockSpec(memory_space=pltpu.VMEM),
        ],
        out_specs=(
            pl.BlockSpec(memory_space=pltpu.VMEM),
            pl.BlockSpec(memory_space=pltpu.VMEM),
        ),
        compiler_params=pltpu.CompilerParams(vmem_limit_bytes=24 * 2**20),
        name="unit",
    )(lengths, embeddings)


def pairs_kernel(slots, base, count, tab_ref, before_ref, *refs):
    ins = refs[: 2 * slots]
    out_ref, tok, tag, sem = refs[2 * slots :]
    for s in range(slots):
        head, tail = ins[2 * s], ins[2 * s + 1]
        for c in (
            pltpu.make_async_copy(head.at[0:HALF, :], tok.at[s, 0:HALF, :], sem.at[s, 0]),
            pltpu.make_async_copy(tail.at[:, :], tok.at[s, HALF : 2 * HALF, :], sem.at[s, 1]),
            pltpu.make_async_copy(head.at[HALF : HALF + TAG, 0:128], tag.at[s], sem.at[s, 2]),
        ):
            c.start()

    def arrive(s):
        pltpu.make_async_copy(ins[0].at[0:HALF, :], tok.at[s, 0:HALF, :], sem.at[s, 0]).wait()
        pltpu.make_async_copy(ins[1].at[:, :], tok.at[s, HALF : 2 * HALF, :], sem.at[s, 1]).wait()
        pltpu.make_async_copy(
            ins[0].at[HALF : HALF + TAG, 0:128], tag.at[s], sem.at[s, 2]
        ).wait()

    out_ref[...] = before_ref[...]
    owners = lax.broadcasted_iota(jnp.int32, out_ref.shape, 0)
    lanes = lax.broadcasted_iota(jnp.int32, out_ref.shape, 1)
    total = out_ref.shape[0]

    def length_of(s):
        value = tag[s].astype(jnp.float32)
        return (
            jnp.max(value[0 : TAG // 2]).astype(jnp.int32) * 16
            + jnp.max(value[TAG // 2 : TAG]).astype(jnp.int32)
        )

    @pl.loop(base, base + count)
    def _(k):
        u, v = tab_ref[0, k], tab_ref[1, k]

        for wait in (4, 5):

            @pl.when(tab_ref[wait, k] > 0)
            def _():
                arrive(tab_ref[wait, k] - 1)

        len_u, len_v = length_of(u), length_of(v)
        own, other = tab_ref[2, k], tab_ref[3, k]
        both = tab_ref[6, k]

        def score(rows, cols):
            right = tok[v, 0:cols, :]
            best_col = None
            ahead = jnp.zeros((1, 1), jnp.float32)
            for start in range(0, rows, HALF):
                similar = lax.dot_general(
                    tok[u, start : start + HALF, :],
                    right,
                    (((1,), (1,)), ((), ())),
                    preferred_element_type=jnp.float32,
                )
                best_row = jnp.max(similar, axis=1, keepdims=True)
                col = jnp.max(similar, axis=0, keepdims=True)
                best_col = col if best_col is None else jnp.maximum(best_col, col)
                places = lax.broadcasted_iota(jnp.int32, (HALF, 1), 0) + start
                ahead += jnp.sum(
                    jnp.where(places < len_u, best_row, 0.0), axis=0, keepdims=True
                )
            places = lax.broadcasted_iota(jnp.int32, (1, cols), 1)
            behind = jnp.sum(jnp.where(places < len_v, best_col, 0.0), axis=1, keepdims=True)
            ahead = ahead / len_u.astype(jnp.float32)
            behind = behind / len_v.astype(jnp.float32)
            at_u = owners == own
            at_v = (owners == other) & (both == 1)
            fore = (at_u & (lanes == other)) | (at_v & (lanes == total + own))
            back = (at_u & (lanes == total + other)) | (at_v & (lanes == own))
            out_ref[...] += jnp.where(fore, ahead, 0.0) + jnp.where(back, behind, 0.0)

        long_u, long_v = len_u > HALF, len_v > HALF
        for bu in (False, True):
            for bv in (False, True):

                @pl.when((long_u == bu) & (long_v == bv))
                def _():
                    score(2 * HALF if bu else HALF, 2 * HALF if bv else HALF)


def run_pairs(table, base, count, before, blocks, name):
    slots = len(blocks)
    width = blocks[0][0].shape[1]
    flops = 2 * count * (2 * HALF) ** 2 * width
    return pl.pallas_call(
        functools.partial(pairs_kernel, slots, base, count),
        out_shape=jax.ShapeDtypeStruct(before.shape, jnp.float32),
        in_specs=[
            pl.BlockSpec(memory_space=pltpu.SMEM),
            pl.BlockSpec(memory_space=pltpu.VMEM),
        ]
        + [pl.BlockSpec(memory_space=pl.ANY)] * (2 * slots),
        out_specs=pl.BlockSpec(memory_space=pltpu.VMEM),
        scratch_shapes=[
            pltpu.VMEM((slots, 2 * HALF, width), jnp.bfloat16),
            pltpu.VMEM((slots, TAG, 128), jnp.bfloat16),
            pltpu.SemaphoreType.DMA((slots, 3)),
        ],
        compiler_params=pltpu.CompilerParams(vmem_limit_bytes=40 * 2**20),
        cost_estimate=pl.CostEstimate(
            flops=flops, bytes_accessed=slots * 2 * 2 * HALF * width, transcendentals=0
        ),
        name=name,
    )(table, before, *[half for block in blocks for half in block])


def body(embeddings, lengths):
    total = lax.axis_size("sample")
    here = lax.axis_index("sample")

    head, tail = make_unit(lengths, embeddings)
    my_h = shift(head, 1, 0)
    mz_h = shift(head, 0, 1)
    py_t = shift(tail, -1, 0)
    pz_t = shift(tail, 0, -1)
    sib_h = shift(head, 0, 0, 1)
    sib_t = shift(tail, 0, 0, 1)
    my_t = shift(tail, 1, 0)
    mz_t = shift(tail, 0, 1)
    py_h = shift(head, -1, 0)
    pz_h = shift(head, 0, -1)
    x_h = shift(my_h, 1, 0)
    y_h = shift(mz_h, 0, 1, flip=True)
    x_t = shift(py_t, -1, 0)
    y_t = shift(pz_t, 0, -1, flip=True)
    pyo_t = shift(py_t, 0, 0, 1)
    pzo_t = shift(pz_t, 0, 0, 1)
    pyo_h = shift(py_h, 0, 0, 1)
    pzo_h = shift(pz_h, 0, 0, 1)

    own = (head, tail)
    sib = (sib_h, sib_t)
    py, pyo, my = (py_h, py_t), (pyo_h, pyo_t), (my_h, my_t)
    pz, pzo, mz = (pz_h, pz_t), (pzo_h, pzo_t), (mz_h, mz_t)
    far_y, far_z = (x_h, x_t), (y_h, y_t)

    table = jnp.asarray(np.stack([plan(i) for i in range(total)]))[here]
    scores = jnp.zeros((total, 128), jnp.float32)
    scores = run_pairs(table, 0, 2, scores, [own, sib], "near_pairs")
    scores = run_pairs(
        table, 2, 10, scores, [own, sib, py, pyo, my, pz, pzo, mz], "mid_pairs"
    )
    scores = run_pairs(table, 12, 5, scores, [far_y, far_z, py, pyo, pz, pzo], "far_pairs")

    parts = lax.all_to_all(scores, "sample", 0, 0, tiled=True)
    mine = jnp.sum(parts, axis=0)
    ahead, behind = mine[:total], mine[total : 2 * total]
    offdiag = jnp.arange(total, dtype=jnp.int32) != here
    utility = jnp.sum(jnp.where(offdiag, ahead + behind, 0.0)) / jnp.float32(2 * (total - 1))
    return ahead[None, :], utility[None]


def solution(mesh):
    in_specs = (P(("prompt", "sample"), None, None), P(("prompt", "sample")))
    out_specs = (P(("prompt", "sample"), None), P(("prompt", "sample")))
    return jax.shard_map(body, mesh=mesh, in_specs=in_specs, out_specs=out_specs, check_vma=False)
```

time: 164 us -> 87.3 us (0.53)
  the two profiles are of different devices: /device:TPU:0 before, /device:TPU:5 now
where the time goes in v1:
time: 87.3 us; the launch traced here: 87.2 us
  starting transfers between devices  23 us (26%)
  blocking collectives  19.5 us (22%)
  Pallas kernels  17.6 us (20%)
  waiting for transfers between devices  15.6 us (18%)
  local copies, waits for them, and re-layouts  7.2 us (8%)
  between operations  3.18 us (4%)
  other arithmetic  1.16 us (1%)
    ppermute x18, starting transfers between devices, shift(): return lax.ppermute(x, 'sample', moves(dy, dz, dcore, flip))  23 us
    all_to_all x1, blocking collectives, body(): parts = lax.all_to_all(scores, 'sample', 0, 0, tiled=True)  19.5 us
    pallas_call x3, Pallas kernels, run_pairs(): pl.pallas_call(functools.partial(pairs_kernel, slots, base, count), out_s...  17.2 us
    ppermute x18, waiting for transfers between devices, shift(): return lax.ppermute(x, 'sample', moves(dy, dz, dcore, flip))  15.6 us
    unnamed x20, local copies, waits for them, and re-layouts  6.52 us
  transfers between devices with their start and end apart: 18, of which 6 were waited for; matrix products, arithmetic and copies ran while one was open for 1% of the time, Pallas kernels for 13%

profile of v1, /device:TPU:5, one launch (start us, length us, event | category | flops | bytes accessed | tf_op | source)
XLA Modules:
  0.0 87.2 jit_solution(4334551342100425721)
XLA Ops:
  1.3 0.0 copy-start
  1.3 1.2 %copy-done = bf16[1,512,1024]{2,1,0:T(8,128)(2,1)S(1)} copy-done((bf16[1,512,1024]{2,1,0:T(8,128)(2,1)S(1)}, bf16[1,512,1024]{2,1,0:T(8,128)(2,1)}, u32[]{:S(2)}) %copy-start) | copy-done | bytes 1048600
  2.5 0.5 unit.1
  3.0 0.8 collective-permute-start.1
  3.7 3.8 %collective-permute-start.9 = (bf16[256,1024]{1,0:T(8,128)(2,1)S(1)}, bf16[256,1024]{1,0:T(8,128)(2,1)}, u32[]{:S(2)}, u32[]{:S(2)}) collective-permute-start(bf16[256,1024]{1,0:T(8,128)(2,1)S(1)} %get-tuple-element.5.refs_1_), channel_id=1, source_target_pairs={{0,6},{1,7},{2,0},{3,1},{4,2},{5,3},{6,4},{7,5},{8,14},{9,15},{10,... | collective-permute-start | bytes 1572872 | tf_op jit(solution)/shard_map/ppermute | solution.py:31
  7.5 2.7 %collective-permute-start.3 = (bf16[256,1024]{1,0:T(8,128)(2,1)S(1)}, bf16[256,1024]{1,0:T(8,128)(2,1)}, u32[]{:S(2)}, u32[]{:S(2)}) collective-permute-start(bf16[256,1024]{1,0:T(8,128)(2,1)S(1)} %get-tuple-element.5.refs_1_), channel_id=1, source_target_pairs={{0,24},{1,25},{2,26},{3,27},{4,28},{5,29},{6,30},{7,31},{8,0},{9,1... | collective-permute-start | bytes 1572872 | tf_op jit(solution)/shard_map/ppermute | solution.py:31
  10.2 0.0 collective-permute-start.13
  10.3 2.7 %collective-permute-start.8 = (bf16[272,1024]{1,0:T(8,128)(2,1)S(1)}, bf16[272,1024]{1,0:T(8,128)(2,1)S(1)}, u32[]{:S(2)}, u32[]{:S(2)}) collective-permute-start(bf16[272,1024]{1,0:T(8,128)(2,1)S(1)} %get-tuple-element.4.refs_0_), channel_id=1, source_target_pairs={{0,6},{1,7},{2,0},{3,1},{4,2},{5,3},{6,4},{7,5},{8,14},{9,15},{10,... | collective-permute-start | bytes 1671176 | tf_op jit(solution)/shard_map/ppermute | solution.py:31
  12.9 0.0 collective-permute-done.1.refs_3_
  12.9 0.0 copy-start.3
  12.9 0.8 copy-done.3
  13.7 0.0 collective-permute-start.7
  13.7 0.0 copy-start.1
  13.7 0.8 copy-done.1
  14.5 4.2 %collective-permute-done.9.refs_11_.refs_9_ = bf16[256,1024]{1,0:T(8,128)(2,1)} collective-permute-done((bf16[256,1024]{1,0:T(8,128)(2,1)S(1)}, bf16[256,1024]{1,0:T(8,128)(2,1)}, u32[]{:S(2)}, u32[]{:S(2)}) %collective-permute-start.9) | collective-permute-done | bytes 524320 | tf_op jit(solution)/shard_map/ppermute | solution.py:31
  18.8 1.3 %collective-permute-start = (bf16[272,1024]{1,0:T(8,128)(2,1)S(1)}, bf16[272,1024]{1,0:T(8,128)(2,1)S(1)}, u32[]{:S(2)}, u32[]{:S(2)}) collective-permute-start(bf16[272,1024]{1,0:T(8,128)(2,1)S(1)} %get-tuple-element.4.refs_0_), channel_id=1, source_target_pairs={{0,1},{1,0},{2,3},{3,2},{4,5},{5,4},{6,7},{7,6},{8,9},{9,8},{10,11... | collective-permute-start | bytes 1671176 | tf_op jit(solution)/shard_map/ppermute | solution.py:31
  20.1 1.1 %collective-permute-done.3.refs_5_ = bf16[256,1024]{1,0:T(8,128)(2,1)} collective-permute-done((bf16[256,1024]{1,0:T(8,128)(2,1)S(1)}, bf16[256,1024]{1,0:T(8,128)(2,1)}, u32[]{:S(2)}, u32[]{:S(2)}) %collective-permute-start.3) | collective-permute-done | bytes 524320 | tf_op jit(solution)/shard_map/ppermute | solution.py:31
  21.2 3.5 %collective-permute-start.2 = (bf16[272,1024]{1,0:T(8,128)(2,1)S(1)}, bf16[272,1024]{1,0:T(8,128)(2,1)S(1)}, u32[]{:S(2)}, u32[]{:S(2)}) collective-permute-start(bf16[272,1024]{1,0:T(8,128)(2,1)S(1)} %get-tuple-element.4.refs_0_), channel_id=1, source_target_pairs={{0,24},{1,25},{2,26},{3,27},{4,28},{5,29},{6,30},{7,31},{8,0},{9,1... | collective-permute-start | bytes 1671176 | tf_op jit(solution)/shard_map/ppermute | solution.py:31
  24.7 0.0 collective-permute-done.13.refs_15_
  24.7 0.0 copy-start.6
  24.7 0.8 copy-done.6
  25.5 0.0 collective-permute-start.12
  25.5 1.6 %collective-permute-done.7.refs_9_ = bf16[256,1024]{1,0:T(8,128)(2,1)S(1)} collective-permute-done((bf16[256,1024]{1,0:T(8,128)(2,1)S(1)}, bf16[256,1024]{1,0:T(8,128)(2,1)S(1)}, u32[]{:S(2)}, u32[]{:S(2)}) %collective-permute-start.7) | collective-permute-done | bytes 524320 | tf_op jit(solution)/shard_map/ppermute | solution.py:31
  27.2 0.0 copy-start.8
  27.2 0.8 copy-done.8
  28.0 0.0 collective-permute-start.6
  28.0 2.8 %collective-permute-done.8.refs_10_.refs_8_ = bf16[272,1024]{1,0:T(8,128)(2,1)S(1)} collective-permute-done((bf16[272,1024]{1,0:T(8,128)(2,1)S(1)}, bf16[272,1024]{1,0:T(8,128)(2,1)S(1)}, u32[]{:S(2)}, u32[]{:S(2)}) %collective-permute-start.8) | collective-permute-done | bytes 557088 | tf_op jit(solution)/shard_map/ppermute | solution.py:31
  30.7 0.9 collective-permute-start.10
  31.6 0.0 collective-permute-done.refs_2_
  31.6 0.0 collective-permute-start.11
  31.6 3.9 %collective-permute-done.2.refs_4_ = bf16[272,1024]{1,0:T(8,128)(2,1)S(1)} collective-permute-done((bf16[272,1024]{1,0:T(8,128)(2,1)S(1)}, bf16[272,1024]{1,0:T(8,128)(2,1)S(1)}, u32[]{:S(2)}, u32[]{:S(2)}) %collective-permute-start.2) | collective-permute-done | bytes 557088 | tf_op jit(solution)/shard_map/ppermute | solution.py:31
  35.5 2.1 %collective-permute-start.5 = (bf16[256,1024]{1,0:T(8,128)(2,1)}, bf16[256,1024]{1,0:T(8,128)(2,1)}, u32[]{:S(2)}, u32[]{:S(2)}) collective-permute-start(bf16[256,1024]{1,0:T(8,128)(2,1)} %collective-permute-done.3.refs_5_), channel_id=1, source_target_pairs={{0,1},{1,0},{2,3},{3,2},{4,5},{5,4},{6,7},{7,6},{8,9},{9,8},{10,11... | collective-permute-start | bytes 1572872 | tf_op jit(solution)/shard_map/ppermute | solution.py:31
  37.6 2.0 %collective-permute-done.12.refs_14_ = bf16[272,1024]{1,0:T(8,128)(2,1)S(1)} collective-permute-done((bf16[272,1024]{1,0:T(8,128)(2,1)S(1)}, bf16[272,1024]{1,0:T(8,128)(2,1)S(1)}, u32[]{:S(2)}, u32[]{:S(2)}) %collective-permute-start.12) | collective-permute-done | bytes 557088 | tf_op jit(solution)/shard_map/ppermute | solution.py:31
  39.5 2.3 %collective-permute-start.4 = (bf16[272,1024]{1,0:T(8,128)(2,1)S(1)}, bf16[272,1024]{1,0:T(8,128)(2,1)}, u32[]{:S(2)}, u32[]{:S(2)}) collective-permute-start(bf16[272,1024]{1,0:T(8,128)(2,1)S(1)} %collective-permute-done.2.refs_4_), channel_id=1, source_target_pairs={{0,1},{1,0},{2,3},{3,2},{4,5},{5,4},{6,7},{7,6},{8,9},{9,8},{10,11... | collective-permute-start | bytes 1671176 | tf_op jit(solution)/shard_map/ppermute | solution.py:31
  41.8 0.7 dynamic-slice_bitcast_fusion.tab_ref
  42.5 0.0 collective-permute-done.6.refs_8_
  42.5 0.1 collective-permute-start.15
  42.6 0.0 collective-permute-done.11.refs_13_.refs_11_
  42.6 0.8 collective-permute-start.17
  43.4 0.0 collective-permute-done.5.refs_7_
  43.4 1.0 %collective-permute-start.14 = (bf16[272,1024]{1,0:T(8,128)(2,1)}, bf16[272,1024]{1,0:T(8,128)(2,1)S(1)}, u32[]{:S(2)}, u32[]{:S(2)}) collective-permute-start(bf16[272,1024]{1,0:T(8,128)(2,1)} %collective-permute-done.6.refs_8_), channel_id=1, source_target_pairs={{0,8},{1,9},{2,10},{3,11},{4,12},{5,13},{6,14},{7,15},{8,16},{9,17... | collective-permute-start | bytes 1671176 | tf_op jit(solution)/shard_map/ppermute | solution.py:31
  44.4 0.0 collective-permute-done.10.refs_12_.refs_10_
  44.4 1.0 %collective-permute-start.16 = (bf16[272,1024]{1,0:T(8,128)(2,1)S(1)}, bf16[272,1024]{1,0:T(8,128)(2,1)S(1)}, u32[]{:S(2)}, u32[]{:S(2)}) collective-permute-start(bf16[272,1024]{1,0:T(8,128)(2,1)S(1)} %collective-permute-done.12.refs_14_), channel_id=1, source_target_pairs={{0,2},{1,3},{2,4},{3,5},{4,6},{5,7},{6,0},{7,1},{8,10},{9,11},{10,... | collective-permute-start | bytes 1671176 | tf_op jit(solution)/shard_map/ppermute | solution.py:31
  45.4 0.0 copy-start.2
  45.4 1.0 %copy-done.2 = bf16[256,1024]{1,0:T(8,128)(2,1)S(1)} copy-done((bf16[256,1024]{1,0:T(8,128)(2,1)S(1)}, bf16[256,1024]{1,0:T(8,128)(2,1)}, u32[]{:S(2)}) %copy-start.2) | copy-done | bytes 524312
  46.5 0.0 copy-start.4
  46.5 1.0 %copy-done.4 = bf16[256,1024]{1,0:T(8,128)(2,1)S(1)} copy-done((bf16[256,1024]{1,0:T(8,128)(2,1)S(1)}, bf16[256,1024]{1,0:T(8,128)(2,1)}, u32[]{:S(2)}) %copy-start.4) | copy-done | bytes 524312
  47.5 0.0 copy-start.5
  47.5 0.0 copy-start.7
  47.5 0.0 copy-start.9
  47.5 2.1 %near_pairs.1.before_ref = f32[32,128]{1,0:T(8,128)S(1)} custom-call(s32[7,17]{1,0:T(8,128)S(1)} %dynamic-slice_bitcast_fusion.tab_ref, f32[32,128]{1,0:T(8,128)S(1)} %broadcast_in_dim.13.before_ref, bf16[272,1024]{1,0:T(8,128)(2,1)S(1)} %get-tuple-element.4.refs_0_, bf16[256,1024]{1,0:T(8,128)(2,1)S(1)} %copy-done.2, ...), custom_call_target="tpu_custom_call" | custom-call | flops 1073741824 | bytes 2097152 | tf_op jit(solution)/shard_map/near_pairs/pallas_call | solution.py:188
  49.7 0.0 collective-permute-done.4.refs_6_
  49.7 0.0 copy-done.5
  49.7 0.0 copy-done.7
  49.7 0.0 copy-done.9
  49.7 9.0 %mid_pairs.1.before_ref = f32[32,128]{1,0:T(8,128)S(1)} custom-call(s32[7,17]{1,0:T(8,128)S(1)} %dynamic-slice_bitcast_fusion.tab_ref, f32[32,128]{1,0:T(8,128)S(1)} %near_pairs.1.before_ref, bf16[272,1024]{1,0:T(8,128)(2,1)S(1)} %get-tuple-element.4.refs_0_, bf16[256,1024]{1,0:T(8,128)(2,1)S(1)} %copy-done.2, ...), custom_call_target="tpu_custom_call" | custom-call | flops 5368709120 | bytes 8388608 | tf_op jit(solution)/shard_map/mid_pairs/pallas_call | solution.py:188
  58.7 0.0 collective-permute-done.15.refs_1_
  58.7 0.0 collective-permute-done.17.refs_3_
  58.7 0.0 collective-permute-done.14.refs_0_
  58.7 0.0 collective-permute-done.16.refs_2_
  58.7 6.1 %far_pairs.1 = f32[32,128]{1,0:T(8,128)S(1)} custom-call(s32[7,17]{1,0:T(8,128)S(1)} %dynamic-slice_bitcast_fusion.tab_ref, f32[32,128]{1,0:T(8,128)S(1)} %mid_pairs.1.before_ref, bf16[272,1024]{1,0:T(8,128)(2,1)S(1)} %collective-permute-done.14.refs_0_, bf16[256,1024]{1,0:T(8,128)(2,1)S(1)} %collective-permute-done.15.refs_1_, ...), custom_call_target="tpu_custom_call" | custom-call | flops 2684354560 | bytes 6291456 | tf_op jit(solution)/shard_map/far_pairs/pallas_call | solution.py:188
  64.8 19.5 %all_to_all.9 = f32[32,1,128]{2,1,0:T(1,128)S(1)} all-to-all(f32[32,1,128]{2,1,0:T(1,128)S(1)} %bitcast.8), channel_id=1, replica_groups=mesh['prompt'=4,'sample'=32] {'sample'}, dimensions={0} | all-to-all | bytes 32768 | tf_op jit(solution)/shard_map/all_to_all | solution.py:248
  84.3 0.1 reduce_sum.18
  84.3 1.1 %fusion = (f32[]{:T(128)}, f32[1,32]{1,0:T(1,128)}) fusion(f32[128]{0:T(128)S(1)} %reduce_sum.18, s32[]{:T(128)S(6)} %axis_index.12), kind=kLoop, calls=%fused_computation.2 | loop fusion | flops 127 | bytes 392 | tf_op jit(solution)/shard_map/reduce_sum | solution.py:252
  (1 shorter events, 0.0 us)
Async XLA Ops:
  1.3 1.2 %copy-start = (bf16[1,512,1024]{2,1,0:T(8,128)(2,1)S(1)}, bf16[1,512,1024]{2,1,0:T(8,128)(2,1)}, u32[]{:S(2)}) copy-start(bf16[1,512,1024]{2,1,0:T(8,128)(2,1)} %emb_ref.1) | copy-start | bytes 3145732
  3.0 9.9 %collective-permute-start.1 = (bf16[256,1024]{1,0:T(8,128)(2,1)S(1)}, bf16[256,1024]{1,0:T(8,128)(2,1)S(1)}, u32[]{:S(2)}, u32[]{:S(2)}) collective-permute-start(bf16[256,1024]{1,0:T(8,128)(2,1)S(1)} %get-tuple-element.5.refs_1_), channel_id=1, source_target_pairs={{0,1},{1,0},{2,3},{3,2},{4,5},{5,4},{6,7},{7,6},{8,9},{9,8},{10,11... | collective-permute-start | bytes 1572872 | tf_op jit(solution)/shard_map/ppermute | solution.py:31
  3.7 15.0 %collective-permute-start.9 = (bf16[256,1024]{1,0:T(8,128)(2,1)S(1)}, bf16[256,1024]{1,0:T(8,128)(2,1)}, u32[]{:S(2)}, u32[]{:S(2)}) collective-permute-start(bf16[256,1024]{1,0:T(8,128)(2,1)S(1)} %get-tuple-element.5.refs_1_), channel_id=1, source_target_pairs={{0,6},{1,7},{2,0},{3,1},{4,2},{5,3},{6,4},{7,5},{8,14},{9,15},{10,... | collective-permute-start | bytes 1572872 | tf_op jit(solution)/shard_map/ppermute | solution.py:31
  7.5 13.7 %collective-permute-start.3 = (bf16[256,1024]{1,0:T(8,128)(2,1)S(1)}, bf16[256,1024]{1,0:T(8,128)(2,1)}, u32[]{:S(2)}, u32[]{:S(2)}) collective-permute-start(bf16[256,1024]{1,0:T(8,128)(2,1)S(1)} %get-tuple-element.5.refs_1_), channel_id=1, source_target_pairs={{0,24},{1,25},{2,26},{3,27},{4,28},{5,29},{6,30},{7,31},{8,0},{9,1... | collective-permute-start | bytes 1572872 | tf_op jit(solution)/shard_map/ppermute | solution.py:31
  10.2 14.5 %collective-permute-start.13 = (bf16[256,1024]{1,0:T(8,128)(2,1)S(1)}, bf16[256,1024]{1,0:T(8,128)(2,1)S(1)}, u32[]{:S(2)}, u32[]{:S(2)}) collective-permute-start(bf16[256,1024]{1,0:T(8,128)(2,1)S(1)} %get-tuple-element.5.refs_1_), channel_id=1, source_target_pairs={{0,2},{1,3},{2,4},{3,5},{4,6},{5,7},{6,0},{7,1},{8,10},{9,11},{10,... | collective-permute-start | bytes 1572872 | tf_op jit(solution)/shard_map/ppermute | solution.py:31
  10.3 20.5 %collective-permute-start.8 = (bf16[272,1024]{1,0:T(8,128)(2,1)S(1)}, bf16[272,1024]{1,0:T(8,128)(2,1)S(1)}, u32[]{:S(2)}, u32[]{:S(2)}) collective-permute-start(bf16[272,1024]{1,0:T(8,128)(2,1)S(1)} %get-tuple-element.4.refs_0_), channel_id=1, source_target_pairs={{0,6},{1,7},{2,0},{3,1},{4,2},{5,3},{6,4},{7,5},{8,14},{9,15},{10,... | collective-permute-start | bytes 1671176 | tf_op jit(solution)/shard_map/ppermute | solution.py:31
  12.9 0.8 copy-start.3
  13.7 13.4 %collective-permute-start.7 = (bf16[256,1024]{1,0:T(8,128)(2,1)S(1)}, bf16[256,1024]{1,0:T(8,128)(2,1)S(1)}, u32[]{:S(2)}, u32[]{:S(2)}) collective-permute-start(bf16[256,1024]{1,0:T(8,128)(2,1)S(1)} %get-tuple-element.5.refs_1_), channel_id=1, source_target_pairs={{0,8},{1,9},{2,10},{3,11},{4,12},{5,13},{6,14},{7,15},{8,16},{9,17... | collective-permute-start | bytes 1572872 | tf_op jit(solution)/shard_map/ppermute | solution.py:31
  13.7 0.8 copy-start.1
  18.8 12.8 %collective-permute-start = (bf16[272,1024]{1,0:T(8,128)(2,1)S(1)}, bf16[272,1024]{1,0:T(8,128)(2,1)S(1)}, u32[]{:S(2)}, u32[]{:S(2)}) collective-permute-start(bf16[272,1024]{1,0:T(8,128)(2,1)S(1)} %get-tuple-element.4.refs_0_), channel_id=1, source_target_pairs={{0,1},{1,0},{2,3},{3,2},{4,5},{5,4},{6,7},{7,6},{8,9},{9,8},{10,11... | collective-permute-start | bytes 1671176 | tf_op jit(solution)/shard_map/ppermute | solution.py:31
  21.2 14.3 %collective-permute-start.2 = (bf16[272,1024]{1,0:T(8,128)(2,1)S(1)}, bf16[272,1024]{1,0:T(8,128)(2,1)S(1)}, u32[]{:S(2)}, u32[]{:S(2)}) collective-permute-start(bf16[272,1024]{1,0:T(8,128)(2,1)S(1)} %get-tuple-element.4.refs_0_), channel_id=1, source_target_pairs={{0,24},{1,25},{2,26},{3,27},{4,28},{5,29},{6,30},{7,31},{8,0},{9,1... | collective-permute-start | bytes 1671176 | tf_op jit(solution)/shard_map/ppermute | solution.py:31
  24.7 0.8 copy-start.6
  25.5 14.0 %collective-permute-start.12 = (bf16[272,1024]{1,0:T(8,128)(2,1)S(1)}, bf16[272,1024]{1,0:T(8,128)(2,1)S(1)}, u32[]{:S(2)}, u32[]{:S(2)}) collective-permute-start(bf16[272,1024]{1,0:T(8,128)(2,1)S(1)} %get-tuple-element.4.refs_0_), channel_id=1, source_target_pairs={{0,2},{1,3},{2,4},{3,5},{4,6},{5,7},{6,0},{7,1},{8,10},{9,11},{10,... | collective-permute-start | bytes 1671176 | tf_op jit(solution)/shard_map/ppermute | solution.py:31
  27.2 0.8 copy-start.8
  28.0 14.5 %collective-permute-start.6 = (bf16[272,1024]{1,0:T(8,128)(2,1)S(1)}, bf16[272,1024]{1,0:T(8,128)(2,1)}, u32[]{:S(2)}, u32[]{:S(2)}) collective-permute-start(bf16[272,1024]{1,0:T(8,128)(2,1)S(1)} %get-tuple-element.4.refs_0_), channel_id=1, source_target_pairs={{0,8},{1,9},{2,10},{3,11},{4,12},{5,13},{6,14},{7,15},{8,16},{9,17... | collective-permute-start | bytes 1671176 | tf_op jit(solution)/shard_map/ppermute | solution.py:31
  30.7 13.7 %collective-permute-start.10 = (bf16[272,1024]{1,0:T(8,128)(2,1)S(1)}, bf16[272,1024]{1,0:T(8,128)(2,1)S(1)}, u32[]{:S(2)}, u32[]{:S(2)}) collective-permute-start(bf16[272,1024]{1,0:T(8,128)(2,1)S(1)} %collective-permute-done.8.refs_10_.refs_8_), channel_id=1, source_target_pairs={{0,1},{1,0},{2,3},{3,2},{4,5},{5,4},{6,7},{7,6},{8,9},{9,8},{10,11... | collective-permute-start | bytes 1671176 | tf_op jit(solution)/shard_map/ppermute | solution.py:31
  31.6 11.0 %collective-permute-start.11 = (bf16[256,1024]{1,0:T(8,128)(2,1)}, bf16[256,1024]{1,0:T(8,128)(2,1)}, u32[]{:S(2)}, u32[]{:S(2)}) collective-permute-start(bf16[256,1024]{1,0:T(8,128)(2,1)} %collective-permute-done.9.refs_11_.refs_9_), channel_id=1, source_target_pairs={{0,1},{1,0},{2,3},{3,2},{4,5},{5,4},{6,7},{7,6},{8,9},{9,8},{10,11... | collective-permute-start | bytes 1572872 | tf_op jit(solution)/shard_map/ppermute | solution.py:31
  35.5 7.9 %collective-permute-start.5 = (bf16[256,1024]{1,0:T(8,128)(2,1)}, bf16[256,1024]{1,0:T(8,128)(2,1)}, u32[]{:S(2)}, u32[]{:S(2)}) collective-permute-start(bf16[256,1024]{1,0:T(8,128)(2,1)} %collective-permute-done.3.refs_5_), channel_id=1, source_target_pairs={{0,1},{1,0},{2,3},{3,2},{4,5},{5,4},{6,7},{7,6},{8,9},{9,8},{10,11... | collective-permute-start | bytes 1572872 | tf_op jit(solution)/shard_map/ppermute | solution.py:31
  39.5 10.2 %collective-permute-start.4 = (bf16[272,1024]{1,0:T(8,128)(2,1)S(1)}, bf16[272,1024]{1,0:T(8,128)(2,1)}, u32[]{:S(2)}, u32[]{:S(2)}) collective-permute-start(bf16[272,1024]{1,0:T(8,128)(2,1)S(1)} %collective-permute-done.2.refs_4_), channel_id=1, source_target_pairs={{0,1},{1,0},{2,3},{3,2},{4,5},{5,4},{6,7},{7,6},{8,9},{9,8},{10,11... | collective-permute-start | bytes 1671176 | tf_op jit(solution)/shard_map/ppermute | solution.py:31
  42.5 16.2 %collective-permute-start.15 = (bf16[256,1024]{1,0:T(8,128)(2,1)}, bf16[256,1024]{1,0:T(8,128)(2,1)S(1)}, u32[]{:S(2)}, u32[]{:S(2)}) collective-permute-start(bf16[256,1024]{1,0:T(8,128)(2,1)} %collective-permute-done.3.refs_5_), channel_id=1, source_target_pairs={{0,24},{1,25},{2,26},{3,27},{4,28},{5,29},{6,30},{7,31},{8,0},{9,1... | collective-permute-start | bytes 1572872 | tf_op jit(solution)/shard_map/ppermute | solution.py:31
  42.6 16.1 %collective-permute-start.17 = (bf16[256,1024]{1,0:T(8,128)(2,1)}, bf16[256,1024]{1,0:T(8,128)(2,1)S(1)}, u32[]{:S(2)}, u32[]{:S(2)}) collective-permute-start(bf16[256,1024]{1,0:T(8,128)(2,1)} %collective-permute-done.9.refs_11_.refs_9_), channel_id=1, source_target_pairs={{0,6},{1,7},{2,0},{3,1},{4,2},{5,3},{6,4},{7,5},{8,14},{9,15},{10,... | collective-permute-start | bytes 1572872 | tf_op jit(solution)/shard_map/ppermute | solution.py:31
  43.4 15.3 %collective-permute-start.14 = (bf16[272,1024]{1,0:T(8,128)(2,1)}, bf16[272,1024]{1,0:T(8,128)(2,1)S(1)}, u32[]{:S(2)}, u32[]{:S(2)}) collective-permute-start(bf16[272,1024]{1,0:T(8,128)(2,1)} %collective-permute-done.6.refs_8_), channel_id=1, source_target_pairs={{0,8},{1,9},{2,10},{3,11},{4,12},{5,13},{6,14},{7,15},{8,16},{9,17... | collective-permute-start | bytes 1671176 | tf_op jit(solution)/shard_map/ppermute | solution.py:31
  44.4 14.3 %collective-permute-start.16 = (bf16[272,1024]{1,0:T(8,128)(2,1)S(1)}, bf16[272,1024]{1,0:T(8,128)(2,1)S(1)}, u32[]{:S(2)}, u32[]{:S(2)}) collective-permute-start(bf16[272,1024]{1,0:T(8,128)(2,1)S(1)} %collective-permute-done.12.refs_14_), channel_id=1, source_target_pairs={{0,2},{1,3},{2,4},{3,5},{4,6},{5,7},{6,0},{7,1},{8,10},{9,11},{10,... | collective-permute-start | bytes 1671176 | tf_op jit(solution)/shard_map/ppermute | solution.py:31
  45.4 1.0 %copy-start.2 = (bf16[256,1024]{1,0:T(8,128)(2,1)S(1)}, bf16[256,1024]{1,0:T(8,128)(2,1)}, u32[]{:S(2)}) copy-start(bf16[256,1024]{1,0:T(8,128)(2,1)} %copy-done.1) | copy-start | bytes 1572868
  46.5 1.0 %copy-start.4 = (bf16[256,1024]{1,0:T(8,128)(2,1)S(1)}, bf16[256,1024]{1,0:T(8,128)(2,1)}, u32[]{:S(2)}) copy-start(bf16[256,1024]{1,0:T(8,128)(2,1)} %copy-done.3) | copy-start | bytes 1572868
  47.5 2.2 %copy-start.5 = (bf16[256,1024]{1,0:T(8,128)(2,1)S(1)}, bf16[256,1024]{1,0:T(8,128)(2,1)}, u32[]{:S(2)}) copy-start(bf16[256,1024]{1,0:T(8,128)(2,1)} %copy-done.3) | copy-start | bytes 1572868
  47.5 2.2 %copy-start.7 = (bf16[256,1024]{1,0:T(8,128)(2,1)S(1)}, bf16[256,1024]{1,0:T(8,128)(2,1)}, u32[]{:S(2)}) copy-start(bf16[256,1024]{1,0:T(8,128)(2,1)} %copy-done.6) | copy-start | bytes 1572868
  47.5 2.2 %copy-start.9 = (bf16[256,1024]{1,0:T(8,128)(2,1)S(1)}, bf16[256,1024]{1,0:T(8,128)(2,1)}, u32[]{:S(2)}) copy-start(bf16[256,1024]{1,0:T(8,128)(2,1)} %copy-done.8) | copy-start | bytes 1572868

commit v2 on v0

v2 whole, which is shorter than its diff:
```python
import functools

import jax
import jax.numpy as jnp
import numpy as np
from jax import lax
from jax.experimental import pallas as pl
from jax.experimental.pallas import tpu as pltpu
from jax.sharding import PartitionSpec as P

N = 4
HALF = 256
LEN = 2 * HALF
TAG = 16
VMEM = 24 * 2**20


def device(line, across, core):
    y, z = (across, line) if core == 0 else (line, across)
    return (y * N + z) * 2 + core


PLACES = [(line, across, core) for line in range(N) for across in range(N) for core in range(2)]


def near(i):
    return i ^ 1


def wide(i):
    return N - 1 - i


def along(x, step):
    moves = [(device(i, j, c), device(step(i), j, c)) for i, j, c in PLACES]
    return lax.ppermute(x, "sample", moves)


def over(x, step):
    moves = [(device(i, j, c), device(i, step(j), c)) for i, j, c in PLACES]
    return lax.ppermute(x, "sample", moves)


def swap(x):
    return lax.ppermute(x, "sample", [(i, i ^ 1) for i in range(2 * N * N)])


def unit_kernel(len_ref, emb_ref, full_ref, head_ref, tail_ref, raw, unit, sem):
    halves = (slice(0, HALF), slice(HALF, LEN))
    loads = [
        pltpu.make_async_copy(emb_ref.at[0, rows, :], raw.at[rows, :], sem.at[n])
        for n, rows in enumerate(halves)
    ]
    for load in loads:
        load.start()
    length = len_ref[0]
    lines = lax.broadcasted_iota(jnp.int32, (TAG, raw.shape[1]), 0)
    tag = jnp.where(lines < TAG // 2, length // 16, length % 16)
    unit[LEN : LEN + TAG, :] = tag.astype(jnp.float32).astype(jnp.bfloat16)
    stores = [
        pltpu.make_async_copy(
            unit.at[LEN : LEN + TAG, :], head_ref.at[HALF : HALF + TAG, :], sem.at[2]
        ),
        pltpu.make_async_copy(
            unit.at[LEN : LEN + TAG, :], full_ref.at[LEN : LEN + TAG, :], sem.at[3]
        ),
    ]
    for store in stores:
        store.start()
    first = None
    for n, rows in enumerate(halves):
        loads[n].wait()
        values = raw[rows, :].astype(jnp.float32)
        norm = jnp.sqrt(jnp.sum(values * values, axis=1, keepdims=True) + 1e-06)
        scaled = values / norm
        if first is None:
            first = scaled[0:1, :]
        places = lax.broadcasted_iota(jnp.int32, (HALF, 1), 0) + n * HALF
        unit[rows, :] = jnp.where(places < length, scaled, first).astype(jnp.bfloat16)
        part = head_ref.at[0:HALF, :] if n == 0 else tail_ref
        for k, target in enumerate((part, full_ref.at[rows, :])):
            store = pltpu.make_async_copy(unit.at[rows, :], target, sem.at[4 + 2 * n + k])
            store.start()
            stores.append(store)
    for store in stores:
        store.wait()


def make_unit(lengths, embeddings):
    width = embeddings.shape[2]
    rows = (LEN + TAG, HALF + TAG, HALF)
    return pl.pallas_call(
        unit_kernel,
        out_shape=tuple(jax.ShapeDtypeStruct((r, width), jnp.bfloat16) for r in rows),
        in_specs=[
            pl.BlockSpec(memory_space=pltpu.SMEM),
            pl.BlockSpec(memory_space=pltpu.HBM),
        ],
        out_specs=tuple(pl.BlockSpec(memory_space=pltpu.HBM) for _ in rows),
        scratch_shapes=[
            pltpu.VMEM((LEN, width), jnp.bfloat16),
            pltpu.VMEM((LEN + TAG, width), jnp.bfloat16),
            pltpu.SemaphoreType.DMA((8,)),
        ],
        compiler_params=pltpu.CompilerParams(vmem_limit_bytes=VMEM),
        name="unit",
    )(lengths, embeddings)


def plan(here):
    core = here % 2
    line, across = (here // 2 % N, here // 2 // N) if core == 0 else (here // 2 // N, here // 2 % N)
    low = across < N // 2

    def mine(i, j):
        return device(i, j, core)

    at = {
        "own": mine(line, across),
        "near": mine(near(line), across),
        "wide": mine(wide(line), across),
        "far": mine((line + 2) % N, across),
        "side": mine(line, wide(across)),
    }
    sender = near(across)
    at["next"] = mine(line, sender if sender in (0, N - 1) else wide(sender))
    for name, place in (
        ("sib", across),
        ("sib_near", near(across)),
        ("sib_wide", wide(across)),
        ("sib_far", (across + 2) % N),
    ):
        at[name] = device(place, line, 1 - core)

    early = [("own", "own")]
    if core == 0:
        early += [("own", "sib"), ("near", "sib")]
    else:
        early += [("near", "sib"), ("near", "sib_near")]
    if low:
        early += [("side", "own"), ("side", "near")]
    if line % 2 == 0:
        early += [("own", "near")]
    middle = [("wide", "sib"), ("wide", "sib_near")]
    if not low:
        middle += [("side", "wide")]
    if line % 2 == 1:
        middle += [("own", "wide")]
    if line in (1, 2):
        middle += [("near", "wide")]
    middle += [("next", "own"), ("next", "near"), ("next", "wide")]
    late = [("wide", "sib_wide")] if core == 1 else []
    late += [("far", "sib"), ("far", "sib_near"), ("far", "sib_wide"), ("next", "far")]
    if not low:
        late += [("side", "far")]
    if core == 0:
        late += [("far", "sib_far")]
    return at, (early, middle, late)


STAGES = (
    ("own", "near", "side", "sib", "sib_near"),
    ("own", "near", "wide", "side", "next", "sib", "sib_near"),
    ("far", "next", "side", "wide", "sib", "sib_near", "sib_wide", "sib_far"),
)


def make_table(total):
    plans = [plan(i) for i in range(total)]
    tables = []
    for stage, slots in enumerate(STAGES):
        steps = max((len(p[1][stage]) + 1) // 2 for p in plans)
        rows = np.zeros((total, 1 + 2 * steps, 8), np.int32)
        for i, (at, stages) in enumerate(plans):
            pairs = stages[stage]
            rows[i, 0, 0] = (len(pairs) + 1) // 2
            seen = set()
            for k, (u, v) in enumerate(pairs):
                waits = [0, 0]
                for n, s in enumerate((u, v)):
                    if s not in seen:
                        waits[n] = slots.index(s) + 1
                        seen.add(s)
                both = u != "own" or v != "own"
                rows[i, 1 + k] = (slots.index(u), slots.index(v), at[u], at[v], *waits, both, 0)
            if len(pairs) % 2:
                rows[i, 1 + len(pairs), :4] = (slots.index(u), slots.index(v), -1, -1)
            rest = [s for s in slots if s not in seen]
            rows[i, 0, 1] = sum(1 << slots.index(s) for s in rest)
        tables.append(rows.reshape(total, -1))
    starts = np.cumsum([0] + [t.shape[1] for t in tables])
    return np.concatenate(tables, axis=1), starts


def pairs_kernel(base, shapes, tab_ref, *refs):
    before_ref, refs = (None, refs) if base == 0 else (refs[0], refs[1:])
    ins = refs[: sum(shapes)]
    out_ref, tok, tag, sem = refs[sum(shapes) :]
    place = 0
    for s, parts in enumerate(shapes):
        head = ins[place]
        if parts == 1:
            tail, tags = head.at[HALF:LEN, :], head.at[LEN : LEN + TAG, 0:128]
        else:
            tail, tags = ins[place + 1], head.at[HALF : HALF + TAG, 0:128]
        place += parts
        pltpu.make_async_copy(head.at[0:HALF, :], tok.at[s, 0:HALF, :], sem.at[s, 0]).start()
        pltpu.make_async_copy(tail, tok.at[s, HALF:LEN, :], sem.at[s, 1]).start()
        pltpu.make_async_copy(tags, tag.at[s], sem.at[s, 2]).start()

    def arrive(s):
        for part in range(2):
            pltpu.make_async_copy(
                ins[0].at[0:HALF, :], tok.at[s, 0:HALF, :], sem.at[s, part]
            ).wait()
        pltpu.make_async_copy(ins[0].at[0:TAG, 0:128], tag.at[s], sem.at[s, 2]).wait()

    out_ref[...] = jnp.zeros_like(out_ref) if before_ref is None else before_ref[...]
    owners = lax.broadcasted_iota(jnp.int32, out_ref.shape, 0)
    lanes = lax.broadcasted_iota(jnp.int32, out_ref.shape, 1)
    total = out_ref.shape[0]
    rows = lax.broadcasted_iota(jnp.int32, (LEN, 1), 0).astype(jnp.float32)
    cols = lax.broadcasted_iota(jnp.int32, (1, LEN), 1).astype(jnp.float32)

    def length(s):
        value = tag[s].astype(jnp.float32)
        return value[0:1, 0:1] * 16.0 + value[TAG // 2 : TAG // 2 + 1, 0:1]

    def score(at):
        u, v = tab_ref[at], tab_ref[at + 1]
        own, other, both = tab_ref[at + 2], tab_ref[at + 3], tab_ref[at + 6]
        len_u, len_v = length(u), length(v)
        similar = lax.dot_general(
            tok[u], tok[v], (((1,), (1,)), ((), ())), preferred_element_type=jnp.float32
        )
        best_row = jnp.max(similar, axis=1, keepdims=True)
        best_col = jnp.max(similar, axis=0, keepdims=True)
        ahead = jnp.sum(jnp.where(rows < len_u, best_row, 0.0), axis=0, keepdims=True)
        behind = jnp.sum(jnp.where(cols < len_v, best_col, 0.0), axis=1, keepdims=True)
        ahead = ahead / len_u
        behind = behind / len_v
        at_u = owners == own
        at_v = (owners == other) & (both == 1)
        fore = (at_u & (lanes == other)) | (at_v & (lanes == total + own))
        back = (at_u & (lanes == total + other)) | (at_v & (lanes == own))
        return jnp.where(fore, ahead, 0.0) + jnp.where(back, behind, 0.0)

    @pl.loop(0, tab_ref[base])
    def _(step):
        first = base + 8 + 16 * step
        for wait in (4, 5, 12, 13):

            @pl.when(tab_ref[first + wait] > 0)
            def _():
                arrive(tab_ref[first + wait] - 1)

        out_ref[...] += score(first) + score(first + 8)

    rest = tab_ref[base + 1]
    for s in range(len(shapes)):

        @pl.when((rest >> s) % 2 == 1)
        def _():
            arrive(s)


def run_pairs(stage, table, starts, before, blocks):
    slots = [blocks[name] for name in STAGES[stage]]
    arrays = [half for block in slots for half in block]
    width = arrays[0].shape[1]
    before = [] if before is None else [before]
    steps = ((starts[stage + 1] - starts[stage]) // 8 - 1) // 2
    return pl.pallas_call(
        functools.partial(pairs_kernel, int(starts[stage]), [len(block) for block in slots]),
        out_shape=jax.ShapeDtypeStruct((2 * N * N, 128), jnp.float32),
        in_specs=[pl.BlockSpec(memory_space=pltpu.SMEM)]
        + [pl.BlockSpec(memory_space=pltpu.VMEM)] * len(before)
        + [pl.BlockSpec(memory_space=pltpu.HBM)] * len(arrays),
        out_specs=pl.BlockSpec(memory_space=pltpu.VMEM),
        scratch_shapes=[
            pltpu.VMEM((len(slots), LEN, width), jnp.bfloat16),
            pltpu.VMEM((len(slots), TAG, 128), jnp.bfloat16),
            pltpu.SemaphoreType.DMA((len(slots), 3)),
        ],
        compiler_params=pltpu.CompilerParams(vmem_limit_bytes=VMEM),
        cost_estimate=pl.CostEstimate(
            flops=int(4 * steps * LEN * LEN * width * 2),
            bytes_accessed=len(slots) * LEN * width * 2,
            transcendentals=0,
        ),
        name=f"pairs_{stage}",
    )(table, *before, *arrays)


def after(x, *others):
    return lax.optimization_barrier((x, *others))[0]


def body(embeddings, lengths):
    total = lax.axis_size("sample")
    here = lax.axis_index("sample")
    core, chip = here % 2, here // 2
    across = jnp.where(core == 0, chip // N, chip % N)
    edge = (across == 0) | (across == N - 1)

    full, head, tail = make_unit(lengths, embeddings)
    tables, starts = make_table(total)
    table = jnp.asarray(tables)[here]
    near_t = along(tail, near)
    side = over(full, wide)
    near_h = along(head, near)
    sib = swap(full)
    wide_h = along(after(head, side), wide)
    following = over(jnp.where(edge, full, side), near)
    wide_t = along(after(tail, side), wide)
    blocks = {
        "own": (full,),
        "near": (near_h, near_t),
        "side": (side,),
        "sib": (sib,),
        "sib_near": (swap(near_h), swap(near_t)),
    }
    scores = run_pairs(0, table, starts, None, blocks)
    far_h = along(after(wide_h, following, scores), near)
    far_t = along(after(near_t, wide_t, scores), wide)
    blocks |= {
        "wide": (wide_h, wide_t),
        "next": (following,),
    }
    scores = run_pairs(1, table, starts, scores, blocks)
    blocks |= {
        "far": (far_h, far_t),
        "sib_wide": (swap(wide_h), swap(wide_t)),
        "sib_far": (swap(after(far_h, scores)), swap(after(far_t, scores))),
    }
    scores = run_pairs(2, table, starts, scores, blocks)

    parts = lax.all_to_all(scores, "sample", 0, 0, tiled=True)
    result = jnp.sum(parts, axis=0)
    ahead, behind = result[:total], result[total : 2 * total]
    offdiag = jnp.arange(total, dtype=jnp.int32) != here
    utility = jnp.sum(jnp.where(offdiag, ahead + behind, 0.0)) / jnp.float32(2 * (total - 1))
    return ahead[None, :], utility[None]


def solution(mesh):
    in_specs = (P(("prompt", "sample"), None, None), P(("prompt", "sample")))
    out_specs = (P(("prompt", "sample"), None), P(("prompt", "sample")))
    return jax.shard_map(body, mesh=mesh, in_specs=in_specs, out_specs=out_specs, check_vma=False)
```

time: 164 us -> 81.1 us (0.49)
  waiting for transfers between devices: 95.5 us -> 26.6 us
  matrix products: 24.3 us -> 0 us
  Pallas kernels: 0 us -> 20.9 us
  starting transfers between devices: 0.04 us -> 13.8 us
  between operations: 16.5 us -> 3.12 us
  blocking collectives: 18.4 us -> 11.4 us
  other arithmetic: 5.47 us -> 2.27 us
    all_gather x1 -> x0, waiting for transfers between devices: 95.5 us -> none  [body(): piece = lax.all_gather(unit, 'sample', axis=0, tiled=True)]
    ppermute x0 -> x15, waiting for transfers between devices: none -> 26.6 us  [the longest x6 23.6 us: along(): return lax.ppermute(x, 'sample', moves)]
    dot_general x1 -> x0, matrix products: 24.3 us -> none  [tile_pairs(): jnp.einsum('aie,bje->abij', own, other, preferred_element_type=jnp.float32)]
    pallas_call x0 -> x4, Pallas kernels: none -> 20.9 us  [the longest x3 19.4 us: run_pairs(): pl.pallas_call(functools.partial(pairs_kernel, int(starts[stage]), [len(b...]
    unnamed x1 -> x0, blocking collectives: 18.4 us -> none
    ppermute x0 -> x15, starting transfers between devices: none -> 13.8 us  [the longest x6 9.1 us: along(): return lax.ppermute(x, 'sample', moves)]
    all_to_all x0 -> x1, blocking collectives: none -> 11.4 us  [body(): parts = lax.all_to_all(scores, 'sample', 0, 0, tiled=True)]
    convert_element_type x1 -> x0, other arithmetic: 2.56 us -> none  [body(): (values / jnp.sqrt(jnp.sum(values * values, axis=2, keepdims=True) + 1e-0...]
  transfers between devices with their start and end apart: 1 -> 15, of which waited for: 1 -> 5; matrix products, arithmetic and copies ran while one was open for 1% -> 2% of each run, Pallas kernels for 0% -> 16%
where the time goes in v2:
time: 81.1 us; the launch traced here: 80 us
  waiting for transfers between devices  26.6 us (33%)
  Pallas kernels  20.9 us (26%)
  starting transfers between devices  13.8 us (17%)
  blocking collectives  11.4 us (14%)
  between operations  3.12 us (4%)
  other arithmetic  2.27 us (3%)
  local copies, waits for them, and re-layouts  1.92 us (2%)
    ppermute x6, waiting for transfers between devices, along(): return lax.ppermute(x, 'sample', moves)  23.6 us
    pallas_call x3, Pallas kernels, run_pairs(): pl.pallas_call(functools.partial(pairs_kernel, int(starts[stage]), [len(b...  19.4 us
    all_to_all x1, blocking collectives, body(): parts = lax.all_to_all(scores, 'sample', 0, 0, tiled=True)  11.4 us
    ppermute x6, starting transfers between devices, along(): return lax.ppermute(x, 'sample', moves)  9.1 us
    ppermute x2, starting transfers between devices, over(): return lax.ppermute(x, 'sample', moves)  3.68 us
    ppermute x7, waiting for transfers between devices, swap(): return lax.ppermute(x, 'sample', [(i, i ^ 1) for i in range(2 * N * N)])  2.95 us
  transfers between devices with their start and end apart: 15, of which 5 were waited for; matrix products, arithmetic and copies ran while one was open for 2% of the time, Pallas kernels for 16%

profile of v2, /device:TPU:0, one launch (start us, length us, event | category | flops | bytes accessed | tf_op | source)
XLA Modules:
  0.0 80.0 jit_solution(16324385122078647235)
XLA Ops:
  1.3 0.0 copy-start
  1.3 1.2 %copy-done = bf16[1,512,1024]{2,1,0:T(8,128)(2,1)S(1)} copy-done((bf16[1,512,1024]{2,1,0:T(8,128)(2,1)S(1)}, bf16[1,512,1024]{2,1,0:T(8,128)(2,1)}, u32[]{:S(2)}) %copy-start) | copy-done | bytes 1048600
  2.5 1.5 %unit.1 = (bf16[528,1024]{1,0:T(8,128)(2,1)S(1)}, bf16[272,1024]{1,0:T(8,128)(2,1)}, bf16[256,1024]{1,0:T(8,128)(2,1)}) custom-call(s32[1]{0:T(128)S(6)} %copy.6.len_ref, bf16[1,512,1024]{2,1,0:T(8,128)(2,1)S(1)} %copy-done), custom_call_target="tpu_custom_call" | custom-call | tf_op jit(solution)/shard_map/unit/pallas_call | solution.py:92
  4.0 3.2 %collective-permute-start.2 = (bf16[528,1024]{1,0:T(8,128)(2,1)S(1)}, bf16[528,1024]{1,0:T(8,128)(2,1)S(1)}, u32[]{:S(2)}, u32[]{:S(2)}) collective-permute-start(bf16[528,1024]{1,0:T(8,128)(2,1)S(1)} %get-tuple-element.11.refs_0_.refs_1_), channel_id=1, source_target_pairs={{0,24},{1,7},{8,16},{3,5},{16,8},{5,3},{24,0},{7,1},{2,26},{9,15},... | collective-permute-start | bytes 3244040 | tf_op jit(solution)/shard_map/ppermute | solution.py:41
  7.2 1.9 %collective-permute-start = (bf16[272,1024]{1,0:T(8,128)(2,1)}, bf16[272,1024]{1,0:T(8,128)(2,1)}, u32[]{:S(2)}, u32[]{:S(2)}) collective-permute-start(bf16[272,1024]{1,0:T(8,128)(2,1)} %get-tuple-element.14), channel_id=1, source_target_pairs={{0,2},{1,9},{8,10},{3,11},{16,18},{5,13},{24,26},{7,15},{2,0},{9,1... | collective-permute-start | bytes 1671176 | tf_op jit(solution)/shard_map/ppermute | solution.py:36
  9.1 0.1 collective-permute-start.1
  9.2 0.0 collective-permute-start.3
  9.2 13.4 %collective-permute-done.1.refs_2_.refs_3_ = bf16[256,1024]{1,0:T(8,128)(2,1)} collective-permute-done((bf16[256,1024]{1,0:T(8,128)(2,1)}, bf16[256,1024]{1,0:T(8,128)(2,1)}, u32[]{:S(2)}, u32[]{:S(2)}) %collective-permute-start.1) | collective-permute-done | bytes 524320 | tf_op jit(solution)/shard_map/ppermute | solution.py:36
  22.7 0.0 collective-permute-start.5
  22.7 0.0 collective-permute-done.refs_1_.refs_2_
  22.7 0.5 collective-permute-start.4
  23.2 0.0 collective-permute-done.2.refs_3_.refs_6_.refs_4_
  23.2 1.1 %broadcast_select_fusion = bf16[528,1024]{1,0:T(8,128)(2,1)} fusion(bf16[528,1024]{1,0:T(8,128)(2,1)S(1)} %get-tuple-element.11.refs_0_.refs_1_, bf16[528,1024]{1,0:T(8,128)(2,1)S(1)} %collective-permute-done.2.refs_3_.refs_6_.refs_4_, pred[]{:T(512)S(6)} %or.3), kind=kLoop, calls=%fused_computation | loop fusion | flops 540672 | bytes 3244033 | tf_op jit(solution)/shard_map/jit(_where)/select_n | solution.py:314
  24.3 0.5 collective-permute-start.8
  24.8 0.7 constant_dynamic-slice_fusion
  25.5 3.7 %collective-permute-start.6 = (bf16[272,1024]{1,0:T(8,128)(2,1)}, bf16[272,1024]{1,0:T(8,128)(2,1)S(1)}, u32[]{:S(2)}, u32[]{:S(2)}) collective-permute-start(bf16[272,1024]{1,0:T(8,128)(2,1)} %get-tuple-element.14), channel_id=1, source_target_pairs={{0,6},{1,25},{8,14},{3,27},{16,22},{5,29},{24,30},{7,31},{2,4},{9,... | collective-permute-start | bytes 1671176 | tf_op jit(solution)/shard_map/ppermute | solution.py:36
  29.2 0.0 collective-permute-done.5.refs_6_.refs_10_.refs_9_
  29.2 0.1 collective-permute-start.7
  29.3 0.0 collective-permute-done.3.refs_4_.refs_8_.refs_7_
  29.3 0.0 collective-permute-done.4.refs_5_.refs_9_.refs_8_
  29.3 5.4 %pairs_0.1.refs_0_ = f32[32,128]{1,0:T(8,128)S(1)} custom-call(s32[184]{0:T(256)S(1)} %bitcast.8, bf16[528,1024]{1,0:T(8,128)(2,1)S(1)} %get-tuple-element.11.refs_0_.refs_1_, bf16[272,1024]{1,0:T(8,128)(2,1)} %collective-permute-done.refs_1_.refs_2_, bf16[256,1024]{1,0:T(8,128)(2,1)} %collective-permute-done.1.refs_2_.refs_3_, ...), custom_call_target="tpu_custom_call" | custom-call | flops 6442450944 | bytes 5242880 | tf_op jit(solution)/shard_map/pairs_0/pallas_call | solution.py:273
  34.7 7.8 %collective-permute-done.7.refs_5_.refs_6_ = bf16[256,1024]{1,0:T(8,128)(2,1)S(1)} collective-permute-done((bf16[256,1024]{1,0:T(8,128)(2,1)}, bf16[256,1024]{1,0:T(8,128)(2,1)S(1)}, u32[]{:S(2)}, u32[]{:S(2)}) %collective-permute-start.7) | collective-permute-done | bytes 524320 | tf_op jit(solution)/shard_map/ppermute | solution.py:36
  42.5 3.2 %collective-permute-start.10 = (bf16[256,1024]{1,0:T(8,128)(2,1)}, bf16[256,1024]{1,0:T(8,128)(2,1)S(1)}, u32[]{:S(2)}, u32[]{:S(2)}) collective-permute-start(bf16[256,1024]{1,0:T(8,128)(2,1)} %collective-permute-done.1.refs_2_.refs_3_), channel_id=1, source_target_pairs={{0,6},{1,25},{8,14},{3,27},{16,22},{5,29},{24,30},{7,31},{2,4},{9,... | collective-permute-start | bytes 1572872 | tf_op jit(solution)/shard_map/ppermute | solution.py:36
  45.8 0.0 collective-permute-done.6.refs_4_.refs_5_
  45.8 0.0 collective-permute-start.11
  45.8 0.0 collective-permute-done.8.refs_7_.refs_3_
  45.8 0.1 collective-permute-start.9
  45.9 7.1 %pairs_1.1.refs_0_ = f32[32,128]{1,0:T(8,128)S(1)} custom-call(s32[184]{0:T(256)S(1)} %bitcast.9, f32[32,128]{1,0:T(8,128)S(1)} %pairs_0.1.refs_0_, bf16[528,1024]{1,0:T(8,128)(2,1)S(1)} %get-tuple-element.11.refs_0_.refs_1_, bf16[272,1024]{1,0:T(8,128)(2,1)} %collective-permute-done.refs_1_.refs_2_, ...), custom_call_target="tpu_custom_call" | custom-call | flops 8589934592 | bytes 7340032 | tf_op jit(solution)/shard_map/pairs_1/pallas_call | solution.py:273
  53.0 2.4 %collective-permute-done.9.refs_1_ = bf16[272,1024]{1,0:T(8,128)(2,1)S(1)} collective-permute-done((bf16[272,1024]{1,0:T(8,128)(2,1)S(1)}, bf16[272,1024]{1,0:T(8,128)(2,1)S(1)}, u32[]{:S(2)}, u32[]{:S(2)}) %collective-permute-start.9) | collective-permute-done | bytes 557088 | tf_op jit(solution)/shard_map/ppermute | solution.py:36
  55.4 0.0 collective-permute-start.13
  55.4 0.5 collective-permute-start.12
  55.9 0.0 collective-permute-done.10.refs_2_
  55.9 0.0 collective-permute-start.14
  55.9 2.2 %collective-permute-done.12.refs_11_ = bf16[256,1024]{1,0:T(8,128)(2,1)S(1)} collective-permute-done((bf16[256,1024]{1,0:T(8,128)(2,1)S(1)}, bf16[256,1024]{1,0:T(8,128)(2,1)S(1)}, u32[]{:S(2)}, u32[]{:S(2)}) %collective-permute-start.12) | collective-permute-done | bytes 524320 | tf_op jit(solution)/shard_map/ppermute | solution.py:45
  58.1 0.0 collective-permute-done.11.refs_10_
  58.1 0.7 collective-permute-done.14.refs_13_
  58.8 0.0 collective-permute-done.13.refs_12_
  58.8 6.9 %pairs_2.1 = f32[32,128]{1,0:T(8,128)S(1)} custom-call(s32[184]{0:T(256)S(1)} %bitcast.10, f32[32,128]{1,0:T(8,128)S(1)} %pairs_1.1.refs_0_, bf16[272,1024]{1,0:T(8,128)(2,1)S(1)} %collective-permute-done.9.refs_1_, bf16[256,1024]{1,0:T(8,128)(2,1)S(1)} %collective-permute-done.10.refs_2_, bf16[528,1024]{1,0:T(8,128)(2,1)} %collective-permute-done.8.refs_7_.refs_3_, ...), custom_call_target="tpu_custom_call" | custom-call | flops 6442450944 | bytes 8388608 | tf_op jit(solution)/shard_map/pairs_2/pallas_call | solution.py:273
  65.7 11.4 %all_to_all.9 = f32[32,1,128]{2,1,0:T(1,128)S(1)} all-to-all(f32[32,1,128]{2,1,0:T(1,128)S(1)} %bitcast.7), channel_id=1, replica_groups=mesh['prompt'=4,'sample'=32] {'sample'}, dimensions={0} | all-to-all | bytes 32768 | tf_op jit(solution)/shard_map/all_to_all | solution.py:338
  77.1 0.1 reduce_sum.18
  77.1 1.1 %fusion = (f32[]{:T(128)}, f32[1,32]{1,0:T(1,128)}) fusion(f32[128]{0:T(128)S(1)} %reduce_sum.18, s32[]{:T(128)S(6)} %axis_index.12), kind=kLoop, calls=%fused_computation.2 | loop fusion | flops 127 | bytes 392 | tf_op jit(solution)/shard_map/reduce_sum | solution.py:342
Async XLA Ops:
  1.3 1.2 %copy-start = (bf16[1,512,1024]{2,1,0:T(8,128)(2,1)S(1)}, bf16[1,512,1024]{2,1,0:T(8,128)(2,1)}, u32[]{:S(2)}) copy-start(bf16[1,512,1024]{2,1,0:T(8,128)(2,1)} %emb_ref.1) | copy-start | bytes 3145732
  4.0 19.2 %collective-permute-start.2 = (bf16[528,1024]{1,0:T(8,128)(2,1)S(1)}, bf16[528,1024]{1,0:T(8,128)(2,1)S(1)}, u32[]{:S(2)}, u32[]{:S(2)}) collective-permute-start(bf16[528,1024]{1,0:T(8,128)(2,1)S(1)} %get-tuple-element.11.refs_0_.refs_1_), channel_id=1, source_target_pairs={{0,24},{1,7},{8,16},{3,5},{16,8},{5,3},{24,0},{7,1},{2,26},{9,15},... | collective-permute-start | bytes 3244040 | tf_op jit(solution)/shard_map/ppermute | solution.py:41
  7.2 15.5 %collective-permute-start = (bf16[272,1024]{1,0:T(8,128)(2,1)}, bf16[272,1024]{1,0:T(8,128)(2,1)}, u32[]{:S(2)}, u32[]{:S(2)}) collective-permute-start(bf16[272,1024]{1,0:T(8,128)(2,1)} %get-tuple-element.14), channel_id=1, source_target_pairs={{0,2},{1,9},{8,10},{3,11},{16,18},{5,13},{24,26},{7,15},{2,0},{9,1... | collective-permute-start | bytes 1671176 | tf_op jit(solution)/shard_map/ppermute | solution.py:36
  9.1 13.5 %collective-permute-start.1 = (bf16[256,1024]{1,0:T(8,128)(2,1)}, bf16[256,1024]{1,0:T(8,128)(2,1)}, u32[]{:S(2)}, u32[]{:S(2)}) collective-permute-start(bf16[256,1024]{1,0:T(8,128)(2,1)} %get-tuple-element.15), channel_id=1, source_target_pairs={{0,2},{1,9},{8,10},{3,11},{16,18},{5,13},{24,26},{7,15},{2,0},{9,1... | collective-permute-start | bytes 1572872 | tf_op jit(solution)/shard_map/ppermute | solution.py:36
  9.2 20.0 %collective-permute-start.3 = (bf16[528,1024]{1,0:T(8,128)(2,1)S(1)}, bf16[528,1024]{1,0:T(8,128)(2,1)S(1)}, u32[]{:S(2)}, u32[]{:S(2)}) collective-permute-start(bf16[528,1024]{1,0:T(8,128)(2,1)S(1)} %get-tuple-element.11.refs_0_.refs_1_), channel_id=1, source_target_pairs={{0,1},{1,0},{2,3},{3,2},{4,5},{5,4},{6,7},{7,6},{8,9},{9,8},{10,11... | collective-permute-start | bytes 3244040 | tf_op jit(solution)/shard_map/ppermute | solution.py:45
  22.7 6.5 %collective-permute-start.5 = (bf16[256,1024]{1,0:T(8,128)(2,1)}, bf16[256,1024]{1,0:T(8,128)(2,1)}, u32[]{:S(2)}, u32[]{:S(2)}) collective-permute-start(bf16[256,1024]{1,0:T(8,128)(2,1)} %collective-permute-done.1.refs_2_.refs_3_), channel_id=1, source_target_pairs={{0,1},{1,0},{2,3},{3,2},{4,5},{5,4},{6,7},{7,6},{8,9},{9,8},{10,11... | collective-permute-start | bytes 1572872 | tf_op jit(solution)/shard_map/ppermute | solution.py:45
  22.7 6.6 %collective-permute-start.4 = (bf16[272,1024]{1,0:T(8,128)(2,1)}, bf16[272,1024]{1,0:T(8,128)(2,1)}, u32[]{:S(2)}, u32[]{:S(2)}) collective-permute-start(bf16[272,1024]{1,0:T(8,128)(2,1)} %collective-permute-done.refs_1_.refs_2_), channel_id=1, source_target_pairs={{0,1},{1,0},{2,3},{3,2},{4,5},{5,4},{6,7},{7,6},{8,9},{9,8},{10,11... | collective-permute-start | bytes 1671176 | tf_op jit(solution)/shard_map/ppermute | solution.py:45
  24.3 21.5 %collective-permute-start.8 = (bf16[528,1024]{1,0:T(8,128)(2,1)}, bf16[528,1024]{1,0:T(8,128)(2,1)}, u32[]{:S(2)}, u32[]{:S(2)}) collective-permute-start(bf16[528,1024]{1,0:T(8,128)(2,1)} %broadcast_select_fusion), channel_id=1, source_target_pairs={{0,8},{1,3},{8,0},{3,1},{16,24},{5,7},{24,16},{7,5},{2,10},{9,11},... | collective-permute-start | bytes 3244040 | tf_op jit(solution)/shard_map/ppermute | solution.py:41
  25.5 20.2 %collective-permute-start.6 = (bf16[272,1024]{1,0:T(8,128)(2,1)}, bf16[272,1024]{1,0:T(8,128)(2,1)S(1)}, u32[]{:S(2)}, u32[]{:S(2)}) collective-permute-start(bf16[272,1024]{1,0:T(8,128)(2,1)} %get-tuple-element.14), channel_id=1, source_target_pairs={{0,6},{1,25},{8,14},{3,27},{16,22},{5,29},{24,30},{7,31},{2,4},{9,... | collective-permute-start | bytes 1671176 | tf_op jit(solution)/shard_map/ppermute | solution.py:36
  29.2 13.3 %collective-permute-start.7 = (bf16[256,1024]{1,0:T(8,128)(2,1)}, bf16[256,1024]{1,0:T(8,128)(2,1)S(1)}, u32[]{:S(2)}, u32[]{:S(2)}) collective-permute-start(bf16[256,1024]{1,0:T(8,128)(2,1)} %get-tuple-element.15), channel_id=1, source_target_pairs={{0,6},{1,25},{8,14},{3,27},{16,22},{5,29},{24,30},{7,31},{2,4},{9,... | collective-permute-start | bytes 1572872 | tf_op jit(solution)/shard_map/ppermute | solution.py:36
  42.5 13.4 %collective-permute-start.10 = (bf16[256,1024]{1,0:T(8,128)(2,1)}, bf16[256,1024]{1,0:T(8,128)(2,1)S(1)}, u32[]{:S(2)}, u32[]{:S(2)}) collective-permute-start(bf16[256,1024]{1,0:T(8,128)(2,1)} %collective-permute-done.1.refs_2_.refs_3_), channel_id=1, source_target_pairs={{0,6},{1,25},{8,14},{3,27},{16,22},{5,29},{24,30},{7,31},{2,4},{9,... | collective-permute-start | bytes 1572872 | tf_op jit(solution)/shard_map/ppermute | solution.py:36
  45.8 12.3 %collective-permute-start.11 = (bf16[272,1024]{1,0:T(8,128)(2,1)S(1)}, bf16[272,1024]{1,0:T(8,128)(2,1)S(1)}, u32[]{:S(2)}, u32[]{:S(2)}) collective-permute-start(bf16[272,1024]{1,0:T(8,128)(2,1)S(1)} %collective-permute-done.6.refs_4_.refs_5_), channel_id=1, source_target_pairs={{0,1},{1,0},{2,3},{3,2},{4,5},{5,4},{6,7},{7,6},{8,9},{9,8},{10,11... | collective-permute-start | bytes 1671176 | tf_op jit(solution)/shard_map/ppermute | solution.py:45
  45.8 9.6 %collective-permute-start.9 = (bf16[272,1024]{1,0:T(8,128)(2,1)S(1)}, bf16[272,1024]{1,0:T(8,128)(2,1)S(1)}, u32[]{:S(2)}, u32[]{:S(2)}) collective-permute-start(bf16[272,1024]{1,0:T(8,128)(2,1)S(1)} %collective-permute-done.6.refs_4_.refs_5_), channel_id=1, source_target_pairs={{0,2},{1,9},{8,10},{3,11},{16,18},{5,13},{24,26},{7,15},{2,0},{9,1... | collective-permute-start | bytes 1671176 | tf_op jit(solution)/shard_map/ppermute | solution.py:36
  55.4 3.5 %collective-permute-start.13 = (bf16[272,1024]{1,0:T(8,128)(2,1)S(1)}, bf16[272,1024]{1,0:T(8,128)(2,1)S(1)}, u32[]{:S(2)}, u32[]{:S(2)}) collective-permute-start(bf16[272,1024]{1,0:T(8,128)(2,1)S(1)} %collective-permute-done.9.refs_1_), channel_id=1, source_target_pairs={{0,1},{1,0},{2,3},{3,2},{4,5},{5,4},{6,7},{7,6},{8,9},{9,8},{10,11... | collective-permute-start | bytes 1671176 | tf_op jit(solution)/shard_map/ppermute | solution.py:45
  55.4 2.7 %collective-permute-start.12 = (bf16[256,1024]{1,0:T(8,128)(2,1)S(1)}, bf16[256,1024]{1,0:T(8,128)(2,1)S(1)}, u32[]{:S(2)}, u32[]{:S(2)}) collective-permute-start(bf16[256,1024]{1,0:T(8,128)(2,1)S(1)} %collective-permute-done.7.refs_5_.refs_6_), channel_id=1, source_target_pairs={{0,1},{1,0},{2,3},{3,2},{4,5},{5,4},{6,7},{7,6},{8,9},{9,8},{10,11... | collective-permute-start | bytes 1572872 | tf_op jit(solution)/shard_map/ppermute | solution.py:45
  55.9 2.9 %collective-permute-start.14 = (bf16[256,1024]{1,0:T(8,128)(2,1)S(1)}, bf16[256,1024]{1,0:T(8,128)(2,1)S(1)}, u32[]{:S(2)}, u32[]{:S(2)}) collective-permute-start(bf16[256,1024]{1,0:T(8,128)(2,1)S(1)} %collective-permute-done.10.refs_2_), channel_id=1, source_target_pairs={{0,1},{1,0},{2,3},{3,2},{4,5},{5,4},{6,7},{7,6},{8,9},{9,8},{10,11... | collective-permute-start | bytes 1572872 | tf_op jit(solution)/shard_map/ppermute | solution.py:45

commit v3 on v2

v3 whole, which is shorter than its diff:
```python
import functools

import jax
import jax.numpy as jnp
import numpy as np
from jax import lax
from jax.experimental import pallas as pl
from jax.experimental.pallas import tpu as pltpu
from jax.sharding import PartitionSpec as P

N = 4
HALF = 256
LEN = 2 * HALF
TAG = 16
VMEM = 24 * 2**20


def device(line, across, core):
    y, z = (across, line) if core == 0 else (line, across)
    return (y * N + z) * 2 + core


PLACES = [(line, across, core) for line in range(N) for across in range(N) for core in range(2)]


def near(i):
    return i ^ 1


def wide(i):
    return N - 1 - i


def along(x, step):
    moves = [(device(i, j, c), device(step(i), j, c)) for i, j, c in PLACES]
    return lax.ppermute(x, "sample", moves)


def over(x, step):
    moves = [(device(i, j, c), device(i, step(j), c)) for i, j, c in PLACES]
    return lax.ppermute(x, "sample", moves)


def swap(x):
    return lax.ppermute(x, "sample", [(i, i ^ 1) for i in range(2 * N * N)])


def unit_kernel(len_ref, emb_ref, out_ref, unit, sem):
    length = len_ref[0]
    lines = lax.broadcasted_iota(jnp.int32, (TAG, unit.shape[1]), 0)
    tag = jnp.where(lines < TAG // 2, length // 16, length % 16)
    unit[LEN : LEN + TAG, :] = tag.astype(jnp.float32).astype(jnp.bfloat16)
    first, stores = None, []
    for n, end in enumerate((HALF, LEN + TAG)):
        start = n * HALF
        values = emb_ref[0, start : start + HALF, :].astype(jnp.float32)
        norm = jnp.sqrt(jnp.sum(values * values, axis=1, keepdims=True) + 1e-06)
        scaled = values / norm
        if first is None:
            first = scaled[0:1, :]
        places = lax.broadcasted_iota(jnp.int32, (HALF, 1), 0) + start
        unit[start : start + HALF, :] = jnp.where(places < length, scaled, first).astype(
            jnp.bfloat16
        )
        store = pltpu.make_async_copy(
            unit.at[start:end, :], out_ref.at[start:end, :], sem.at[n]
        )
        store.start()
        stores.append(store)
    for store in stores:
        store.wait()


def make_unit(lengths, embeddings):
    shape = (LEN + TAG, embeddings.shape[2])
    return pl.pallas_call(
        unit_kernel,
        out_shape=jax.ShapeDtypeStruct(shape, jnp.bfloat16),
        in_specs=[
            pl.BlockSpec(memory_space=pltpu.SMEM),
            pl.BlockSpec(memory_space=pltpu.VMEM),
        ],
        out_specs=pl.BlockSpec(memory_space=pltpu.HBM),
        scratch_shapes=[pltpu.VMEM(shape, jnp.bfloat16), pltpu.SemaphoreType.DMA((2,))],
        compiler_params=pltpu.CompilerParams(vmem_limit_bytes=VMEM),
        name="unit",
    )(lengths, embeddings)


def plan(here):
    core = here % 2
    line, across = (here // 2 % N, here // 2 // N) if core == 0 else (here // 2 // N, here // 2 % N)
    low = across < N // 2

    def mine(i, j):
        return device(i, j, core)

    at = {
        "own": mine(line, across),
        "near": mine(near(line), across),
        "wide": mine(wide(line), across),
        "far": mine((line + 2) % N, across),
        "side": mine(line, wide(across)),
    }
    sender = near(across)
    at["next"] = mine(line, sender if sender in (0, N - 1) else wide(sender))
    for name, place in (
        ("sib", across),
        ("sib_near", near(across)),
        ("sib_wide", wide(across)),
        ("sib_far", (across + 2) % N),
    ):
        at[name] = device(place, line, 1 - core)

    early = [("own", "own")]
    if core == 0:
        early += [("own", "sib"), ("near", "sib")]
    else:
        early += [("near", "sib"), ("near", "sib_near")]
    if line % 2 == 0:
        early += [("own", "near")]
    else:
        early += [("own", "wide")]
    if line in (1, 2):
        early += [("near", "wide")]
    early += [("wide", "sib"), ("wide", "sib_near")]
    if core == 1:
        early += [("wide", "sib_wide")]
    if low:
        middle = [("side", "own"), ("side", "near")]
    else:
        middle = [("side", "wide"), ("side", "far")]
    middle += [("far", "sib"), ("far", "sib_near"), ("far", "sib_wide")]
    if core == 0:
        middle += [("far", "sib_far")]
    late = [("next", "own"), ("next", "near"), ("next", "wide"), ("next", "far")]
    return at, (early, middle, late)


STAGES = (
    ("own", "sib", "near", "sib_near", "wide", "sib_wide"),
    ("side", "own", "near", "wide", "far", "sib", "sib_near", "sib_wide", "sib_far"),
    ("own", "next", "near", "wide", "far"),
)


def make_table(total):
    plans = [plan(i) for i in range(total)]
    tables = []
    for stage, slots in enumerate(STAGES):
        steps = max((len(p[1][stage]) + 1) // 2 for p in plans)
        rows = np.zeros((total, 1 + 2 * steps, 8), np.int32)
        for i, (at, stages) in enumerate(plans):
            pairs = stages[stage]
            rows[i, 0, 0] = (len(pairs) + 1) // 2
            seen = set()
            for k, (u, v) in enumerate(pairs):
                waits = [0, 0]
                for n, s in enumerate((u, v)):
                    if s not in seen:
                        waits[n] = slots.index(s) + 1
                        seen.add(s)
                both = u != "own" or v != "own"
                rows[i, 1 + k] = (slots.index(u), slots.index(v), at[u], at[v], *waits, both, 0)
            if len(pairs) % 2:
                rows[i, 1 + len(pairs), :4] = (slots.index(u), slots.index(v), -1, -1)
            rest = [s for s in slots if s not in seen]
            rows[i, 0, 1] = sum(1 << slots.index(s) for s in rest)
        tables.append(rows.reshape(total, -1))
    starts = np.cumsum([0] + [t.shape[1] for t in tables])
    return np.concatenate(tables, axis=1), starts


def pairs_kernel(base, slots, tab_ref, *refs):
    before_ref, refs = (None, refs) if base == 0 else (refs[0], refs[1:])
    ins = refs[:slots]
    out_ref, tok, tag, sem = refs[slots:]

    def copies(block, s):
        return (
            pltpu.make_async_copy(block.at[0:LEN, :], tok.at[s], sem.at[s, 0]),
            pltpu.make_async_copy(
                block.at[LEN : LEN + TAG, 0:128], tag.at[s], sem.at[s, 1]
            ),
        )

    for s in range(slots):
        for copy in copies(ins[s], s):
            copy.start()

    def arrive(s):
        for copy in copies(ins[0], s):
            copy.wait()

    out_ref[...] = jnp.zeros_like(out_ref) if before_ref is None else before_ref[...]
    owners = lax.broadcasted_iota(jnp.int32, out_ref.shape, 0)
    lanes = lax.broadcasted_iota(jnp.int32, out_ref.shape, 1)
    total = out_ref.shape[0]
    rows = lax.broadcasted_iota(jnp.int32, (LEN, 1), 0).astype(jnp.float32)
    cols = lax.broadcasted_iota(jnp.int32, (1, LEN), 1).astype(jnp.float32)

    def length(s):
        value = tag[s].astype(jnp.float32)
        return value[0:1, 0:1] * 16.0 + value[TAG // 2 : TAG // 2 + 1, 0:1]

    def score(at):
        u, v = tab_ref[at], tab_ref[at + 1]
        own, other, both = tab_ref[at + 2], tab_ref[at + 3], tab_ref[at + 6]
        len_u, len_v = length(u), length(v)
        similar = lax.dot_general(
            tok[u], tok[v], (((1,), (1,)), ((), ())), preferred_element_type=jnp.float32
        )
        best_row = jnp.max(similar, axis=1, keepdims=True)
        best_col = jnp.max(similar, axis=0, keepdims=True)
        ahead = jnp.sum(jnp.where(rows < len_u, best_row, 0.0), axis=0, keepdims=True)
        behind = jnp.sum(jnp.where(cols < len_v, best_col, 0.0), axis=1, keepdims=True)
        ahead = ahead / len_u
        behind = behind / len_v
        at_u = owners == own
        at_v = (owners == other) & (both == 1)
        fore = (at_u & (lanes == other)) | (at_v & (lanes == total + own))
        back = (at_u & (lanes == total + other)) | (at_v & (lanes == own))
        return jnp.where(fore, ahead, 0.0) + jnp.where(back, behind, 0.0)

    @pl.loop(0, tab_ref[base])
    def _(step):
        first = base + 8 + 16 * step
        for wait in (4, 5, 12, 13):

            @pl.when(tab_ref[first + wait] > 0)
            def _():
                arrive(tab_ref[first + wait] - 1)

        out_ref[...] += score(first) + score(first + 8)

    rest = tab_ref[base + 1]
    for s in range(slots):

        @pl.when((rest >> s) % 2 == 1)
        def _():
            arrive(s)


def run_pairs(stage, table, starts, before, blocks):
    arrays = [blocks[name] for name in STAGES[stage]]
    slots, width = len(arrays), arrays[0].shape[1]
    before = [] if before is None else [before]
    steps = ((starts[stage + 1] - starts[stage]) // 8 - 1) // 2
    return pl.pallas_call(
        functools.partial(pairs_kernel, int(starts[stage]), slots),
        out_shape=jax.ShapeDtypeStruct((2 * N * N, 128), jnp.float32),
        in_specs=[pl.BlockSpec(memory_space=pltpu.SMEM)]
        + [pl.BlockSpec(memory_space=pltpu.VMEM)] * len(before)
        + [pl.BlockSpec(memory_space=pltpu.HBM)] * slots,
        out_specs=pl.BlockSpec(memory_space=pltpu.VMEM),
        scratch_shapes=[
            pltpu.VMEM((slots, LEN, width), jnp.bfloat16),
            pltpu.VMEM((slots, TAG, 128), jnp.bfloat16),
            pltpu.SemaphoreType.DMA((slots, 2)),
        ],
        compiler_params=pltpu.CompilerParams(vmem_limit_bytes=VMEM),
        cost_estimate=pl.CostEstimate(
            flops=int(4 * steps * LEN * LEN * width * 2),
            bytes_accessed=slots * LEN * width * 2,
            transcendentals=0,
        ),
        name=f"pairs_{stage}",
    )(table, *before, *arrays)


def after(x, *others):
    return lax.optimization_barrier((x, *others))[0]


def body(embeddings, lengths):
    total = lax.axis_size("sample")
    here = lax.axis_index("sample")
    core, chip = here % 2, here // 2
    across = jnp.where(core == 0, chip // N, chip % N)
    edge = (across == 0) | (across == N - 1)

    tables, starts = make_table(total)
    table = jnp.asarray(tables)[here]
    blocks = {"own": make_unit(lengths, embeddings)}
    blocks["wide"] = along(blocks["own"], wide)
    blocks["near"] = along(blocks["own"], near)
    blocks["sib"] = swap(blocks["own"])
    blocks["side"] = over(after(blocks["own"], blocks["wide"]), wide)
    blocks["far"] = along(after(blocks["wide"], blocks["near"]), near)
    blocks["sib_near"] = swap(blocks["near"])
    blocks["sib_wide"] = swap(blocks["wide"])
    scores = run_pairs(0, table, starts, None, blocks)
    pick = jnp.where(edge, blocks["own"], after(blocks["side"], scores))
    blocks["next"] = over(after(pick, blocks["far"], scores), near)
    blocks["sib_far"] = swap(after(blocks["far"], scores))
    scores = run_pairs(1, table, starts, scores, blocks)
    scores = run_pairs(2, table, starts, scores, blocks)

    parts = lax.all_to_all(scores, "sample", 0, 0, tiled=True)
    result = jnp.sum(parts, axis=0)
    ahead, behind = result[:total], result[total : 2 * total]
    offdiag = jnp.arange(total, dtype=jnp.int32) != here
    utility = jnp.sum(jnp.where(offdiag, ahead + behind, 0.0)) / jnp.float32(2 * (total - 1))
    return ahead[None, :], utility[None]


def solution(mesh):
    in_specs = (P(("prompt", "sample"), None, None), P(("prompt", "sample")))
    out_specs = (P(("prompt", "sample"), None), P(("prompt", "sample")))
    return jax.shard_map(body, mesh=mesh, in_specs=in_specs, out_specs=out_specs, check_vma=False)
```

time: 81.1 us -> 77.2 us (0.952)
  starting transfers between devices: 13.8 us -> 8.38 us
  Pallas kernels: 20.9 us -> 16.9 us
  blocking collectives: 11.4 us -> 15 us
  waiting for transfers between devices: 26.6 us -> 29.6 us
  other arithmetic: 2.27 us -> 1.28 us
    ppermute x2, waiting for transfers between devices: 0.01 us -> 10 us  [over(): return lax.ppermute(x, 'sample', moves)]
    ppermute x6 -> x3, waiting for transfers between devices: 23.6 us -> 19 us  [along(): return lax.ppermute(x, 'sample', moves)]
    ppermute x6 -> x3, starting transfers between devices: 9.1 us -> 4.91 us  [along(): return lax.ppermute(x, 'sample', moves)]
    pallas_call x4, Pallas kernels: 20.9 us -> 16.9 us  [the longest x3 16.3 us: run_pairs(): pl.pallas_call(functools.partial(pairs_kernel, int(starts[stage]), slots)...]
    all_to_all x1, blocking collectives: 11.4 us -> 15 us  [body(): parts = lax.all_to_all(scores, 'sample', 0, 0, tiled=True)]
    ppermute x7 -> x4, waiting for transfers between devices: 2.95 us -> 0.59 us  [swap(): return lax.ppermute(x, 'sample', [(i, i ^ 1) for i in range(2 * N * N)])]
    ppermute x7 -> x4, starting transfers between devices: 1.04 us -> 0.01 us  [swap(): return lax.ppermute(x, 'sample', [(i, i ^ 1) for i in range(2 * N * N)])]
    select_n x1, other arithmetic: 1.11 us -> 0.11 us  [body(): pick = jnp.where(edge, blocks['own'], after(blocks['side'], scores))]
  transfers between devices with their start and end apart: 15 -> 9, of which waited for: 5 -> 6; matrix products, arithmetic and copies ran while one was open for 2% -> 1% of each run, Pallas kernels for 16% -> 16%
where the time goes in v3:
time: 77.2 us; the launch traced here: 76.2 us
  waiting for transfers between devices  29.6 us (38%)
  Pallas kernels  16.9 us (22%)
  blocking collectives  15 us (19%)
  starting transfers between devices  8.38 us (11%)
  between operations  3.11 us (4%)
  local copies, waits for them, and re-layouts  1.92 us (2%)
  other arithmetic  1.28 us (2%)
    ppermute x3, waiting for transfers between devices, along(): return lax.ppermute(x, 'sample', moves)  19 us
    pallas_call x3, Pallas kernels, run_pairs(): pl.pallas_call(functools.partial(pairs_kernel, int(starts[stage]), slots)...  16.3 us
    all_to_all x1, blocking collectives, body(): parts = lax.all_to_all(scores, 'sample', 0, 0, tiled=True)  15 us
    ppermute x2, waiting for transfers between devices, over(): return lax.ppermute(x, 'sample', moves)  10 us
    ppermute x3, starting transfers between devices, along(): return lax.ppermute(x, 'sample', moves)  4.91 us
    ppermute x2, starting transfers between devices, over(): return lax.ppermute(x, 'sample', moves)  3.46 us
  transfers between devices with their start and end apart: 9, of which 6 were waited for; matrix products, arithmetic and copies ran while one was open for 1% of the time, Pallas kernels for 16%

profile of v3, /device:TPU:0, one launch (start us, length us, event | category | flops | bytes accessed | tf_op | source)
XLA Modules:
  0.0 76.2 jit_solution(3594025521546221970)
XLA Ops:
  1.3 0.0 copy-start
  1.3 1.2 %copy-done = bf16[1,512,1024]{2,1,0:T(8,128)(2,1)S(1)} copy-done((bf16[1,512,1024]{2,1,0:T(8,128)(2,1)S(1)}, bf16[1,512,1024]{2,1,0:T(8,128)(2,1)}, u32[]{:S(2)}) %copy-start) | copy-done | bytes 1048600
  2.5 0.6 unit.1.refs_0_.refs_2_.refs_1_
  3.1 2.1 %collective-permute-start.1 = (bf16[528,1024]{1,0:T(8,128)(2,1)S(1)}, bf16[528,1024]{1,0:T(8,128)(2,1)S(1)}, u32[]{:S(2)}, u32[]{:S(2)}) collective-permute-start(bf16[528,1024]{1,0:T(8,128)(2,1)S(1)} %unit.1.refs_0_.refs_2_.refs_1_), channel_id=1, source_target_pairs={{0,2},{1,9},{8,10},{3,11},{16,18},{5,13},{24,26},{7,15},{2,0},{9,1... | collective-permute-start | bytes 3244040 | tf_op jit(solution)/shard_map/ppermute | solution.py:36
  5.2 2.5 %collective-permute-start.3 = (bf16[528,1024]{1,0:T(8,128)(2,1)S(1)}, bf16[528,1024]{1,0:T(8,128)(2,1)}, u32[]{:S(2)}, u32[]{:S(2)}) collective-permute-start(bf16[528,1024]{1,0:T(8,128)(2,1)S(1)} %unit.1.refs_0_.refs_2_.refs_1_), channel_id=1, source_target_pairs={{0,6},{1,25},{8,14},{3,27},{16,22},{5,29},{24,30},{7,31},{2,4},{9,... | collective-permute-start | bytes 3244040 | tf_op jit(solution)/shard_map/ppermute | solution.py:36
  7.7 0.0 collective-permute-start
  7.7 10.6 %collective-permute-done.1.refs_2_.refs_3_ = bf16[528,1024]{1,0:T(8,128)(2,1)S(1)} collective-permute-done((bf16[528,1024]{1,0:T(8,128)(2,1)S(1)}, bf16[528,1024]{1,0:T(8,128)(2,1)S(1)}, u32[]{:S(2)}, u32[]{:S(2)}) %collective-permute-start.1) | collective-permute-done | bytes 1081376 | tf_op jit(solution)/shard_map/ppermute | solution.py:36
  18.4 0.0 collective-permute-start.2
  18.4 3.3 %collective-permute-done.3.refs_4_ = bf16[528,1024]{1,0:T(8,128)(2,1)} collective-permute-done((bf16[528,1024]{1,0:T(8,128)(2,1)S(1)}, bf16[528,1024]{1,0:T(8,128)(2,1)}, u32[]{:S(2)}, u32[]{:S(2)}) %collective-permute-start.3) | collective-permute-done | bytes 1081376 | tf_op jit(solution)/shard_map/ppermute | solution.py:36
  21.7 0.0 collective-permute-start.4
  21.7 0.3 collective-permute-start.6
  22.0 0.7 constant_dynamic-slice_fusion
  22.7 3.0 %collective-permute-start.5 = (bf16[528,1024]{1,0:T(8,128)(2,1)S(1)}, bf16[528,1024]{1,0:T(8,128)(2,1)S(1)}, u32[]{:S(2)}, u32[]{:S(2)}) collective-permute-start(bf16[528,1024]{1,0:T(8,128)(2,1)S(1)} %unit.1.refs_0_.refs_2_.refs_1_), channel_id=1, source_target_pairs={{0,24},{1,7},{8,16},{3,5},{16,8},{5,3},{24,0},{7,1},{2,26},{9,15},... | collective-permute-start | bytes 3244040 | tf_op jit(solution)/shard_map/ppermute | solution.py:41
  25.7 0.0 collective-permute-done.refs_1_.refs_6_
  25.7 0.0 collective-permute-done.2.refs_3_.refs_7_
  25.7 0.0 collective-permute-done.4.refs_5_.refs_8_
  25.7 6.4 %pairs_0.1.refs_0_ = f32[32,128]{1,0:T(8,128)S(1)} custom-call(s32[168]{0:T(256)S(1)} %bitcast.8, bf16[528,1024]{1,0:T(8,128)(2,1)S(1)} %unit.1.refs_0_.refs_2_.refs_1_, bf16[528,1024]{1,0:T(8,128)(2,1)} %collective-permute-done.refs_1_.refs_6_, bf16[528,1024]{1,0:T(8,128)(2,1)S(1)} %collective-permute-done.1.refs_2_.refs_3_, ...), custom_call_target="tpu_custom_call" | custom-call | flops 8589934592 | bytes 6291456 | tf_op jit(solution)/shard_map/pairs_0/pallas_call | solution.py:249
  32.1 5.1 %collective-permute-done.6.refs_5_ = bf16[528,1024]{1,0:T(8,128)(2,1)} collective-permute-done((bf16[528,1024]{1,0:T(8,128)(2,1)}, bf16[528,1024]{1,0:T(8,128)(2,1)}, u32[]{:S(2)}, u32[]{:S(2)}) %collective-permute-start.6) | collective-permute-done | bytes 1081376 | tf_op jit(solution)/shard_map/ppermute | solution.py:36
  37.2 0.0 collective-permute-start.7
  37.2 1.9 %collective-permute-done.5.refs_1_ = bf16[528,1024]{1,0:T(8,128)(2,1)S(1)} collective-permute-done((bf16[528,1024]{1,0:T(8,128)(2,1)S(1)}, bf16[528,1024]{1,0:T(8,128)(2,1)S(1)}, u32[]{:S(2)}, u32[]{:S(2)}) %collective-permute-start.5) | collective-permute-done | bytes 1081376 | tf_op jit(solution)/shard_map/ppermute | solution.py:41
  39.1 0.1 broadcast_select_fusion
  39.2 0.4 collective-permute-start.8
  39.6 0.6 collective-permute-done.7.refs_9_
  40.2 6.1 %pairs_1.1.refs_0_ = f32[32,128]{1,0:T(8,128)S(1)} custom-call(s32[168]{0:T(256)S(1)} %bitcast.9, f32[32,128]{1,0:T(8,128)S(1)} %pairs_0.1.refs_0_, bf16[528,1024]{1,0:T(8,128)(2,1)S(1)} %collective-permute-done.5.refs_1_, bf16[528,1024]{1,0:T(8,128)(2,1)S(1)} %unit.1.refs_0_.refs_2_.refs_1_, bf16[528,1024]{1,0:T(8,128)(2,1)S(1)} %collective-permute-done.1.refs_2_.refs_3_, ...), custom_call_target="tpu_custom_call" | custom-call | flops 6442450944 | bytes 9437184 | tf_op jit(solution)/shard_map/pairs_1/pallas_call | solution.py:249
  46.3 8.1 %collective-permute-done.8.refs_2_ = bf16[528,1024]{1,0:T(8,128)(2,1)S(1)} collective-permute-done((bf16[528,1024]{1,0:T(8,128)(2,1)S(1)}, bf16[528,1024]{1,0:T(8,128)(2,1)S(1)}, u32[]{:S(2)}, u32[]{:S(2)}) %collective-permute-start.8) | collective-permute-done | bytes 1081376 | tf_op jit(solution)/shard_map/ppermute | solution.py:41
  54.4 3.9 %pairs_2.1 = f32[32,128]{1,0:T(8,128)S(1)} custom-call(s32[168]{0:T(256)S(1)} %bitcast.10, f32[32,128]{1,0:T(8,128)S(1)} %pairs_1.1.refs_0_, bf16[528,1024]{1,0:T(8,128)(2,1)S(1)} %unit.1.refs_0_.refs_2_.refs_1_, bf16[528,1024]{1,0:T(8,128)(2,1)S(1)} %collective-permute-done.8.refs_2_, bf16[528,1024]{1,0:T(8,128)(2,1)S(1)} %collective-permute-done.1.refs_2_.refs_3_, ...), custom_call_target="tpu_custom_call" | custom-call | flops 4294967296 | bytes 5242880 | tf_op jit(solution)/shard_map/pairs_2/pallas_call | solution.py:249
  58.3 15.0 %all_to_all.9 = f32[32,1,128]{2,1,0:T(1,128)S(1)} all-to-all(f32[32,1,128]{2,1,0:T(1,128)S(1)} %bitcast.7), channel_id=1, replica_groups=mesh['prompt'=4,'sample'=32] {'sample'}, dimensions={0} | all-to-all | bytes 32768 | tf_op jit(solution)/shard_map/all_to_all | solution.py:299
  73.2 0.1 reduce_sum.18
  73.3 1.1 %fusion = (f32[]{:T(128)}, f32[1,32]{1,0:T(1,128)}) fusion(f32[128]{0:T(128)S(1)} %reduce_sum.18, s32[]{:T(128)S(6)} %axis_index.12), kind=kLoop, calls=%fused_computation.2 | loop fusion | flops 127 | bytes 392 | tf_op jit(solution)/shard_map/reduce_sum | solution.py:303
Async XLA Ops:
  1.3 1.2 %copy-start = (bf16[1,512,1024]{2,1,0:T(8,128)(2,1)S(1)}, bf16[1,512,1024]{2,1,0:T(8,128)(2,1)}, u32[]{:S(2)}) copy-start(bf16[1,512,1024]{2,1,0:T(8,128)(2,1)} %emb_ref.1) | copy-start | bytes 3145732
  3.1 15.2 %collective-permute-start.1 = (bf16[528,1024]{1,0:T(8,128)(2,1)S(1)}, bf16[528,1024]{1,0:T(8,128)(2,1)S(1)}, u32[]{:S(2)}, u32[]{:S(2)}) collective-permute-start(bf16[528,1024]{1,0:T(8,128)(2,1)S(1)} %unit.1.refs_0_.refs_2_.refs_1_), channel_id=1, source_target_pairs={{0,2},{1,9},{8,10},{3,11},{16,18},{5,13},{24,26},{7,15},{2,0},{9,1... | collective-permute-start | bytes 3244040 | tf_op jit(solution)/shard_map/ppermute | solution.py:36
  5.2 16.5 %collective-permute-start.3 = (bf16[528,1024]{1,0:T(8,128)(2,1)S(1)}, bf16[528,1024]{1,0:T(8,128)(2,1)}, u32[]{:S(2)}, u32[]{:S(2)}) collective-permute-start(bf16[528,1024]{1,0:T(8,128)(2,1)S(1)} %unit.1.refs_0_.refs_2_.refs_1_), channel_id=1, source_target_pairs={{0,6},{1,25},{8,14},{3,27},{16,22},{5,29},{24,30},{7,31},{2,4},{9,... | collective-permute-start | bytes 3244040 | tf_op jit(solution)/shard_map/ppermute | solution.py:36
  7.7 18.0 %collective-permute-start = (bf16[528,1024]{1,0:T(8,128)(2,1)S(1)}, bf16[528,1024]{1,0:T(8,128)(2,1)}, u32[]{:S(2)}, u32[]{:S(2)}) collective-permute-start(bf16[528,1024]{1,0:T(8,128)(2,1)S(1)} %unit.1.refs_0_.refs_2_.refs_1_), channel_id=1, source_target_pairs={{0,1},{1,0},{2,3},{3,2},{4,5},{5,4},{6,7},{7,6},{8,9},{9,8},{10,11... | collective-permute-start | bytes 3244040 | tf_op jit(solution)/shard_map/ppermute | solution.py:45
  18.4 7.3 %collective-permute-start.2 = (bf16[528,1024]{1,0:T(8,128)(2,1)S(1)}, bf16[528,1024]{1,0:T(8,128)(2,1)}, u32[]{:S(2)}, u32[]{:S(2)}) collective-permute-start(bf16[528,1024]{1,0:T(8,128)(2,1)S(1)} %collective-permute-done.1.refs_2_.refs_3_), channel_id=1, source_target_pairs={{0,1},{1,0},{2,3},{3,2},{4,5},{5,4},{6,7},{7,6},{8,9},{9,8},{10,11... | collective-permute-start | bytes 3244040 | tf_op jit(solution)/shard_map/ppermute | solution.py:45
  21.7 4.0 %collective-permute-start.4 = (bf16[528,1024]{1,0:T(8,128)(2,1)}, bf16[528,1024]{1,0:T(8,128)(2,1)}, u32[]{:S(2)}, u32[]{:S(2)}) collective-permute-start(bf16[528,1024]{1,0:T(8,128)(2,1)} %collective-permute-done.3.refs_4_), channel_id=1, source_target_pairs={{0,1},{1,0},{2,3},{3,2},{4,5},{5,4},{6,7},{7,6},{8,9},{9,8},{10,11... | collective-permute-start | bytes 3244040 | tf_op jit(solution)/shard_map/ppermute | solution.py:45
  21.7 15.5 %collective-permute-start.6 = (bf16[528,1024]{1,0:T(8,128)(2,1)}, bf16[528,1024]{1,0:T(8,128)(2,1)}, u32[]{:S(2)}, u32[]{:S(2)}) collective-permute-start(bf16[528,1024]{1,0:T(8,128)(2,1)} %collective-permute-done.3.refs_4_), channel_id=1, source_target_pairs={{0,2},{1,9},{8,10},{3,11},{16,18},{5,13},{24,26},{7,15},{2,0},{9,1... | collective-permute-start | bytes 3244040 | tf_op jit(solution)/shard_map/ppermute | solution.py:36
  22.7 16.4 %collective-permute-start.5 = (bf16[528,1024]{1,0:T(8,128)(2,1)S(1)}, bf16[528,1024]{1,0:T(8,128)(2,1)S(1)}, u32[]{:S(2)}, u32[]{:S(2)}) collective-permute-start(bf16[528,1024]{1,0:T(8,128)(2,1)S(1)} %unit.1.refs_0_.refs_2_.refs_1_), channel_id=1, source_target_pairs={{0,24},{1,7},{8,16},{3,5},{16,8},{5,3},{24,0},{7,1},{2,26},{9,15},... | collective-permute-start | bytes 3244040 | tf_op jit(solution)/shard_map/ppermute | solution.py:41
  37.2 3.0 %collective-permute-start.7 = (bf16[528,1024]{1,0:T(8,128)(2,1)}, bf16[528,1024]{1,0:T(8,128)(2,1)}, u32[]{:S(2)}, u32[]{:S(2)}) collective-permute-start(bf16[528,1024]{1,0:T(8,128)(2,1)} %collective-permute-done.6.refs_5_), channel_id=1, source_target_pairs={{0,1},{1,0},{2,3},{3,2},{4,5},{5,4},{6,7},{7,6},{8,9},{9,8},{10,11... | collective-permute-start | bytes 3244040 | tf_op jit(solution)/shard_map/ppermute | solution.py:45
  39.2 15.2 %collective-permute-start.8 = (bf16[528,1024]{1,0:T(8,128)(2,1)S(1)}, bf16[528,1024]{1,0:T(8,128)(2,1)S(1)}, u32[]{:S(2)}, u32[]{:S(2)}) collective-permute-start(bf16[528,1024]{1,0:T(8,128)(2,1)S(1)} %broadcast_select_fusion), channel_id=1, source_target_pairs={{0,8},{1,3},{8,0},{3,1},{16,24},{5,7},{24,16},{7,5},{2,10},{9,11},... | collective-permute-start | bytes 3244040 | tf_op jit(solution)/shard_map/ppermute | solution.py:41

commit v4 on v3

--- a/solution.py
+++ b/solution.py
@@ -112,35 +112,32 @@
     ):
         at[name] = device(place, line, 1 - core)
 
-    early = [("own", "own")]
+    early = [("own", "own"), ("near", "sib"), ("wide", "sib")]
     if core == 0:
-        early += [("own", "sib"), ("near", "sib")]
-    else:
-        early += [("near", "sib"), ("near", "sib_near")]
+        early += [("own", "sib")]
     if line % 2 == 0:
         early += [("own", "near")]
     else:
         early += [("own", "wide")]
     if line in (1, 2):
         early += [("near", "wide")]
-    early += [("wide", "sib"), ("wide", "sib_near")]
-    if core == 1:
-        early += [("wide", "sib_wide")]
     if low:
         middle = [("side", "own"), ("side", "near")]
     else:
         middle = [("side", "wide"), ("side", "far")]
-    middle += [("far", "sib"), ("far", "sib_near"), ("far", "sib_wide")]
+    middle += [("wide", "sib_near"), ("far", "sib"), ("far", "sib_near"), ("far", "sib_wide")]
     if core == 0:
         middle += [("far", "sib_far")]
+    else:
+        middle += [("near", "sib_near"), ("wide", "sib_wide")]
     late = [("next", "own"), ("next", "near"), ("next", "wide"), ("next", "far")]
     return at, (early, middle, late)
 
 
 STAGES = (
-    ("own", "sib", "near", "sib_near", "wide", "sib_wide"),
+    ("own", "near", "sib", "wide"),
     ("side", "own", "near", "wide", "far", "sib", "sib_near", "sib_wide", "sib_far"),
-    ("own", "next", "near", "wide", "far"),
+    ("next", "own", "near", "wide", "far"),
 )
 
 
@@ -171,44 +168,22 @@
     return np.concatenate(tables, axis=1), starts
 
 
-def pairs_kernel(base, slots, tab_ref, *refs):
-    before_ref, refs = (None, refs) if base == 0 else (refs[0], refs[1:])
-    ins = refs[:slots]
-    out_ref, tok, tag, sem = refs[slots:]
-
-    def copies(block, s):
-        return (
-            pltpu.make_async_copy(block.at[0:LEN, :], tok.at[s], sem.at[s, 0]),
-            pltpu.make_async_copy(
-                block.at[LEN : LEN + TAG, 0:128], tag.at[s], sem.at[s, 1]
-            ),
-        )
-
-    for s in range(slots):
-        for copy in copies(ins[s], s):
-            copy.start()
-
-    def arrive(s):
-        for copy in copies(ins[0], s):
-            copy.wait()
-
-    out_ref[...] = jnp.zeros_like(out_ref) if before_ref is None else before_ref[...]
-    owners = lax.broadcasted_iota(jnp.int32, out_ref.shape, 0)
-    lanes = lax.broadcasted_iota(jnp.int32, out_ref.shape, 1)
-    total = out_ref.shape[0]
+def make_score(tab_ref, shape):
+    owners = lax.broadcasted_iota(jnp.int32, shape, 0)
+    lanes = lax.broadcasted_iota(jnp.int32, shape, 1)
+    total = shape[0]
     rows = lax.broadcasted_iota(jnp.int32, (LEN, 1), 0).astype(jnp.float32)
     cols = lax.broadcasted_iota(jnp.int32, (1, LEN), 1).astype(jnp.float32)
 
-    def length(s):
-        value = tag[s].astype(jnp.float32)
+    def length(tag):
+        value = tag.astype(jnp.float32)
         return value[0:1, 0:1] * 16.0 + value[TAG // 2 : TAG // 2 + 1, 0:1]
 
-    def score(at):
-        u, v = tab_ref[at], tab_ref[at + 1]
+    def score(at, tok_u, tok_v, tag_u, tag_v):
         own, other, both = tab_ref[at + 2], tab_ref[at + 3], tab_ref[at + 6]
-        len_u, len_v = length(u), length(v)
+        len_u, len_v = length(tag_u), length(tag_v)
         similar = lax.dot_general(
-            tok[u], tok[v], (((1,), (1,)), ((), ())), preferred_element_type=jnp.float32
+            tok_u, tok_v, (((1,), (1,)), ((), ())), preferred_element_type=jnp.float32
         )
         best_row = jnp.max(similar, axis=1, keepdims=True)
         best_col = jnp.max(similar, axis=0, keepdims=True)
@@ -221,6 +196,52 @@
         fore = (at_u & (lanes == other)) | (at_v & (lanes == total + own))
         back = (at_u & (lanes == total + other)) | (at_v & (lanes == own))
         return jnp.where(fore, ahead, 0.0) + jnp.where(back, behind, 0.0)
+
+    return score
+
+
+def last_kernel(base, tab_ref, before_ref, first_ref, *refs):
+    *others, out_ref = refs
+    score = make_score(tab_ref, out_ref.shape)
+    result = before_ref[...]
+    for k, block in enumerate(others):
+        result += score(
+            base + 8 + 8 * k,
+            first_ref[0:LEN, :],
+            block[0:LEN, :],
+            first_ref[LEN : LEN + TAG, 0:128],
+            block[LEN : LEN + TAG, 0:128],
+        )
+    out_ref[...] = result
+
+
+def pairs_kernel(base, slots, tab_ref, *refs):
+    before_ref, refs = (None, refs) if base == 0 else (refs[0], refs[1:])
+    ins = refs[:slots]
+    out_ref, tok, tag, sem = refs[slots:]
+
+    def copies(block, s):
+        return (
+            pltpu.make_async_copy(block.at[0:LEN, :], tok.at[s], sem.at[s, 0]),
+            pltpu.make_async_copy(
+                block.at[LEN : LEN + TAG, 0:128], tag.at[s], sem.at[s, 1]
+            ),
+        )
+
+    for s in range(slots):
+        for copy in copies(ins[s], s):
+            copy.start()
+
+    def arrive(s):
+        for copy in copies(ins[0], s):
+            copy.wait()
+
+    out_ref[...] = jnp.zeros_like(out_ref) if before_ref is None else before_ref[...]
+    score_of = make_score(tab_ref, out_ref.shape)
+
+    def score(at):
+        u, v = tab_ref[at], tab_ref[at + 1]
+        return score_of(at, tok[u], tok[v], tag[u], tag[v])
 
     @pl.loop(0, tab_ref[base])
     def _(step):
@@ -260,12 +281,26 @@
         ],
         compiler_params=pltpu.CompilerParams(vmem_limit_bytes=VMEM),
         cost_estimate=pl.CostEstimate(
-            flops=int(4 * steps * LEN * LEN * width * 2),
-            bytes_accessed=slots * LEN * width * 2,
+            flops=int(4 * steps * LEN * LEN * width * 2) if stage < 2 else 0,
+            bytes_accessed=slots * LEN * width * 2 if stage < 2 else 0,
             transcendentals=0,
         ),
         name=f"pairs_{stage}",
     )(table, *before, *arrays)
+
+
+def run_last(stage, table, starts, before, blocks):
+    arrays = [blocks[name] for name in STAGES[stage]]
+    return pl.pallas_call(
+        functools.partial(last_kernel, int(starts[stage])),
+        out_shape=jax.ShapeDtypeStruct((2 * N * N, 128), jnp.float32),
+        in_specs=[pl.BlockSpec(memory_space=pltpu.SMEM)]
+        + [pl.BlockSpec(memory_space=pltpu.VMEM)] * (1 + len(arrays)),
+        out_specs=pl.BlockSpec(memory_space=pltpu.VMEM),
+        compiler_params=pltpu.CompilerParams(vmem_limit_bytes=VMEM),
+        cost_estimate=pl.CostEstimate(flops=0, bytes_accessed=0, transcendentals=0),
+        name=f"pairs_{stage}",
+    )(table, before, *arrays)
 
 
 def after(x, *others):
@@ -284,17 +319,17 @@
     blocks = {"own": make_unit(lengths, embeddings)}
     blocks["wide"] = along(blocks["own"], wide)
     blocks["near"] = along(blocks["own"], near)
-    blocks["sib"] = swap(blocks["own"])
+    blocks["sib"] = swap(after(blocks["own"], table))
     blocks["side"] = over(after(blocks["own"], blocks["wide"]), wide)
     blocks["far"] = along(after(blocks["wide"], blocks["near"]), near)
+    scores = run_pairs(0, table, starts, None, blocks)
+    pick = jnp.where(edge, blocks["own"], after(blocks["side"], scores))
+    blocks["next"] = over(pick, near)
     blocks["sib_near"] = swap(blocks["near"])
     blocks["sib_wide"] = swap(blocks["wide"])
-    scores = run_pairs(0, table, starts, None, blocks)
-    pick = jnp.where(edge, blocks["own"], after(blocks["side"], scores))
-    blocks["next"] = over(after(pick, blocks["far"], scores), near)
-    blocks["sib_far"] = swap(after(blocks["far"], scores))
+    blocks["sib_far"] = swap(after(blocks["far"], pick))
     scores = run_pairs(1, table, starts, scores, blocks)
-    scores = run_pairs(2, table, starts, scores, blocks)
+    scores = run_last(2, table, starts, scores, blocks)
 
     parts = lax.all_to_all(scores, "sample", 0, 0, tiled=True)
     result = jnp.sum(parts, axis=0)

time: 77.2 us -> 74.9 us (0.970)
  waiting for transfers between devices: 29.6 us -> 27.4 us
  blocking collectives: 15 us -> 13.2 us
  Pallas kernels: 16.9 us -> 18.6 us
    ppermute x3, waiting for transfers between devices: 19 us -> 14.1 us  [along(): return lax.ppermute(x, 'sample', moves)]
    pallas_call x0 -> x1, Pallas kernels: none -> 3.79 us  [run_last(): pl.pallas_call(functools.partial(last_kernel, int(starts[stage])), out_sh...]
    pallas_call x3 -> x2, Pallas kernels: 16.3 us -> 14.2 us  [run_pairs(): pl.pallas_call(functools.partial(pairs_kernel, int(starts[stage]), slots)...]
    all_to_all x1, blocking collectives: 15 us -> 13.2 us  [body(): parts = lax.all_to_all(scores, 'sample', 0, 0, tiled=True)]
    ppermute x4, waiting for transfers between devices: 0.59 us -> 2.34 us  [swap(): return lax.ppermute(x, 'sample', [(i, i ^ 1) for i in range(2 * N * N)])]
    ppermute x2, waiting for transfers between devices: 10 us -> 10.9 us  [over(): return lax.ppermute(x, 'sample', moves)]
  transfers between devices with their start and end apart: 9 -> 9, of which waited for: 6 -> 5; matrix products, arithmetic and copies ran while one was open for 1% -> 1% of each run, Pallas kernels for 16% -> 19%
where the time goes in v4:
time: 74.9 us; the launch traced here: 73.8 us
  waiting for transfers between devices  27.4 us (37%)
  Pallas kernels  18.6 us (25%)
  blocking collectives  13.2 us (18%)
  starting transfers between devices  8.31 us (11%)
  between operations  3.11 us (4%)
  local copies, waits for them, and re-layouts  1.92 us (3%)
  other arithmetic  1.28 us (2%)
    pallas_call x2, Pallas kernels, run_pairs(): pl.pallas_call(functools.partial(pairs_kernel, int(starts[stage]), slots)...  14.2 us
    ppermute x3, waiting for transfers between devices, along(): return lax.ppermute(x, 'sample', moves)  14.1 us
    all_to_all x1, blocking collectives, body(): parts = lax.all_to_all(scores, 'sample', 0, 0, tiled=True)  13.2 us
    ppermute x2, waiting for transfers between devices, over(): return lax.ppermute(x, 'sample', moves)  10.9 us
    ppermute x3, starting transfers between devices, along(): return lax.ppermute(x, 'sample', moves)  4.21 us
    pallas_call x1, Pallas kernels, run_last(): pl.pallas_call(functools.partial(last_kernel, int(starts[stage])), out_sh...  3.79 us
    ppermute x2, starting transfers between devices, over(): return lax.ppermute(x, 'sample', moves)  3.59 us
    ppermute x4, waiting for transfers between devices, swap(): return lax.ppermute(x, 'sample', [(i, i ^ 1) for i in range(2 * N * N)])  2.34 us
  transfers between devices with their start and end apart: 9, of which 5 were waited for; matrix products, arithmetic and copies ran while one was open for 1% of the time, Pallas kernels for 19%

profile of v4, /device:TPU:0, one launch (start us, length us, event | category | flops | bytes accessed | tf_op | source)
XLA Modules:
  0.0 73.8 jit_solution(4892811469549961675)
XLA Ops:
  1.3 0.0 copy-start
  1.3 1.2 %copy-done = bf16[1,512,1024]{2,1,0:T(8,128)(2,1)S(1)} copy-done((bf16[1,512,1024]{2,1,0:T(8,128)(2,1)S(1)}, bf16[1,512,1024]{2,1,0:T(8,128)(2,1)}, u32[]{:S(2)}) %copy-start) | copy-done | bytes 1048600
  2.5 0.6 unit.1.refs_0_.refs_2_
  3.1 4.2 %collective-permute-start.2 = (bf16[528,1024]{1,0:T(8,128)(2,1)S(1)}, bf16[528,1024]{1,0:T(8,128)(2,1)S(1)}, u32[]{:S(2)}, u32[]{:S(2)}) collective-permute-start(bf16[528,1024]{1,0:T(8,128)(2,1)S(1)} %unit.1.refs_0_.refs_2_), channel_id=1, source_target_pairs={{0,6},{1,25},{8,14},{3,27},{16,22},{5,29},{24,30},{7,31},{2,4},{9,... | collective-permute-start | bytes 3244040 | tf_op jit(solution)/shard_map/ppermute | solution.py:36
  7.3 0.0 collective-permute-start
  7.3 0.7 constant_dynamic-slice_fusion
  8.0 0.0 collective-permute-start.1
  8.1 12.4 %collective-permute-done.2.refs_3_.refs_4_.refs_2_ = bf16[528,1024]{1,0:T(8,128)(2,1)S(1)} collective-permute-done((bf16[528,1024]{1,0:T(8,128)(2,1)S(1)}, bf16[528,1024]{1,0:T(8,128)(2,1)S(1)}, u32[]{:S(2)}, u32[]{:S(2)}) %collective-permute-start.2) | collective-permute-done | bytes 1081376 | tf_op jit(solution)/shard_map/ppermute | solution.py:36
  20.5 3.0 %collective-permute-start.3 = (bf16[528,1024]{1,0:T(8,128)(2,1)S(1)}, bf16[528,1024]{1,0:T(8,128)(2,1)}, u32[]{:S(2)}, u32[]{:S(2)}) collective-permute-start(bf16[528,1024]{1,0:T(8,128)(2,1)S(1)} %unit.1.refs_0_.refs_2_), channel_id=1, source_target_pairs={{0,24},{1,7},{8,16},{3,5},{16,8},{5,3},{24,0},{7,1},{2,26},{9,15},... | collective-permute-start | bytes 3244040 | tf_op jit(solution)/shard_map/ppermute | solution.py:41
  23.5 0.0 collective-permute-done.refs_1_.refs_3_
  23.5 0.0 collective-permute-start.4
  23.5 0.0 collective-permute-start.6
  23.5 0.5 collective-permute-start.5
  24.0 0.0 collective-permute-done.1.refs_2_.refs_6_
  24.0 6.4 %pairs_0.1.refs_0_ = f32[32,128]{1,0:T(8,128)S(1)} custom-call(s32[168]{0:T(256)S(1)} %bitcast.8, bf16[528,1024]{1,0:T(8,128)(2,1)S(1)} %unit.1.refs_0_.refs_2_, bf16[528,1024]{1,0:T(8,128)(2,1)S(1)} %collective-permute-done.refs_1_.refs_3_, bf16[528,1024]{1,0:T(8,128)(2,1)} %collective-permute-done.1.refs_2_.refs_6_, ...), custom_call_target="tpu_custom_call" | custom-call | flops 6442450944 | bytes 4194304 | tf_op jit(solution)/shard_map/pairs_0/pallas_call | solution.py:270
  30.4 6.5 %collective-permute-done.3.refs_1_ = bf16[528,1024]{1,0:T(8,128)(2,1)} collective-permute-done((bf16[528,1024]{1,0:T(8,128)(2,1)S(1)}, bf16[528,1024]{1,0:T(8,128)(2,1)}, u32[]{:S(2)}, u32[]{:S(2)}) %collective-permute-start.3) | collective-permute-done | bytes 1081376 | tf_op jit(solution)/shard_map/ppermute | solution.py:41
  36.9 0.1 broadcast_select_fusion
  37.1 1.7 %collective-permute-done.4.refs_5_.refs_3_ = bf16[528,1024]{1,0:T(8,128)(2,1)} collective-permute-done((bf16[528,1024]{1,0:T(8,128)(2,1)S(1)}, bf16[528,1024]{1,0:T(8,128)(2,1)}, u32[]{:S(2)}, u32[]{:S(2)}) %collective-permute-start.4) | collective-permute-done | bytes 1081376 | tf_op jit(solution)/shard_map/ppermute | solution.py:36
  38.7 0.0 collective-permute-start.7
  38.8 0.6 collective-permute-start.8
  39.3 0.0 collective-permute-done.6.refs_8_
  39.3 0.0 collective-permute-done.5.refs_7_
  39.3 2.3 %collective-permute-done.7.refs_9_ = bf16[528,1024]{1,0:T(8,128)(2,1)S(1)} collective-permute-done((bf16[528,1024]{1,0:T(8,128)(2,1)}, bf16[528,1024]{1,0:T(8,128)(2,1)S(1)}, u32[]{:S(2)}, u32[]{:S(2)}) %collective-permute-start.7) | collective-permute-done | bytes 1081376 | tf_op jit(solution)/shard_map/ppermute | solution.py:45
  41.7 7.8 %pairs_1.1.before_ref = f32[32,128]{1,0:T(8,128)S(1)} custom-call(s32[168]{0:T(256)S(1)} %bitcast.9, f32[32,128]{1,0:T(8,128)S(1)} %pairs_0.1.refs_0_, bf16[528,1024]{1,0:T(8,128)(2,1)} %collective-permute-done.3.refs_1_, bf16[528,1024]{1,0:T(8,128)(2,1)S(1)} %unit.1.refs_0_.refs_2_, bf16[528,1024]{1,0:T(8,128)(2,1)S(1)} %collective-permute-done.refs_1_.refs_3_, ...), custom_call_target="tpu_custom_call" | custom-call | flops 8589934592 | bytes 9437184 | tf_op jit(solution)/shard_map/pairs_1/pallas_call | solution.py:270
  49.5 4.4 %collective-permute-done.8.first_ref = bf16[528,1024]{1,0:T(8,128)(2,1)S(1)} collective-permute-done((bf16[528,1024]{1,0:T(8,128)(2,1)S(1)}, bf16[528,1024]{1,0:T(8,128)(2,1)S(1)}, u32[]{:S(2)}, u32[]{:S(2)}) %collective-permute-start.8) | collective-permute-done | bytes 1081376 | tf_op jit(solution)/shard_map/ppermute | solution.py:41
  53.9 3.8 %pairs_2.1 = f32[32,128]{1,0:T(8,128)S(1)} custom-call(s32[168]{0:T(256)S(1)} %bitcast.10, f32[32,128]{1,0:T(8,128)S(1)} %pairs_1.1.before_ref, bf16[528,1024]{1,0:T(8,128)(2,1)S(1)} %collective-permute-done.8.first_ref, bf16[528,1024]{1,0:T(8,128)(2,1)S(1)} %unit.1.refs_0_.refs_2_, bf16[528,1024]{1,0:T(8,128)(2,1)S(1)} %collective-permute-done.refs_1_.refs_3_, ...), custom_call_target="tpu_custom_call" | custom-call | tf_op jit(solution)/shard_map/pairs_2/pallas_call | solution.py:294
  57.7 13.2 %all_to_all.9 = f32[32,1,128]{2,1,0:T(1,128)S(1)} all-to-all(f32[32,1,128]{2,1,0:T(1,128)S(1)} %bitcast.7), channel_id=1, replica_groups=mesh['prompt'=4,'sample'=32] {'sample'}, dimensions={0} | all-to-all | bytes 32768 | tf_op jit(solution)/shard_map/all_to_all | solution.py:334
  70.9 0.1 reduce_sum.18
  71.0 1.1 %fusion = (f32[]{:T(128)}, f32[1,32]{1,0:T(1,128)}) fusion(f32[128]{0:T(128)S(1)} %reduce_sum.18, s32[]{:T(128)S(6)} %axis_index.12), kind=kLoop, calls=%fused_computation.2 | loop fusion | flops 127 | bytes 392 | tf_op jit(solution)/shard_map/reduce_sum | solution.py:338
Async XLA Ops:
  1.3 1.2 %copy-start = (bf16[1,512,1024]{2,1,0:T(8,128)(2,1)S(1)}, bf16[1,512,1024]{2,1,0:T(8,128)(2,1)}, u32[]{:S(2)}) copy-start(bf16[1,512,1024]{2,1,0:T(8,128)(2,1)} %emb_ref.1) | copy-start | bytes 3145732
  3.1 17.3 %collective-permute-start.2 = (bf16[528,1024]{1,0:T(8,128)(2,1)S(1)}, bf16[528,1024]{1,0:T(8,128)(2,1)S(1)}, u32[]{:S(2)}, u32[]{:S(2)}) collective-permute-start(bf16[528,1024]{1,0:T(8,128)(2,1)S(1)} %unit.1.refs_0_.refs_2_), channel_id=1, source_target_pairs={{0,6},{1,25},{8,14},{3,27},{16,22},{5,29},{24,30},{7,31},{2,4},{9,... | collective-permute-start | bytes 3244040 | tf_op jit(solution)/shard_map/ppermute | solution.py:36
  7.3 16.1 %collective-permute-start = (bf16[528,1024]{1,0:T(8,128)(2,1)S(1)}, bf16[528,1024]{1,0:T(8,128)(2,1)S(1)}, u32[]{:S(2)}, u32[]{:S(2)}) collective-permute-start(bf16[528,1024]{1,0:T(8,128)(2,1)S(1)} %unit.1.refs_0_.refs_2_), channel_id=1, source_target_pairs={{0,2},{1,9},{8,10},{3,11},{16,18},{5,13},{24,26},{7,15},{2,0},{9,1... | collective-permute-start | bytes 3244040 | tf_op jit(solution)/shard_map/ppermute | solution.py:36
  8.0 16.0 %collective-permute-start.1 = (bf16[528,1024]{1,0:T(8,128)(2,1)S(1)}, bf16[528,1024]{1,0:T(8,128)(2,1)}, u32[]{:S(2)}, u32[]{:S(2)}) collective-permute-start(bf16[528,1024]{1,0:T(8,128)(2,1)S(1)} %unit.1.refs_0_.refs_2_), channel_id=1, source_target_pairs={{0,1},{1,0},{2,3},{3,2},{4,5},{5,4},{6,7},{7,6},{8,9},{9,8},{10,11... | collective-permute-start | bytes 3244040 | tf_op jit(solution)/shard_map/ppermute | solution.py:45
  20.5 16.5 %collective-permute-start.3 = (bf16[528,1024]{1,0:T(8,128)(2,1)S(1)}, bf16[528,1024]{1,0:T(8,128)(2,1)}, u32[]{:S(2)}, u32[]{:S(2)}) collective-permute-start(bf16[528,1024]{1,0:T(8,128)(2,1)S(1)} %unit.1.refs_0_.refs_2_), channel_id=1, source_target_pairs={{0,24},{1,7},{8,16},{3,5},{16,8},{5,3},{24,0},{7,1},{2,26},{9,15},... | collective-permute-start | bytes 3244040 | tf_op jit(solution)/shard_map/ppermute | solution.py:41
  23.5 15.3 %collective-permute-start.4 = (bf16[528,1024]{1,0:T(8,128)(2,1)S(1)}, bf16[528,1024]{1,0:T(8,128)(2,1)}, u32[]{:S(2)}, u32[]{:S(2)}) collective-permute-start(bf16[528,1024]{1,0:T(8,128)(2,1)S(1)} %collective-permute-done.2.refs_3_.refs_4_.refs_2_), channel_id=1, source_target_pairs={{0,2},{1,9},{8,10},{3,11},{16,18},{5,13},{24,26},{7,15},{2,0},{9,1... | collective-permute-start | bytes 3244040 | tf_op jit(solution)/shard_map/ppermute | solution.py:36
  23.5 15.8 %collective-permute-start.6 = (bf16[528,1024]{1,0:T(8,128)(2,1)S(1)}, bf16[528,1024]{1,0:T(8,128)(2,1)S(1)}, u32[]{:S(2)}, u32[]{:S(2)}) collective-permute-start(bf16[528,1024]{1,0:T(8,128)(2,1)S(1)} %collective-permute-done.2.refs_3_.refs_4_.refs_2_), channel_id=1, source_target_pairs={{0,1},{1,0},{2,3},{3,2},{4,5},{5,4},{6,7},{7,6},{8,9},{9,8},{10,11... | collective-permute-start | bytes 3244040 | tf_op jit(solution)/shard_map/ppermute | solution.py:45
  23.5 15.8 %collective-permute-start.5 = (bf16[528,1024]{1,0:T(8,128)(2,1)S(1)}, bf16[528,1024]{1,0:T(8,128)(2,1)S(1)}, u32[]{:S(2)}, u32[]{:S(2)}) collective-permute-start(bf16[528,1024]{1,0:T(8,128)(2,1)S(1)} %collective-permute-done.refs_1_.refs_3_), channel_id=1, source_target_pairs={{0,1},{1,0},{2,3},{3,2},{4,5},{5,4},{6,7},{7,6},{8,9},{9,8},{10,11... | collective-permute-start | bytes 3244040 | tf_op jit(solution)/shard_map/ppermute | solution.py:45
  38.7 2.9 %collective-permute-start.7 = (bf16[528,1024]{1,0:T(8,128)(2,1)}, bf16[528,1024]{1,0:T(8,128)(2,1)S(1)}, u32[]{:S(2)}, u32[]{:S(2)}) collective-permute-start(bf16[528,1024]{1,0:T(8,128)(2,1)} %collective-permute-done.4.refs_5_.refs_3_), channel_id=1, source_target_pairs={{0,1},{1,0},{2,3},{3,2},{4,5},{5,4},{6,7},{7,6},{8,9},{9,8},{10,11... | collective-permute-start | bytes 3244040 | tf_op jit(solution)/shard_map/ppermute | solution.py:45
  38.8 15.2 %collective-permute-start.8 = (bf16[528,1024]{1,0:T(8,128)(2,1)S(1)}, bf16[528,1024]{1,0:T(8,128)(2,1)S(1)}, u32[]{:S(2)}, u32[]{:S(2)}) collective-permute-start(bf16[528,1024]{1,0:T(8,128)(2,1)S(1)} %broadcast_select_fusion), channel_id=1, source_target_pairs={{0,8},{1,3},{8,0},{3,1},{16,24},{5,7},{24,16},{7,5},{2,10},{9,11},... | collective-permute-start | bytes 3244040 | tf_op jit(solution)/shard_map/ppermute | solution.py:41

commit v5 on v3

v5 whole, which is shorter than its diff:
```python
import functools

import jax
import jax.numpy as jnp
import numpy as np
from jax import lax
from jax.experimental import pallas as pl
from jax.experimental.pallas import tpu as pltpu
from jax.sharding import PartitionSpec as P

N = 4
HALF = 256
LEN = 2 * HALF
TAG = 16
VMEM = 24 * 2**20


def device(line, across, core):
    y, z = (across, line) if core == 0 else (line, across)
    return (y * N + z) * 2 + core


PLACES = [(line, across, core) for line in range(N) for across in range(N) for core in range(2)]


def near(i):
    return i ^ 1


def wide(i):
    return N - 1 - i


def along(x, step):
    moves = [(device(i, j, c), device(step(i), j, c)) for i, j, c in PLACES]
    return lax.ppermute(x, "sample", moves)


def over(x, step):
    moves = [(device(i, j, c), device(i, step(j), c)) for i, j, c in PLACES]
    return lax.ppermute(x, "sample", moves)


def swap(x):
    return lax.ppermute(x, "sample", [(i, i ^ 1) for i in range(2 * N * N)])


def unit_kernel(len_ref, emb_ref, out_ref, unit, sem):
    length = len_ref[0]
    lines = lax.broadcasted_iota(jnp.int32, (TAG, unit.shape[1]), 0)
    tag = jnp.where(lines < TAG // 2, length // 16, length % 16)
    unit[LEN : LEN + TAG, :] = tag.astype(jnp.float32).astype(jnp.bfloat16)
    first, stores = None, []
    for n, end in enumerate((HALF, LEN + TAG)):
        start = n * HALF
        values = emb_ref[0, start : start + HALF, :].astype(jnp.float32)
        norm = jnp.sqrt(jnp.sum(values * values, axis=1, keepdims=True) + 1e-06)
        scaled = values / norm
        if first is None:
            first = scaled[0:1, :]
        places = lax.broadcasted_iota(jnp.int32, (HALF, 1), 0) + start
        unit[start : start + HALF, :] = jnp.where(places < length, scaled, first).astype(
            jnp.bfloat16
        )
        store = pltpu.make_async_copy(
            unit.at[start:end, :], out_ref.at[start:end, :], sem.at[n]
        )
        store.start()
        stores.append(store)
    for store in stores:
        store.wait()


def make_unit(lengths, embeddings):
    shape = (LEN + TAG, embeddings.shape[2])
    return pl.pallas_call(
        unit_kernel,
        out_shape=jax.ShapeDtypeStruct(shape, jnp.bfloat16),
        in_specs=[
            pl.BlockSpec(memory_space=pltpu.SMEM),
            pl.BlockSpec(memory_space=pltpu.VMEM),
        ],
        out_specs=pl.BlockSpec(memory_space=pltpu.HBM),
        scratch_shapes=[pltpu.VMEM(shape, jnp.bfloat16), pltpu.SemaphoreType.DMA((2,))],
        compiler_params=pltpu.CompilerParams(vmem_limit_bytes=VMEM),
        name="unit",
    )(lengths, embeddings)


NAMES = (
    "own",
    "near",
    "wide",
    "far",
    "side",
    "next",
    "sib",
    "sib_near",
    "sib_wide",
    "sib_far",
)
FLAGS = ("even", "odd", "inner", "low", "high", "first", "second")
STAGES = (
    (
        (None, (("near", "sib"), ("wide", "sib"))),
        ("even", (("own", "near"),)),
        ("odd", (("own", "wide"),)),
        ("inner", (("near", "wide"),)),
    ),
    (
        (None, (("far", "sib"), ("far", "sib_near"), ("wide", "sib_near"))),
        ("low", (("side", "own"), ("side", "near"))),
        ("high", (("side", "wide"), ("side", "far"))),
        ("second", (("near", "sib_near"),)),
    ),
    (
        (None, (("far", "sib_wide"),)),
        ("first", (("far", "sib_far"),)),
        ("second", (("wide", "sib_wide"),)),
    ),
    ((None, (("next", "own"), ("next", "near"), ("next", "wide"), ("next", "far"))),),
)


def plan(here):
    core = here % 2
    line, across = (here // 2 % N, here // 2 // N) if core == 0 else (here // 2 // N, here // 2 % N)
    sender = near(across)
    low = across < N // 2
    samples = (
        here,
        device(near(line), across, core),
        device(wide(line), across, core),
        device((line + 2) % N, across, core),
        device(line, wide(across), core),
        device(line, sender if sender in (0, N - 1) else wide(sender), core),
        device(across, line, 1 - core),
        device(near(across), line, 1 - core),
        device(wide(across), line, 1 - core),
        device((across + 2) % N, line, 1 - core),
    )
    flags = (line % 2 == 0, line % 2 == 1, line in (1, 2), low, not low, core == 0, core == 1)
    return np.array(samples + flags, np.int32)


def make_score(shape):
    owners = lax.broadcasted_iota(jnp.int32, shape, 0)
    lanes = lax.broadcasted_iota(jnp.int32, shape, 1)
    total = shape[0]
    rows = lax.broadcasted_iota(jnp.int32, (LEN, 1), 0).astype(jnp.float32)
    cols = lax.broadcasted_iota(jnp.int32, (1, LEN), 1).astype(jnp.float32)

    def length(tag):
        value = tag.astype(jnp.float32)
        return value[0:1, 0:1] * 16.0 + value[TAG // 2 : TAG // 2 + 1, 0:1]

    def score(own, other, both, tok_u, tok_v, tag_u, tag_v):
        len_u, len_v = length(tag_u), length(tag_v)
        similar = lax.dot_general(
            tok_u, tok_v, (((1,), (1,)), ((), ())), preferred_element_type=jnp.float32
        )
        best_row = jnp.max(similar, axis=1, keepdims=True)
        best_col = jnp.max(similar, axis=0, keepdims=True)
        ahead = jnp.sum(jnp.where(rows < len_u, best_row, 0.0), axis=0, keepdims=True)
        behind = jnp.sum(jnp.where(cols < len_v, best_col, 0.0), axis=1, keepdims=True)
        ahead = ahead / len_u
        behind = behind / len_v
        at_u = owners == own
        at_v = (owners == other) & (both == 1)
        fore = (at_u & (lanes == other)) | (at_v & (lanes == total + own))
        back = (at_u & (lanes == total + other)) | (at_v & (lanes == own))
        return jnp.where(fore, ahead, 0.0) + jnp.where(back, behind, 0.0)

    return score


def first_kernel(here_ref, own_ref, sib_ref, out_ref):
    score = make_score(out_ref.shape)
    here = here_ref[0]
    owner = jnp.where(here % 2 == 0, here, -1)
    own, own_tag = own_ref[0:LEN, :], own_ref[LEN : LEN + TAG, 0:128]
    out_ref[...] = score(here, here, 0, own, own, own_tag, own_tag) + score(
        owner, here + 1, 1 - here % 2, own, sib_ref[0:LEN, :], own_tag, sib_ref[LEN : LEN + TAG, 0:128]
    )


def run_first(here, own, sib):
    return pl.pallas_call(
        first_kernel,
        out_shape=jax.ShapeDtypeStruct((2 * N * N, 128), jnp.float32),
        in_specs=[pl.BlockSpec(memory_space=pltpu.SMEM)]
        + [pl.BlockSpec(memory_space=pltpu.VMEM)] * 2,
        out_specs=pl.BlockSpec(memory_space=pltpu.VMEM),
        compiler_params=pltpu.CompilerParams(vmem_limit_bytes=VMEM),
        cost_estimate=pl.CostEstimate(
            flops=4 * LEN * LEN * own.shape[1], bytes_accessed=2 * own.size, transcendentals=0
        ),
        name="pairs_0",
    )(here, own, sib)


def pairs_kernel(stage, names, parts, keep, tab_ref, before_ref, *refs):
    ins, out_ref = refs[: sum(parts)], refs[sum(parts)]
    score_of = make_score(out_ref.shape)
    blocks, place = {}, 0
    for name, count in zip(names, parts):
        blocks[name] = ins[place : place + count]
        place += count

    if keep:
        refs[-1][...] = blocks[keep][0][...]

    def tokens(name):
        *heads, last = blocks[name]
        rows = LEN - sum(head.shape[0] for head in heads)
        pieces = [head[...] for head in heads] + [last[0:rows, :]]
        pieces = pieces[0] if len(pieces) == 1 else jnp.concatenate(pieces, axis=0)
        return pieces, last[rows : rows + TAG, 0:128]

    def score(pairs):
        result = None
        for u, v in pairs:
            (tok_u, tag_u), (tok_v, tag_v) = tokens(u), tokens(v)
            own, other = tab_ref[NAMES.index(u)], tab_ref[NAMES.index(v)]
            part = score_of(own, other, 1, tok_u, tok_v, tag_u, tag_v)
            result = part if result is None else result + part
        return result

    result = before_ref[...]
    for flag, pairs in STAGES[stage]:
        if flag is None:
            out_ref[...] = result + score(pairs)
        else:

            @pl.when(tab_ref[len(NAMES) + FLAGS.index(flag)] == 1)
            def _():
                out_ref[...] += score(pairs)


def run_pairs(stage, table, before, blocks, keep=None):
    groups = [pair for _, pairs in STAGES[stage] for pair in pairs]
    names = sorted({name for pair in groups for name in pair} | ({keep} if keep else set()))
    chosen = [blocks[name] for name in names]
    chosen = [block if isinstance(block, tuple) else (block,) for block in chosen]
    arrays = [part for block in chosen for part in block]
    width = arrays[0].shape[1]
    hide = stage < 2
    outs = [jax.ShapeDtypeStruct(before.shape, jnp.float32)]
    outs += [jax.ShapeDtypeStruct(blocks[keep].shape, jnp.bfloat16)] if keep else []
    return pl.pallas_call(
        functools.partial(pairs_kernel, stage, names, [len(b) for b in chosen], keep),
        out_shape=outs,
        in_specs=[pl.BlockSpec(memory_space=pltpu.SMEM)]
        + [pl.BlockSpec(memory_space=pltpu.VMEM)] * (1 + len(arrays)),
        out_specs=[pl.BlockSpec(memory_space=pltpu.VMEM)] * len(outs),
        compiler_params=pltpu.CompilerParams(vmem_limit_bytes=VMEM),
        cost_estimate=pl.CostEstimate(
            flops=2 * len(groups) * LEN * LEN * width if hide else 0,
            bytes_accessed=len(names) * LEN * width * 2 if hide else 0,
            transcendentals=0,
        ),
        name=f"pairs_{stage + 1}",
    )(table, before, *arrays)


def after(x, *others):
    return lax.optimization_barrier((x, *others))[0]


def body(embeddings, lengths):
    total = lax.axis_size("sample")
    here = lax.axis_index("sample")
    core, chip = here % 2, here // 2
    across = jnp.where(core == 0, chip // N, chip % N)
    edge = (across == 0) | (across == N - 1)

    blocks = {"own": make_unit(lengths, embeddings)}
    table = jnp.asarray(np.stack([plan(i) for i in range(total)]))[here]
    blocks["wide"] = along(blocks["own"], wide)
    blocks["near"] = along(blocks["own"], near)
    blocks["sib"] = swap(after(blocks["own"], table))
    scores = run_first(here[None], blocks["own"], blocks["sib"])
    blocks["side"] = over(after(blocks["own"], blocks["wide"]), wide)
    blocks["far"] = along(after(blocks["wide"], blocks["near"]), near)
    blocks["sib_near"] = swap(blocks["near"])
    blocks["sib_wide"] = swap(blocks["wide"])
    (scores,) = run_pairs(0, table, scores, blocks)
    pick = jnp.where(edge, blocks["own"], after(blocks["side"], scores))
    blocks["next"] = over(pick, near)
    (scores,) = run_pairs(1, table, after(scores, pick), blocks)
    far = after(blocks["far"], scores)
    blocks["sib_far"] = (swap(far[:HALF]), swap(far[HALF:]))
    scores, blocks["near"] = run_pairs(2, table, scores, blocks, keep="near")
    (scores,) = run_pairs(3, table, scores, blocks)

    parts = lax.all_to_all(scores, "sample", 0, 0, tiled=True)
    result = jnp.sum(parts, axis=0)
    ahead, behind = result[:total], result[total : 2 * total]
    offdiag = jnp.arange(total, dtype=jnp.int32) != here
    utility = jnp.sum(jnp.where(offdiag, ahead + behind, 0.0)) / jnp.float32(2 * (total - 1))
    return ahead[None, :], utility[None]


def solution(mesh):
    in_specs = (P(("prompt", "sample"), None, None), P(("prompt", "sample")))
    out_specs = (P(("prompt", "sample"), None), P(("prompt", "sample")))
    return jax.shard_map(body, mesh=mesh, in_specs=in_specs, out_specs=out_specs, check_vma=False)
```

time: 77.2 us -> 74.1 us (0.960)
  waiting for transfers between devices: 29.6 us -> 22.7 us
  Pallas kernels: 16.9 us -> 19 us
  starting transfers between devices: 8.38 us -> 10.2 us
    ppermute x3, waiting for transfers between devices: 19 us -> 12.7 us  [along(): return lax.ppermute(x, 'sample', moves)]
    ppermute x2, waiting for transfers between devices: 10 us -> 7.9 us  [over(): return lax.ppermute(x, 'sample', moves)]
    pallas_call x3 -> x5, Pallas kernels: 16.3 us -> 18.4 us  [the longest x4 15.7 us: run_pairs(): pl.pallas_call(functools.partial(pairs_kernel, stage, names, [len(b) for...]
    ppermute x4 -> x5, waiting for transfers between devices: 0.59 us -> 2.09 us  [swap(): return lax.ppermute(x, 'sample', [(i, i ^ 1) for i in range(2 * N * N)])]
    ppermute x4 -> x5, starting transfers between devices: 0.01 us -> 1.29 us  [swap(): return lax.ppermute(x, 'sample', [(i, i ^ 1) for i in range(2 * N * N)])]
    ppermute x2, starting transfers between devices: 3.46 us -> 4.69 us  [over(): return lax.ppermute(x, 'sample', moves)]
  transfers between devices with their start and end apart: 9 -> 10, of which waited for: 6 -> 5; matrix products, arithmetic and copies ran while one was open for 1% -> 1% of each run, Pallas kernels for 16% -> 21%
where the time goes in v5:
time: 74.1 us; the launch traced here: 73 us
  waiting for transfers between devices  22.7 us (31%)
  Pallas kernels  19 us (26%)
  blocking collectives  14.7 us (20%)
  starting transfers between devices  10.2 us (14%)
  between operations  3.12 us (4%)
  local copies, waits for them, and re-layouts  1.98 us (3%)
  other arithmetic  1.27 us (2%)
    pallas_call x4, Pallas kernels, run_pairs(): pl.pallas_call(functools.partial(pairs_kernel, stage, names, [len(b) for...  15.7 us
    all_to_all x1, blocking collectives, body(): parts = lax.all_to_all(scores, 'sample', 0, 0, tiled=True)  14.7 us
    ppermute x3, waiting for transfers between devices, along(): return lax.ppermute(x, 'sample', moves)  12.7 us
    ppermute x2, waiting for transfers between devices, over(): return lax.ppermute(x, 'sample', moves)  7.9 us
    ppermute x2, starting transfers between devices, over(): return lax.ppermute(x, 'sample', moves)  4.69 us
    ppermute x3, starting transfers between devices, along(): return lax.ppermute(x, 'sample', moves)  4.21 us
    pallas_call x1, Pallas kernels, run_first(): pl.pallas_call(first_kernel, out_shape=jax.ShapeDtypeStruct((2 * N * N, 1...  2.66 us
    ppermute x5, waiting for transfers between devices, swap(): return lax.ppermute(x, 'sample', [(i, i ^ 1) for i in range(2 * N * N)])  2.09 us
  transfers between devices with their start and end apart: 10, of which 5 were waited for; matrix products, arithmetic and copies ran while one was open for 1% of the time, Pallas kernels for 21%

profile of v5, /device:TPU:0, one launch (start us, length us, event | category | flops | bytes accessed | tf_op | source)
XLA Modules:
  0.0 73.0 jit_solution(9253931700002382167)
XLA Ops:
  1.3 0.0 copy-start
  1.3 1.2 %copy-done = bf16[1,512,1024]{2,1,0:T(8,128)(2,1)S(1)} copy-done((bf16[1,512,1024]{2,1,0:T(8,128)(2,1)S(1)}, bf16[1,512,1024]{2,1,0:T(8,128)(2,1)}, u32[]{:S(2)}) %copy-start) | copy-done | bytes 1048600
  2.5 0.6 unit.1.own_ref.refs_1_.refs_2_.refs_3_
  3.1 4.2 %collective-permute-start.2 = (bf16[528,1024]{1,0:T(8,128)(2,1)S(1)}, bf16[528,1024]{1,0:T(8,128)(2,1)S(1)}, u32[]{:S(2)}, u32[]{:S(2)}) collective-permute-start(bf16[528,1024]{1,0:T(8,128)(2,1)S(1)} %unit.1.own_ref.refs_1_.refs_2_.refs_3_), channel_id=1, source_target_pairs={{0,6},{1,25},{8,14},{3,27},{16,22},{5,29},{24,30},{7,31},{2,4},{9,... | collective-permute-start | bytes 3244040 | tf_op jit(solution)/shard_map/ppermute | solution.py:36
  7.3 0.0 collective-permute-start.1
  7.3 0.7 dynamic-slice_bitcast_fusion.tab_ref
  8.0 0.0 collective-permute-start
  8.0 12.4 %collective-permute-done.2.refs_3_.refs_6_.refs_5_.refs_4_ = bf16[528,1024]{1,0:T(8,128)(2,1)S(1)} collective-permute-done((bf16[528,1024]{1,0:T(8,128)(2,1)S(1)}, bf16[528,1024]{1,0:T(8,128)(2,1)S(1)}, u32[]{:S(2)}, u32[]{:S(2)}) %collective-permute-start.2) | collective-permute-done | bytes 1081376 | tf_op jit(solution)/shard_map/ppermute | solution.py:36
  20.5 3.0 %collective-permute-start.3 = (bf16[528,1024]{1,0:T(8,128)(2,1)S(1)}, bf16[528,1024]{1,0:T(8,128)(2,1)}, u32[]{:S(2)}, u32[]{:S(2)}) collective-permute-start(bf16[528,1024]{1,0:T(8,128)(2,1)S(1)} %unit.1.own_ref.refs_1_.refs_2_.refs_3_), channel_id=1, source_target_pairs={{0,24},{1,7},{8,16},{3,5},{16,8},{5,3},{24,0},{7,1},{2,26},{9,15},... | collective-permute-start | bytes 3244040 | tf_op jit(solution)/shard_map/ppermute | solution.py:41
  23.5 0.0 collective-permute-done.1.refs_0_.refs_1_
  23.5 0.0 collective-permute-start.4
  23.5 0.0 collective-permute-start.5
  23.6 0.4 collective-permute-start.8
  24.0 0.0 collective-permute-done.sib_ref.refs_2_.refs_3_
  24.0 2.7 %pairs_0.1.before_ref = f32[32,128]{1,0:T(8,128)S(1)} custom-call(s32[1]{0:T(128)} %bitcast.1.here_ref, bf16[528,1024]{1,0:T(8,128)(2,1)S(1)} %unit.1.own_ref.refs_1_.refs_2_.refs_3_, bf16[528,1024]{1,0:T(8,128)(2,1)} %collective-permute-done.sib_ref.refs_2_.refs_3_), custom_call_target="tpu_custom_call" | custom-call | flops 1073741824 | bytes 1081344 | tf_op jit(solution)/shard_map/pairs_0/pallas_call | solution.py:188
  26.7 3.9 %pairs_1.1.before_ref = f32[32,128]{1,0:T(8,128)S(1)} custom-call(s32[17]{0:T(128)S(1)} %dynamic-slice_bitcast_fusion.tab_ref, f32[32,128]{1,0:T(8,128)S(1)} %pairs_0.1.before_ref, bf16[528,1024]{1,0:T(8,128)(2,1)} %collective-permute-done.1.refs_0_.refs_1_, bf16[528,1024]{1,0:T(8,128)(2,1)S(1)} %unit.1.own_ref.refs_1_.refs_2_.refs_3_, ...), custom_call_target="tpu_custom_call" | custom-call | flops 2684354560 | bytes 4194304 | tf_op jit(solution)/shard_map/pairs_1/pallas_call | solution.py:250
  30.6 6.4 %collective-permute-done.3.refs_5_ = bf16[528,1024]{1,0:T(8,128)(2,1)} collective-permute-done((bf16[528,1024]{1,0:T(8,128)(2,1)S(1)}, bf16[528,1024]{1,0:T(8,128)(2,1)}, u32[]{:S(2)}, u32[]{:S(2)}) %collective-permute-start.3) | collective-permute-done | bytes 1081376 | tf_op jit(solution)/shard_map/ppermute | solution.py:41
  36.9 0.1 broadcast_select_fusion
  37.1 1.7 %collective-permute-start.9 = (bf16[528,1024]{1,0:T(8,128)(2,1)S(1)}, bf16[528,1024]{1,0:T(8,128)(2,1)S(1)}, u32[]{:S(2)}, u32[]{:S(2)}) collective-permute-start(bf16[528,1024]{1,0:T(8,128)(2,1)S(1)} %broadcast_select_fusion), channel_id=1, source_target_pairs={{0,8},{1,3},{8,0},{3,1},{16,24},{5,7},{24,16},{7,5},{2,10},{9,11},... | collective-permute-start | bytes 3244040 | tf_op jit(solution)/shard_map/ppermute | solution.py:41
  38.7 0.3 collective-permute-done.4.refs_0_
  39.0 0.0 collective-permute-done.5.refs_4_
  39.0 5.6 %pairs_2.1.before_ref = f32[32,128]{1,0:T(8,128)S(1)} custom-call(s32[17]{0:T(128)S(1)} %dynamic-slice_bitcast_fusion.tab_ref, f32[32,128]{1,0:T(8,128)S(1)} %pairs_1.1.before_ref, bf16[528,1024]{1,0:T(8,128)(2,1)S(1)} %collective-permute-done.4.refs_0_, bf16[528,1024]{1,0:T(8,128)(2,1)} %collective-permute-done.1.refs_0_.refs_1_, ...), custom_call_target="tpu_custom_call" | custom-call | flops 4294967296 | bytes 7340032 | tf_op jit(solution)/shard_map/pairs_2/pallas_call | solution.py:250
  44.7 0.3 collective-permute-start.7
  45.0 0.6 collective-permute-start.6
  45.6 0.0 collective-permute-done.8.refs_4_
  45.6 2.1 %collective-permute-done.6.refs_2_ = bf16[256,1024]{1,0:T(8,128)(2,1)S(1)} collective-permute-done((bf16[256,1024]{1,0:T(8,128)(2,1)S(1)}, bf16[256,1024]{1,0:T(8,128)(2,1)S(1)}, u32[]{:S(2)}, u32[]{:S(2)}) %collective-permute-start.6) | collective-permute-done | bytes 524320 | tf_op jit(solution)/shard_map/ppermute | solution.py:45
  47.7 0.0 collective-permute-done.7.refs_3_
  47.7 3.1 %pairs_3.1 = (f32[32,128]{1,0:T(8,128)S(1)}, bf16[528,1024]{1,0:T(8,128)(2,1)S(1)}) custom-call(s32[17]{0:T(128)S(1)} %dynamic-slice_bitcast_fusion.tab_ref, f32[32,128]{1,0:T(8,128)S(1)} %pairs_2.1.before_ref, bf16[528,1024]{1,0:T(8,128)(2,1)S(1)} %collective-permute-done.4.refs_0_, bf16[528,1024]{1,0:T(8,128)(2,1)} %collective-permute-done.1.refs_0_.refs_1_, ...), custom_call_target="tpu_custom_call" | custom-call | tf_op jit(solution)/shard_map/pairs_3/pallas_call | solution.py:250
  50.8 1.5 %collective-permute-done.9.refs_2_ = bf16[528,1024]{1,0:T(8,128)(2,1)S(1)} collective-permute-done((bf16[528,1024]{1,0:T(8,128)(2,1)S(1)}, bf16[528,1024]{1,0:T(8,128)(2,1)S(1)}, u32[]{:S(2)}, u32[]{:S(2)}) %collective-permute-start.9) | collective-permute-done | bytes 1081376 | tf_op jit(solution)/shard_map/ppermute | solution.py:41
  52.3 3.1 %pairs_4.1 = f32[32,128]{1,0:T(8,128)S(1)} custom-call(s32[17]{0:T(128)S(1)} %dynamic-slice_bitcast_fusion.tab_ref, f32[32,128]{1,0:T(8,128)S(1)} %get-tuple-element.16.before_ref, bf16[528,1024]{1,0:T(8,128)(2,1)S(1)} %collective-permute-done.4.refs_0_, bf16[528,1024]{1,0:T(8,128)(2,1)S(1)} %get-tuple-element.17.refs_1_, ...), custom_call_target="tpu_custom_call" | custom-call | tf_op jit(solution)/shard_map/pairs_4/pallas_call | solution.py:250
  55.4 14.7 %all_to_all.9 = f32[32,1,128]{2,1,0:T(1,128)S(1)} all-to-all(f32[32,1,128]{2,1,0:T(1,128)S(1)} %bitcast.9), channel_id=1, replica_groups=mesh['prompt'=4,'sample'=32] {'sample'}, dimensions={0} | all-to-all | bytes 32768 | tf_op jit(solution)/shard_map/all_to_all | solution.py:296
  70.1 0.1 reduce_sum.18
  70.2 1.1 %fusion = (f32[]{:T(128)}, f32[1,32]{1,0:T(1,128)}) fusion(f32[128]{0:T(128)S(1)} %reduce_sum.18, s32[]{:T(128)} %axis_index.12), kind=kLoop, calls=%fused_computation.2 | loop fusion | flops 127 | bytes 392 | tf_op jit(solution)/shard_map/reduce_sum | solution.py:300
  (2 shorter events, 0.1 us)
Async XLA Ops:
  1.3 1.2 %copy-start = (bf16[1,512,1024]{2,1,0:T(8,128)(2,1)S(1)}, bf16[1,512,1024]{2,1,0:T(8,128)(2,1)}, u32[]{:S(2)}) copy-start(bf16[1,512,1024]{2,1,0:T(8,128)(2,1)} %emb_ref.1) | copy-start | bytes 3145732
  3.1 17.3 %collective-permute-start.2 = (bf16[528,1024]{1,0:T(8,128)(2,1)S(1)}, bf16[528,1024]{1,0:T(8,128)(2,1)S(1)}, u32[]{:S(2)}, u32[]{:S(2)}) collective-permute-start(bf16[528,1024]{1,0:T(8,128)(2,1)S(1)} %unit.1.own_ref.refs_1_.refs_2_.refs_3_), channel_id=1, source_target_pairs={{0,6},{1,25},{8,14},{3,27},{16,22},{5,29},{24,30},{7,31},{2,4},{9,... | collective-permute-start | bytes 3244040 | tf_op jit(solution)/shard_map/ppermute | solution.py:36
  7.3 16.1 %collective-permute-start.1 = (bf16[528,1024]{1,0:T(8,128)(2,1)S(1)}, bf16[528,1024]{1,0:T(8,128)(2,1)}, u32[]{:S(2)}, u32[]{:S(2)}) collective-permute-start(bf16[528,1024]{1,0:T(8,128)(2,1)S(1)} %unit.1.own_ref.refs_1_.refs_2_.refs_3_), channel_id=1, source_target_pairs={{0,2},{1,9},{8,10},{3,11},{16,18},{5,13},{24,26},{7,15},{2,0},{9,1... | collective-permute-start | bytes 3244040 | tf_op jit(solution)/shard_map/ppermute | solution.py:36
  8.0 16.0 %collective-permute-start = (bf16[528,1024]{1,0:T(8,128)(2,1)S(1)}, bf16[528,1024]{1,0:T(8,128)(2,1)}, u32[]{:S(2)}, u32[]{:S(2)}) collective-permute-start(bf16[528,1024]{1,0:T(8,128)(2,1)S(1)} %unit.1.own_ref.refs_1_.refs_2_.refs_3_), channel_id=1, source_target_pairs={{0,1},{1,0},{2,3},{3,2},{4,5},{5,4},{6,7},{7,6},{8,9},{9,8},{10,11... | collective-permute-start | bytes 3244040 | tf_op jit(solution)/shard_map/ppermute | solution.py:45
  20.5 16.5 %collective-permute-start.3 = (bf16[528,1024]{1,0:T(8,128)(2,1)S(1)}, bf16[528,1024]{1,0:T(8,128)(2,1)}, u32[]{:S(2)}, u32[]{:S(2)}) collective-permute-start(bf16[528,1024]{1,0:T(8,128)(2,1)S(1)} %unit.1.own_ref.refs_1_.refs_2_.refs_3_), channel_id=1, source_target_pairs={{0,24},{1,7},{8,16},{3,5},{16,8},{5,3},{24,0},{7,1},{2,26},{9,15},... | collective-permute-start | bytes 3244040 | tf_op jit(solution)/shard_map/ppermute | solution.py:41
  23.5 15.5 %collective-permute-start.4 = (bf16[528,1024]{1,0:T(8,128)(2,1)S(1)}, bf16[528,1024]{1,0:T(8,128)(2,1)S(1)}, u32[]{:S(2)}, u32[]{:S(2)}) collective-permute-start(bf16[528,1024]{1,0:T(8,128)(2,1)S(1)} %collective-permute-done.2.refs_3_.refs_6_.refs_5_.refs_4_), channel_id=1, source_target_pairs={{0,2},{1,9},{8,10},{3,11},{16,18},{5,13},{24,26},{7,15},{2,0},{9,1... | collective-permute-start | bytes 3244040 | tf_op jit(solution)/shard_map/ppermute | solution.py:36
  23.5 15.5 %collective-permute-start.5 = (bf16[528,1024]{1,0:T(8,128)(2,1)}, bf16[528,1024]{1,0:T(8,128)(2,1)}, u32[]{:S(2)}, u32[]{:S(2)}) collective-permute-start(bf16[528,1024]{1,0:T(8,128)(2,1)} %collective-permute-done.1.refs_0_.refs_1_), channel_id=1, source_target_pairs={{0,1},{1,0},{2,3},{3,2},{4,5},{5,4},{6,7},{7,6},{8,9},{9,8},{10,11... | collective-permute-start | bytes 3244040 | tf_op jit(solution)/shard_map/ppermute | solution.py:45
  23.6 22.0 %collective-permute-start.8 = (bf16[528,1024]{1,0:T(8,128)(2,1)S(1)}, bf16[528,1024]{1,0:T(8,128)(2,1)S(1)}, u32[]{:S(2)}, u32[]{:S(2)}) collective-permute-start(bf16[528,1024]{1,0:T(8,128)(2,1)S(1)} %collective-permute-done.2.refs_3_.refs_6_.refs_5_.refs_4_), channel_id=1, source_target_pairs={{0,1},{1,0},{2,3},{3,2},{4,5},{5,4},{6,7},{7,6},{8,9},{9,8},{10,11... | collective-permute-start | bytes 3244040 | tf_op jit(solution)/shard_map/ppermute | solution.py:45
  37.1 15.2 %collective-permute-start.9 = (bf16[528,1024]{1,0:T(8,128)(2,1)S(1)}, bf16[528,1024]{1,0:T(8,128)(2,1)S(1)}, u32[]{:S(2)}, u32[]{:S(2)}) collective-permute-start(bf16[528,1024]{1,0:T(8,128)(2,1)S(1)} %broadcast_select_fusion), channel_id=1, source_target_pairs={{0,8},{1,3},{8,0},{3,1},{16,24},{5,7},{24,16},{7,5},{2,10},{9,11},... | collective-permute-start | bytes 3244040 | tf_op jit(solution)/shard_map/ppermute | solution.py:41
  44.7 3.0 %collective-permute-start.7 = (bf16[272,1024]{1,0:T(8,128)(2,1)S(1)}, bf16[272,1024]{1,0:T(8,128)(2,1)S(1)}, u32[]{:S(2)}, u32[]{:S(2)}) collective-permute-start(bf16[272,1024]{1,0:T(8,128)(2,1)S(1)} %slice.13), channel_id=1, source_target_pairs={{0,1},{1,0},{2,3},{3,2},{4,5},{5,4},{6,7},{7,6},{8,9},{9,8},{10,11... | collective-permute-start | bytes 1671176 | tf_op jit(solution)/shard_map/ppermute | solution.py:45
  45.0 2.6 %collective-permute-start.6 = (bf16[256,1024]{1,0:T(8,128)(2,1)S(1)}, bf16[256,1024]{1,0:T(8,128)(2,1)S(1)}, u32[]{:S(2)}, u32[]{:S(2)}) collective-permute-start(bf16[256,1024]{1,0:T(8,128)(2,1)S(1)} %slice.12), channel_id=1, source_target_pairs={{0,1},{1,0},{2,3},{3,2},{4,5},{5,4},{6,7},{7,6},{8,9},{9,8},{10,11... | collective-permute-start | bytes 1572872 | tf_op jit(solution)/shard_map/ppermute | solution.py:45

commit v6 on v5

--- a/solution.py
+++ b/solution.py
@@ -29,6 +29,10 @@
 
 def wide(i):
     return N - 1 - i
+
+
+def ahead_of(i):
+    return (2, 0, 3, 1)[i]
 
 
 def along(x, step):
@@ -99,6 +103,7 @@
     "sib_wide",
     "sib_far",
 )
+SIDE, NEXT, OTHER, ROWS = N, N + 1, 2 * N, 4 * N
 FLAGS = ("even", "odd", "inner", "low", "high", "first", "second")
 STAGES = (
     (
@@ -125,7 +130,6 @@
 def plan(here):
     core = here % 2
     line, across = (here // 2 % N, here // 2 // N) if core == 0 else (here // 2 // N, here // 2 % N)
-    sender = near(across)
     low = across < N // 2
     samples = (
         here,
@@ -133,20 +137,21 @@
         device(wide(line), across, core),
         device((line + 2) % N, across, core),
         device(line, wide(across), core),
-        device(line, sender if sender in (0, N - 1) else wide(sender), core),
+        device(line, ahead_of(across), core),
         device(across, line, 1 - core),
         device(near(across), line, 1 - core),
         device(wide(across), line, 1 - core),
         device((across + 2) % N, line, 1 - core),
     )
     flags = (line % 2 == 0, line % 2 == 1, line in (1, 2), low, not low, core == 0, core == 1)
-    return np.array(samples + flags, np.int32)
-
-
-def make_score(shape):
+    lines = [(i, near(i), wide(i), (i + 2) % N) for i in (line, across)]
+    rows = (*lines[0], SIDE, NEXT, *(OTHER + i for i in lines[1]))
+    return np.array(samples + rows + flags, np.int32)
+
+
+def make_score(shape, total=2 * N * N):
     owners = lax.broadcasted_iota(jnp.int32, shape, 0)
     lanes = lax.broadcasted_iota(jnp.int32, shape, 1)
-    total = shape[0]
     rows = lax.broadcasted_iota(jnp.int32, (LEN, 1), 0).astype(jnp.float32)
     cols = lax.broadcasted_iota(jnp.int32, (1, LEN), 1).astype(jnp.float32)
 
@@ -154,7 +159,7 @@
         value = tag.astype(jnp.float32)
         return value[0:1, 0:1] * 16.0 + value[TAG // 2 : TAG // 2 + 1, 0:1]
 
-    def score(own, other, both, tok_u, tok_v, tag_u, tag_v):
+    def score(row_u, row_v, own, other, both, tok_u, tok_v, tag_u, tag_v):
         len_u, len_v = length(tag_u), length(tag_v)
         similar = lax.dot_general(
             tok_u, tok_v, (((1,), (1,)), ((), ())), preferred_element_type=jnp.float32
@@ -165,8 +170,8 @@
         behind = jnp.sum(jnp.where(cols < len_v, best_col, 0.0), axis=1, keepdims=True)
         ahead = ahead / len_u
         behind = behind / len_v
-        at_u = owners == own
-        at_v = (owners == other) & (both == 1)
+        at_u = owners == row_u
+        at_v = (owners == row_v) & (both == 1)
         fore = (at_u & (lanes == other)) | (at_v & (lanes == total + own))
         back = (at_u & (lanes == total + other)) | (at_v & (lanes == own))
         return jnp.where(fore, ahead, 0.0) + jnp.where(back, behind, 0.0)
@@ -177,17 +182,20 @@
 def first_kernel(here_ref, own_ref, sib_ref, out_ref):
     score = make_score(out_ref.shape)
     here = here_ref[0]
-    owner = jnp.where(here % 2 == 0, here, -1)
+    first, y, z = 1 - here % 2, here // 2 // N, here // 2 % N
+    line = jnp.where(first == 1, z, y)
     own, own_tag = own_ref[0:LEN, :], own_ref[LEN : LEN + TAG, 0:128]
-    out_ref[...] = score(here, here, 0, own, own, own_tag, own_tag) + score(
-        owner, here + 1, 1 - here % 2, own, sib_ref[0:LEN, :], own_tag, sib_ref[LEN : LEN + TAG, 0:128]
+    sib, sib_tag = sib_ref[0:LEN, :], sib_ref[LEN : LEN + TAG, 0:128]
+    row = jnp.where(first == 1, line, -1)
+    out_ref[...] = score(line, line, here, here, 0, own, own, own_tag, own_tag) + score(
+        row, OTHER + y, here, here + 1, first, own, sib, own_tag, sib_tag
     )
 
 
 def run_first(here, own, sib):
     return pl.pallas_call(
         first_kernel,
-        out_shape=jax.ShapeDtypeStruct((2 * N * N, 128), jnp.float32),
+        out_shape=jax.ShapeDtypeStruct((ROWS, 128), jnp.float32),
         in_specs=[pl.BlockSpec(memory_space=pltpu.SMEM)]
         + [pl.BlockSpec(memory_space=pltpu.VMEM)] * 2,
         out_specs=pl.BlockSpec(memory_space=pltpu.VMEM),
@@ -200,8 +208,10 @@
 
 
 def pairs_kernel(stage, names, parts, keep, tab_ref, before_ref, *refs):
+    last = stage == len(STAGES) - 1
+    given_ref, refs = (refs[0], refs[1:]) if last else (None, refs)
     ins, out_ref = refs[: sum(parts)], refs[sum(parts)]
-    score_of = make_score(out_ref.shape)
+    score_of = make_score(before_ref.shape)
     blocks, place = {}, 0
     for name, count in zip(names, parts):
         blocks[name] = ins[place : place + count]
@@ -221,23 +231,28 @@
         result = None
         for u, v in pairs:
             (tok_u, tag_u), (tok_v, tag_v) = tokens(u), tokens(v)
-            own, other = tab_ref[NAMES.index(u)], tab_ref[NAMES.index(v)]
-            part = score_of(own, other, 1, tok_u, tok_v, tag_u, tag_v)
+            at, to = NAMES.index(u), NAMES.index(v)
+            row_u, row_v = tab_ref[len(NAMES) + at], tab_ref[len(NAMES) + to]
+            part = score_of(row_u, row_v, tab_ref[at], tab_ref[to], 1, tok_u, tok_v, tag_u, tag_v)
             result = part if result is None else result + part
         return result
 
     result = before_ref[...]
     for flag, pairs in STAGES[stage]:
-        if flag is None:
+        if last:
+            result += score(pairs)
+            out_ref[...] = result[0:N] + given_ref[OTHER : OTHER + N, :]
+            refs[-1][...] = jnp.broadcast_to(result[NEXT : NEXT + 1], refs[-1].shape)
+        elif flag is None:
             out_ref[...] = result + score(pairs)
         else:
 
-            @pl.when(tab_ref[len(NAMES) + FLAGS.index(flag)] == 1)
+            @pl.when(tab_ref[2 * len(NAMES) + FLAGS.index(flag)] == 1)
             def _():
                 out_ref[...] += score(pairs)
 
 
-def run_pairs(stage, table, before, blocks, keep=None):
+def run_pairs(stage, table, before, blocks, keep=None, given=()):
     groups = [pair for _, pairs in STAGES[stage] for pair in pairs]
     names = sorted({name for pair in groups for name in pair} | ({keep} if keep else set()))
     chosen = [blocks[name] for name in names]
@@ -245,13 +260,14 @@
     arrays = [part for block in chosen for part in block]
     width = arrays[0].shape[1]
     hide = stage < 2
-    outs = [jax.ShapeDtypeStruct(before.shape, jnp.float32)]
+    shapes = [(N, 128), (2 * N, 128)] if given else [before.shape]
+    outs = [jax.ShapeDtypeStruct(shape, jnp.float32) for shape in shapes]
     outs += [jax.ShapeDtypeStruct(blocks[keep].shape, jnp.bfloat16)] if keep else []
     return pl.pallas_call(
         functools.partial(pairs_kernel, stage, names, [len(b) for b in chosen], keep),
         out_shape=outs,
         in_specs=[pl.BlockSpec(memory_space=pltpu.SMEM)]
-        + [pl.BlockSpec(memory_space=pltpu.VMEM)] * (1 + len(arrays)),
+        + [pl.BlockSpec(memory_space=pltpu.VMEM)] * (1 + len(given) + len(arrays)),
         out_specs=[pl.BlockSpec(memory_space=pltpu.VMEM)] * len(outs),
         compiler_params=pltpu.CompilerParams(vmem_limit_bytes=VMEM),
         cost_estimate=pl.CostEstimate(
@@ -260,7 +276,7 @@
             transcendentals=0,
         ),
         name=f"pairs_{stage + 1}",
-    )(table, before, *arrays)
+    )(table, before, *given, *arrays)
 
 
 def after(x, *others):
@@ -288,13 +304,16 @@
     pick = jnp.where(edge, blocks["own"], after(blocks["side"], scores))
     blocks["next"] = over(pick, near)
     (scores,) = run_pairs(1, table, after(scores, pick), blocks)
+    from_side = over(scores, wide)
     far = after(blocks["far"], scores)
     blocks["sib_far"] = (swap(far[:HALF]), swap(far[HALF:]))
     scores, blocks["near"] = run_pairs(2, table, scores, blocks, keep="near")
-    (scores,) = run_pairs(3, table, scores, blocks)
-
-    parts = lax.all_to_all(scores, "sample", 0, 0, tiled=True)
-    result = jnp.sum(parts, axis=0)
+    line, last = run_pairs(3, table, scores, blocks, given=(swap(scores),))
+
+    from_next = over(last, ahead_of)
+    groups = [[device(i, j, c) for i in range(N)] for j in range(N) for c in range(2)]
+    parts = lax.all_to_all(line, "sample", 0, 0, tiled=True, axis_index_groups=groups)
+    result = jnp.sum(parts, axis=0) + from_side[SIDE] + from_next[0]
     ahead, behind = result[:total], result[total : 2 * total]
     offdiag = jnp.arange(total, dtype=jnp.int32) != here
     utility = jnp.sum(jnp.where(offdiag, ahead + behind, 0.0)) / jnp.float32(2 * (total - 1))

time: 74.1 us -> 71.6 us (0.966)
  blocking collectives: 14.7 us -> 9.56 us
  starting transfers between devices: 10.2 us -> 15.2 us
  waiting for transfers between devices: 22.7 us -> 21 us
    all_to_all x1, blocking collectives: 14.7 us -> 9.56 us  [body(): lax.all_to_all(line, 'sample', 0, 0, tiled=True, axis_index_groups=groups)]
    ppermute x2 -> x4, starting transfers between devices: 4.69 us -> 9.45 us  [over(): return lax.ppermute(x, 'sample', moves)]
    ppermute x2 -> x4, waiting for transfers between devices: 7.9 us -> 6.39 us  [over(): return lax.ppermute(x, 'sample', moves)]
    ppermute x5 -> x6, starting transfers between devices: 1.29 us -> 1.53 us  [swap(): return lax.ppermute(x, 'sample', [(i, i ^ 1) for i in range(2 * N * N)])]
    ppermute x5 -> x6, waiting for transfers between devices: 2.09 us -> 1.91 us  [swap(): return lax.ppermute(x, 'sample', [(i, i ^ 1) for i in range(2 * N * N)])]
  transfers between devices with their start and end apart: 10 -> 13, of which waited for: 5 -> 4; matrix products, arithmetic and copies ran while one was open for 1% -> 1% of each run, Pallas kernels for 21% -> 26%
where the time goes in v6:
time: 71.6 us; the launch traced here: 71.2 us
  waiting for transfers between devices  21 us (29%)
  Pallas kernels  18.9 us (26%)
  starting transfers between devices  15.2 us (21%)
  blocking collectives  9.56 us (13%)
  between operations  3.2 us (4%)
  local copies, waits for them, and re-layouts  1.98 us (3%)
  other arithmetic  1.32 us (2%)
    pallas_call x4, Pallas kernels, run_pairs(): pl.pallas_call(functools.partial(pairs_kernel, stage, names, [len(b) for...  15.7 us
    ppermute x3, waiting for transfers between devices, along(): return lax.ppermute(x, 'sample', moves)  12.7 us
    all_to_all x1, blocking collectives, body(): lax.all_to_all(line, 'sample', 0, 0, tiled=True, axis_index_groups=groups)  9.56 us
    ppermute x4, starting transfers between devices, over(): return lax.ppermute(x, 'sample', moves)  9.45 us
    ppermute x4, waiting for transfers between devices, over(): return lax.ppermute(x, 'sample', moves)  6.39 us
    ppermute x3, starting transfers between devices, along(): return lax.ppermute(x, 'sample', moves)  4.21 us
    pallas_call x1, Pallas kernels, run_first(): pl.pallas_call(first_kernel, out_shape=jax.ShapeDtypeStruct((ROWS, 128),...  2.66 us
    ppermute x6, waiting for transfers between devices, swap(): return lax.ppermute(x, 'sample', [(i, i ^ 1) for i in range(2 * N * N)])  1.91 us
  transfers between devices with their start and end apart: 13, of which 4 were waited for; matrix products, arithmetic and copies ran while one was open for 1% of the time, Pallas kernels for 26%

profile of v6, /device:TPU:0, one launch (start us, length us, event | category | flops | bytes accessed | tf_op | source)
XLA Modules:
  0.0 71.2 jit_solution(7783160422339657860)
XLA Ops:
  1.3 0.0 copy-start
  1.3 1.2 %copy-done = bf16[1,512,1024]{2,1,0:T(8,128)(2,1)S(1)} copy-done((bf16[1,512,1024]{2,1,0:T(8,128)(2,1)S(1)}, bf16[1,512,1024]{2,1,0:T(8,128)(2,1)}, u32[]{:S(2)}) %copy-start) | copy-done | bytes 1048600
  2.5 0.6 unit.1.own_ref.refs_1_.refs_2_.refs_4_
  3.1 4.2 %collective-permute-start.2 = (bf16[528,1024]{1,0:T(8,128)(2,1)S(1)}, bf16[528,1024]{1,0:T(8,128)(2,1)S(1)}, u32[]{:S(2)}, u32[]{:S(2)}) collective-permute-start(bf16[528,1024]{1,0:T(8,128)(2,1)S(1)} %unit.1.own_ref.refs_1_.refs_2_.refs_4_), channel_id=1, source_target_pairs={{0,6},{1,25},{8,14},{3,27},{16,22},{5,29},{24,30},{7,31},{2,4},{9,... | collective-permute-start | bytes 3244040 | tf_op jit(solution)/shard_map/ppermute | solution.py:40
  7.3 0.0 collective-permute-start.1
  7.3 0.7 dynamic-slice_bitcast_fusion.tab_ref
  8.0 0.0 collective-permute-start
  8.0 12.4 %collective-permute-done.2.refs_3_.refs_6_.refs_5_ = bf16[528,1024]{1,0:T(8,128)(2,1)S(1)} collective-permute-done((bf16[528,1024]{1,0:T(8,128)(2,1)S(1)}, bf16[528,1024]{1,0:T(8,128)(2,1)S(1)}, u32[]{:S(2)}, u32[]{:S(2)}) %collective-permute-start.2) | collective-permute-done | bytes 1081376 | tf_op jit(solution)/shard_map/ppermute | solution.py:40
  20.5 3.0 %collective-permute-start.3 = (bf16[528,1024]{1,0:T(8,128)(2,1)S(1)}, bf16[528,1024]{1,0:T(8,128)(2,1)}, u32[]{:S(2)}, u32[]{:S(2)}) collective-permute-start(bf16[528,1024]{1,0:T(8,128)(2,1)S(1)} %unit.1.own_ref.refs_1_.refs_2_.refs_4_), channel_id=1, source_target_pairs={{0,24},{1,7},{8,16},{3,5},{16,8},{5,3},{24,0},{7,1},{2,26},{9,15},... | collective-permute-start | bytes 3244040 | tf_op jit(solution)/shard_map/ppermute | solution.py:45
  23.5 0.0 collective-permute-done.1.refs_0_.refs_1_
  23.5 0.0 collective-permute-start.4
  23.5 0.0 collective-permute-start.5
  23.6 0.4 collective-permute-start.8
  24.0 0.0 collective-permute-done.sib_ref.refs_2_.refs_3_
  24.0 2.7 %pairs_0.1.before_ref = f32[16,128]{1,0:T(8,128)S(1)} custom-call(s32[1]{0:T(128)} %bitcast.1.here_ref, bf16[528,1024]{1,0:T(8,128)(2,1)S(1)} %unit.1.own_ref.refs_1_.refs_2_.refs_4_, bf16[528,1024]{1,0:T(8,128)(2,1)} %collective-permute-done.sib_ref.refs_2_.refs_3_), custom_call_target="tpu_custom_call" | custom-call | flops 1073741824 | bytes 1081344 | tf_op jit(solution)/shard_map/pairs_0/pallas_call | solution.py:196
  26.7 3.9 %pairs_1.1.before_ref = f32[16,128]{1,0:T(8,128)S(1)} custom-call(s32[27]{0:T(128)S(1)} %dynamic-slice_bitcast_fusion.tab_ref, f32[16,128]{1,0:T(8,128)S(1)} %pairs_0.1.before_ref, bf16[528,1024]{1,0:T(8,128)(2,1)} %collective-permute-done.1.refs_0_.refs_1_, bf16[528,1024]{1,0:T(8,128)(2,1)S(1)} %unit.1.own_ref.refs_1_.refs_2_.refs_4_, ...), custom_call_target="tpu_custom_call" | custom-call | flops 2684354560 | bytes 4194304 | tf_op jit(solution)/shard_map/pairs_1/pallas_call | solution.py:266
  30.6 6.4 %collective-permute-done.3.refs_5_ = bf16[528,1024]{1,0:T(8,128)(2,1)} collective-permute-done((bf16[528,1024]{1,0:T(8,128)(2,1)S(1)}, bf16[528,1024]{1,0:T(8,128)(2,1)}, u32[]{:S(2)}, u32[]{:S(2)}) %collective-permute-start.3) | collective-permute-done | bytes 1081376 | tf_op jit(solution)/shard_map/ppermute | solution.py:45
  36.9 0.1 broadcast_select_fusion
  37.1 1.7 %collective-permute-start.10 = (bf16[528,1024]{1,0:T(8,128)(2,1)S(1)}, bf16[528,1024]{1,0:T(8,128)(2,1)S(1)}, u32[]{:S(2)}, u32[]{:S(2)}) collective-permute-start(bf16[528,1024]{1,0:T(8,128)(2,1)S(1)} %broadcast_select_fusion), channel_id=1, source_target_pairs={{0,8},{1,3},{8,0},{3,1},{16,24},{5,7},{24,16},{7,5},{2,10},{9,11},... | collective-permute-start | bytes 3244040 | tf_op jit(solution)/shard_map/ppermute | solution.py:45
  38.7 0.3 collective-permute-done.4.refs_0_.refs_1_
  39.0 0.0 collective-permute-done.5.refs_4_
  39.0 5.6 %pairs_2.1.before_ref = f32[16,128]{1,0:T(8,128)S(1)} custom-call(s32[27]{0:T(128)S(1)} %dynamic-slice_bitcast_fusion.tab_ref, f32[16,128]{1,0:T(8,128)S(1)} %pairs_1.1.before_ref, bf16[528,1024]{1,0:T(8,128)(2,1)S(1)} %collective-permute-done.4.refs_0_.refs_1_, bf16[528,1024]{1,0:T(8,128)(2,1)} %collective-permute-done.1.refs_0_.refs_1_, ...), custom_call_target="tpu_custom_call" | custom-call | flops 4294967296 | bytes 7340032 | tf_op jit(solution)/shard_map/pairs_2/pallas_call | solution.py:266
  44.7 0.1 collective-permute-start.7
  44.8 0.8 %collective-permute-start.6 = (bf16[256,1024]{1,0:T(8,128)(2,1)S(1)}, bf16[256,1024]{1,0:T(8,128)(2,1)S(1)}, u32[]{:S(2)}, u32[]{:S(2)}) collective-permute-start(bf16[256,1024]{1,0:T(8,128)(2,1)S(1)} %slice.18), channel_id=1, source_target_pairs={{0,1},{1,0},{2,3},{3,2},{4,5},{5,4},{6,7},{7,6},{8,9},{9,8},{10,11... | collective-permute-start | bytes 1572872 | tf_op jit(solution)/shard_map/ppermute | solution.py:49
  45.6 0.0 collective-permute-done.8.refs_4_
  45.6 1.9 %collective-permute-done.6.refs_2_ = bf16[256,1024]{1,0:T(8,128)(2,1)S(1)} collective-permute-done((bf16[256,1024]{1,0:T(8,128)(2,1)S(1)}, bf16[256,1024]{1,0:T(8,128)(2,1)S(1)}, u32[]{:S(2)}, u32[]{:S(2)}) %collective-permute-start.6) | collective-permute-done | bytes 524320 | tf_op jit(solution)/shard_map/ppermute | solution.py:49
  47.5 0.0 collective-permute-done.7.refs_3_
  47.5 3.1 %pairs_3.1 = (f32[16,128]{1,0:T(8,128)S(1)}, bf16[528,1024]{1,0:T(8,128)(2,1)S(1)}) custom-call(s32[27]{0:T(128)S(1)} %dynamic-slice_bitcast_fusion.tab_ref, f32[16,128]{1,0:T(8,128)S(1)} %pairs_2.1.before_ref, bf16[528,1024]{1,0:T(8,128)(2,1)S(1)} %collective-permute-done.4.refs_0_.refs_1_, bf16[528,1024]{1,0:T(8,128)(2,1)} %collective-permute-done.1.refs_0_.refs_1_, ...), custom_call_target="tpu_custom_call" | custom-call | tf_op jit(solution)/shard_map/pairs_3/pallas_call | solution.py:266
  50.6 0.2 collective-permute-start.9
  50.8 1.9 %collective-permute-start.11 = (f32[16,128]{1,0:T(8,128)S(1)}, f32[16,128]{1,0:T(8,128)S(1)}, u32[]{:S(2)}, u32[]{:S(2)}) collective-permute-start(f32[16,128]{1,0:T(8,128)S(1)} %pairs_2.1.before_ref), channel_id=1, source_target_pairs={{0,24},{1,7},{8,16},{3,5},{16,8},{5,3},{24,0},{7,1},{2,26},{9,15},... | collective-permute-start | bytes 24584 | tf_op jit(solution)/shard_map/ppermute | solution.py:45
  52.7 0.0 collective-permute-done.9.refs_0_
  52.7 0.0 collective-permute-done.10.refs_3_
  52.7 3.1 %pairs_4.1 = (f32[4,128]{1,0:T(4,128)S(1)}, f32[8,128]{1,0:T(8,128)S(1)}) custom-call(s32[27]{0:T(128)S(1)} %dynamic-slice_bitcast_fusion.tab_ref, f32[16,128]{1,0:T(8,128)S(1)} %get-tuple-element.18.before_ref, f32[16,128]{1,0:T(8,128)S(1)} %collective-permute-done.9.refs_0_, bf16[528,1024]{1,0:T(8,128)(2,1)S(1)} %collective-permute-done.4.refs_0_.refs_1_, ...), custom_call_target="tpu_custom_call" | custom-call | tf_op jit(solution)/shard_map/pairs_4/pallas_call | solution.py:266
  55.8 2.8 %collective-permute-start.12 = (f32[8,128]{1,0:T(8,128)S(1)}, f32[8,128]{1,0:T(8,128)S(1)}, u32[]{:S(2)}, u32[]{:S(2)}) collective-permute-start(f32[8,128]{1,0:T(8,128)S(1)} %get-tuple-element.21), channel_id=1, source_target_pairs={{0,16},{1,5},{8,0},{3,1},{16,24},{5,7},{24,8},{7,3},{2,18},{9,13},... | collective-permute-start | bytes 12296 | tf_op jit(solution)/shard_map/ppermute | solution.py:45
  58.7 9.6 %all_to_all.9 = f32[4,1,128]{2,1,0:T(1,128)S(1)} all-to-all(f32[4,1,128]{2,1,0:T(1,128)S(1)} %bitcast.17), channel_id=1, replica_groups={{0,2,4,6},{1,9,17,25},{8,10,12,14},{3,11,19,27},{16,18,20,22},{5,13,21,..., dimensions={0} | all-to-all | bytes 4096 | tf_op jit(solution)/shard_map/all_to_all | solution.py:315
  68.2 0.0 collective-permute-done.11
  68.2 0.0 collective-permute-done.12
  68.3 1.2 %fusion = (f32[]{:T(128)}, f32[1,32]{1,0:T(1,128)}) fusion(f32[128]{0:T(128)S(1)} %fusion.2, s32[]{:T(128)} %axis_index.12), kind=kLoop, calls=%fused_computation.2 | loop fusion | flops 127 | bytes 392 | tf_op jit(solution)/shard_map/reduce_sum | solution.py:319
  (4 shorter events, 0.1 us)
Async XLA Ops:
  1.3 1.2 %copy-start = (bf16[1,512,1024]{2,1,0:T(8,128)(2,1)S(1)}, bf16[1,512,1024]{2,1,0:T(8,128)(2,1)}, u32[]{:S(2)}) copy-start(bf16[1,512,1024]{2,1,0:T(8,128)(2,1)} %emb_ref.1) | copy-start | bytes 3145732
  3.1 17.3 %collective-permute-start.2 = (bf16[528,1024]{1,0:T(8,128)(2,1)S(1)}, bf16[528,1024]{1,0:T(8,128)(2,1)S(1)}, u32[]{:S(2)}, u32[]{:S(2)}) collective-permute-start(bf16[528,1024]{1,0:T(8,128)(2,1)S(1)} %unit.1.own_ref.refs_1_.refs_2_.refs_4_), channel_id=1, source_target_pairs={{0,6},{1,25},{8,14},{3,27},{16,22},{5,29},{24,30},{7,31},{2,4},{9,... | collective-permute-start | bytes 3244040 | tf_op jit(solution)/shard_map/ppermute | solution.py:40
  7.3 16.1 %collective-permute-start.1 = (bf16[528,1024]{1,0:T(8,128)(2,1)S(1)}, bf16[528,1024]{1,0:T(8,128)(2,1)}, u32[]{:S(2)}, u32[]{:S(2)}) collective-permute-start(bf16[528,1024]{1,0:T(8,128)(2,1)S(1)} %unit.1.own_ref.refs_1_.refs_2_.refs_4_), channel_id=1, source_target_pairs={{0,2},{1,9},{8,10},{3,11},{16,18},{5,13},{24,26},{7,15},{2,0},{9,1... | collective-permute-start | bytes 3244040 | tf_op jit(solution)/shard_map/ppermute | solution.py:40
  8.0 16.0 %collective-permute-start = (bf16[528,1024]{1,0:T(8,128)(2,1)S(1)}, bf16[528,1024]{1,0:T(8,128)(2,1)}, u32[]{:S(2)}, u32[]{:S(2)}) collective-permute-start(bf16[528,1024]{1,0:T(8,128)(2,1)S(1)} %unit.1.own_ref.refs_1_.refs_2_.refs_4_), channel_id=1, source_target_pairs={{0,1},{1,0},{2,3},{3,2},{4,5},{5,4},{6,7},{7,6},{8,9},{9,8},{10,11... | collective-permute-start | bytes 3244040 | tf_op jit(solution)/shard_map/ppermute | solution.py:49
  20.5 16.5 %collective-permute-start.3 = (bf16[528,1024]{1,0:T(8,128)(2,1)S(1)}, bf16[528,1024]{1,0:T(8,128)(2,1)}, u32[]{:S(2)}, u32[]{:S(2)}) collective-permute-start(bf16[528,1024]{1,0:T(8,128)(2,1)S(1)} %unit.1.own_ref.refs_1_.refs_2_.refs_4_), channel_id=1, source_target_pairs={{0,24},{1,7},{8,16},{3,5},{16,8},{5,3},{24,0},{7,1},{2,26},{9,15},... | collective-permute-start | bytes 3244040 | tf_op jit(solution)/shard_map/ppermute | solution.py:45
  23.5 15.5 %collective-permute-start.4 = (bf16[528,1024]{1,0:T(8,128)(2,1)S(1)}, bf16[528,1024]{1,0:T(8,128)(2,1)S(1)}, u32[]{:S(2)}, u32[]{:S(2)}) collective-permute-start(bf16[528,1024]{1,0:T(8,128)(2,1)S(1)} %collective-permute-done.2.refs_3_.refs_6_.refs_5_), channel_id=1, source_target_pairs={{0,2},{1,9},{8,10},{3,11},{16,18},{5,13},{24,26},{7,15},{2,0},{9,1... | collective-permute-start | bytes 3244040 | tf_op jit(solution)/shard_map/ppermute | solution.py:40
  23.5 15.5 %collective-permute-start.5 = (bf16[528,1024]{1,0:T(8,128)(2,1)}, bf16[528,1024]{1,0:T(8,128)(2,1)}, u32[]{:S(2)}, u32[]{:S(2)}) collective-permute-start(bf16[528,1024]{1,0:T(8,128)(2,1)} %collective-permute-done.1.refs_0_.refs_1_), channel_id=1, source_target_pairs={{0,1},{1,0},{2,3},{3,2},{4,5},{5,4},{6,7},{7,6},{8,9},{9,8},{10,11... | collective-permute-start | bytes 3244040 | tf_op jit(solution)/shard_map/ppermute | solution.py:49
  23.6 22.0 %collective-permute-start.8 = (bf16[528,1024]{1,0:T(8,128)(2,1)S(1)}, bf16[528,1024]{1,0:T(8,128)(2,1)S(1)}, u32[]{:S(2)}, u32[]{:S(2)}) collective-permute-start(bf16[528,1024]{1,0:T(8,128)(2,1)S(1)} %collective-permute-done.2.refs_3_.refs_6_.refs_5_), channel_id=1, source_target_pairs={{0,1},{1,0},{2,3},{3,2},{4,5},{5,4},{6,7},{7,6},{8,9},{9,8},{10,11... | collective-permute-start | bytes 3244040 | tf_op jit(solution)/shard_map/ppermute | solution.py:49
  37.1 15.7 %collective-permute-start.10 = (bf16[528,1024]{1,0:T(8,128)(2,1)S(1)}, bf16[528,1024]{1,0:T(8,128)(2,1)S(1)}, u32[]{:S(2)}, u32[]{:S(2)}) collective-permute-start(bf16[528,1024]{1,0:T(8,128)(2,1)S(1)} %broadcast_select_fusion), channel_id=1, source_target_pairs={{0,8},{1,3},{8,0},{3,1},{16,24},{5,7},{24,16},{7,5},{2,10},{9,11},... | collective-permute-start | bytes 3244040 | tf_op jit(solution)/shard_map/ppermute | solution.py:45
  44.7 2.8 %collective-permute-start.7 = (bf16[272,1024]{1,0:T(8,128)(2,1)S(1)}, bf16[272,1024]{1,0:T(8,128)(2,1)S(1)}, u32[]{:S(2)}, u32[]{:S(2)}) collective-permute-start(bf16[272,1024]{1,0:T(8,128)(2,1)S(1)} %slice.19), channel_id=1, source_target_pairs={{0,1},{1,0},{2,3},{3,2},{4,5},{5,4},{6,7},{7,6},{8,9},{9,8},{10,11... | collective-permute-start | bytes 1671176 | tf_op jit(solution)/shard_map/ppermute | solution.py:49
  44.8 2.6 %collective-permute-start.6 = (bf16[256,1024]{1,0:T(8,128)(2,1)S(1)}, bf16[256,1024]{1,0:T(8,128)(2,1)S(1)}, u32[]{:S(2)}, u32[]{:S(2)}) collective-permute-start(bf16[256,1024]{1,0:T(8,128)(2,1)S(1)} %slice.18), channel_id=1, source_target_pairs={{0,1},{1,0},{2,3},{3,2},{4,5},{5,4},{6,7},{7,6},{8,9},{9,8},{10,11... | collective-permute-start | bytes 1572872 | tf_op jit(solution)/shard_map/ppermute | solution.py:49
  50.6 2.2 %collective-permute-start.9 = (f32[16,128]{1,0:T(8,128)S(1)}, f32[16,128]{1,0:T(8,128)S(1)}, u32[]{:S(2)}, u32[]{:S(2)}) collective-permute-start(f32[16,128]{1,0:T(8,128)S(1)} %get-tuple-element.18.before_ref), channel_id=1, source_target_pairs={{0,1},{1,0},{2,3},{3,2},{4,5},{5,4},{6,7},{7,6},{8,9},{9,8},{10,11... | collective-permute-start | bytes 24584 | tf_op jit(solution)/shard_map/ppermute | solution.py:49
  50.8 17.4 %collective-permute-start.11 = (f32[16,128]{1,0:T(8,128)S(1)}, f32[16,128]{1,0:T(8,128)S(1)}, u32[]{:S(2)}, u32[]{:S(2)}) collective-permute-start(f32[16,128]{1,0:T(8,128)S(1)} %pairs_2.1.before_ref), channel_id=1, source_target_pairs={{0,24},{1,7},{8,16},{3,5},{16,8},{5,3},{24,0},{7,1},{2,26},{9,15},... | collective-permute-start | bytes 24584 | tf_op jit(solution)/shard_map/ppermute | solution.py:45
  55.8 12.4 %collective-permute-start.12 = (f32[8,128]{1,0:T(8,128)S(1)}, f32[8,128]{1,0:T(8,128)S(1)}, u32[]{:S(2)}, u32[]{:S(2)}) collective-permute-start(f32[8,128]{1,0:T(8,128)S(1)} %get-tuple-element.21), channel_id=1, source_target_pairs={{0,16},{1,5},{8,0},{3,1},{16,24},{5,7},{24,8},{7,3},{2,18},{9,13},... | collective-permute-start | bytes 12296 | tf_op jit(solution)/shard_map/ppermute | solution.py:45

commit v7 on v6

--- a/solution.py
+++ b/solution.py
@@ -29,6 +29,10 @@
 
 def wide(i):
     return N - 1 - i
+
+
+def across_from(i):
+    return (i + 2) % N
 
 
 def ahead_of(i):
@@ -104,7 +108,7 @@
     "sib_far",
 )
 SIDE, NEXT, OTHER, ROWS = N, N + 1, 2 * N, 4 * N
-FLAGS = ("even", "odd", "inner", "low", "high", "first", "second")
+FLAGS = ("even", "odd", "inner", "low", "high", "first", "second", "edge")
 STAGES = (
     (
         (None, (("near", "sib"), ("wide", "sib"))),
@@ -144,8 +148,8 @@
         device((across + 2) % N, line, 1 - core),
     )
     flags = (line % 2 == 0, line % 2 == 1, line in (1, 2), low, not low, core == 0, core == 1)
-    lines = [(i, near(i), wide(i), (i + 2) % N) for i in (line, across)]
-    rows = (*lines[0], SIDE, NEXT, *(OTHER + i for i in lines[1]))
+    flags += (across in (0, N - 1),)
+    rows = (*range(N), SIDE, NEXT, *range(OTHER, OTHER + N))
     return np.array(samples + rows + flags, np.int32)
 
 
@@ -182,13 +186,12 @@
 def first_kernel(here_ref, own_ref, sib_ref, out_ref):
     score = make_score(out_ref.shape)
     here = here_ref[0]
-    first, y, z = 1 - here % 2, here // 2 // N, here // 2 % N
-    line = jnp.where(first == 1, z, y)
+    first = 1 - here % 2
     own, own_tag = own_ref[0:LEN, :], own_ref[LEN : LEN + TAG, 0:128]
     sib, sib_tag = sib_ref[0:LEN, :], sib_ref[LEN : LEN + TAG, 0:128]
-    row = jnp.where(first == 1, line, -1)
-    out_ref[...] = score(line, line, here, here, 0, own, own, own_tag, own_tag) + score(
-        row, OTHER + y, here, here + 1, first, own, sib, own_tag, sib_tag
+    row = jnp.where(first == 1, 0, -1)
+    out_ref[...] = score(0, 0, here, here, 0, own, own, own_tag, own_tag) + score(
+        row, OTHER, here, here + 1, first, own, sib, own_tag, sib_tag
     )
 
 
@@ -241,8 +244,10 @@
     for flag, pairs in STAGES[stage]:
         if last:
             result += score(pairs)
-            out_ref[...] = result[0:N] + given_ref[OTHER : OTHER + N, :]
-            refs[-1][...] = jnp.broadcast_to(result[NEXT : NEXT + 1], refs[-1].shape)
+            line = result[0:N] + given_ref[OTHER : OTHER + N, :]
+            for k, ref in enumerate(refs[sum(parts) :]):
+                row = line[k : k + 1] if k < N else result[NEXT : NEXT + 1]
+                ref[...] = jnp.broadcast_to(row, ref.shape)
         elif flag is None:
             out_ref[...] = result + score(pairs)
         else:
@@ -260,7 +265,7 @@
     arrays = [part for block in chosen for part in block]
     width = arrays[0].shape[1]
     hide = stage < 2
-    shapes = [(N, 128), (2 * N, 128)] if given else [before.shape]
+    shapes = [(2 * N, 128)] * (N + 1) if given else [before.shape]
     outs = [jax.ShapeDtypeStruct(shape, jnp.float32) for shape in shapes]
     outs += [jax.ShapeDtypeStruct(blocks[keep].shape, jnp.bfloat16)] if keep else []
     return pl.pallas_call(
@@ -279,6 +284,39 @@
     )(table, before, *given, *arrays)
 
 
+def pick_kernel(tab_ref, own_ref, side_ref, out_ref, sem):
+    edge = tab_ref[2 * len(NAMES) + FLAGS.index("edge")]
+    step = (LEN + TAG) // 3
+    for flag, block in ((1, own_ref), (0, side_ref)):
+
+        @pl.when(edge == flag)
+        def _():
+            copies = []
+            for k in range(3):
+                rows = pl.ds(k * step, step)
+                copies.append(
+                    pltpu.make_async_copy(block.at[rows, :], out_ref.at[rows, :], sem.at[k])
+                )
+            for copy in copies:
+                copy.start()
+            for copy in copies:
+                copy.wait()
+
+
+def run_pick(table, own, side):
+    return pl.pallas_call(
+        pick_kernel,
+        out_shape=jax.ShapeDtypeStruct(own.shape, own.dtype),
+        in_specs=[pl.BlockSpec(memory_space=pltpu.SMEM)]
+        + [pl.BlockSpec(memory_space=pl.ANY)] * 2,
+        out_specs=pl.BlockSpec(memory_space=pl.ANY),
+        scratch_shapes=[pltpu.SemaphoreType.DMA((3,))],
+        compiler_params=pltpu.CompilerParams(vmem_limit_bytes=VMEM),
+        cost_estimate=pl.CostEstimate(flops=0, bytes_accessed=0, transcendentals=0),
+        name="pick",
+    )(table, own, side)
+
+
 def after(x, *others):
     return lax.optimization_barrier((x, *others))[0]
 
@@ -286,10 +324,6 @@
 def body(embeddings, lengths):
     total = lax.axis_size("sample")
     here = lax.axis_index("sample")
-    core, chip = here % 2, here // 2
-    across = jnp.where(core == 0, chip // N, chip % N)
-    edge = (across == 0) | (across == N - 1)
-
     blocks = {"own": make_unit(lengths, embeddings)}
     table = jnp.asarray(np.stack([plan(i) for i in range(total)]))[here]
     blocks["wide"] = along(blocks["own"], wide)
@@ -301,19 +335,18 @@
     blocks["sib_near"] = swap(blocks["near"])
     blocks["sib_wide"] = swap(blocks["wide"])
     (scores,) = run_pairs(0, table, scores, blocks)
-    pick = jnp.where(edge, blocks["own"], after(blocks["side"], scores))
+    pick = run_pick(table, blocks["own"], after(blocks["side"], scores))
     blocks["next"] = over(pick, near)
     (scores,) = run_pairs(1, table, after(scores, pick), blocks)
     from_side = over(scores, wide)
     far = after(blocks["far"], scores)
     blocks["sib_far"] = (swap(far[:HALF]), swap(far[HALF:]))
     scores, blocks["near"] = run_pairs(2, table, scores, blocks, keep="near")
-    line, last = run_pairs(3, table, scores, blocks, given=(swap(scores),))
-
-    from_next = over(last, ahead_of)
-    groups = [[device(i, j, c) for i in range(N)] for j in range(N) for c in range(2)]
-    parts = lax.all_to_all(line, "sample", 0, 0, tiled=True, axis_index_groups=groups)
-    result = jnp.sum(parts, axis=0) + from_side[SIDE] + from_next[0]
+    mine, *rest = run_pairs(3, table, scores, blocks, given=(swap(scores),))
+    result = mine[0] + from_side[SIDE]
+    for rows, step in zip(rest, (near, wide, across_from)):
+        result += along(rows, step)[0]
+    result += over(rest[-1], ahead_of)[0]
     ahead, behind = result[:total], result[total : 2 * total]
     offdiag = jnp.arange(total, dtype=jnp.int32) != here
     utility = jnp.sum(jnp.where(offdiag, ahead + behind, 0.0)) / jnp.float32(2 * (total - 1))

time: 71.6 us -> 68.2 us (0.953)
  blocking collectives: 9.56 us -> 0 us
  waiting for transfers between devices: 21 us -> 27.2 us
  starting transfers between devices: 15.2 us -> 18.8 us
  Pallas kernels: 18.9 us -> 15.3 us
    all_to_all x1 -> x0, blocking collectives: 9.56 us -> none  [body(): lax.all_to_all(line, 'sample', 0, 0, tiled=True, axis_index_groups=groups)]
    ppermute x4, waiting for transfers between devices: 6.39 us -> 11.3 us  [over(): return lax.ppermute(x, 'sample', moves)]
    ppermute x3 -> x6, starting transfers between devices: 4.21 us -> 8.98 us  [along(): return lax.ppermute(x, 'sample', moves)]
    pallas_call x4, Pallas kernels: 15.7 us -> 12.3 us  [run_pairs(): pl.pallas_call(functools.partial(pairs_kernel, stage, names, [len(b) for...]
    ppermute x3 -> x6, waiting for transfers between devices: 12.7 us -> 14 us  [along(): return lax.ppermute(x, 'sample', moves)]
    pallas_call x1, Pallas kernels: 2.66 us -> 1.42 us  [run_first(): pl.pallas_call(first_kernel, out_shape=jax.ShapeDtypeStruct((ROWS, 128),...]
    ppermute x4, starting transfers between devices: 9.45 us -> 8.25 us  [over(): return lax.ppermute(x, 'sample', moves)]
    pallas_call x0 -> x1, Pallas kernels: none -> 1.01 us  [run_pick(): pl.pallas_call(pick_kernel, out_shape=jax.ShapeDtypeStruct(own.shape, own...]
  transfers between devices with their start and end apart: 13 -> 16, of which waited for: 4 -> 6; matrix products, arithmetic and copies ran while one was open for 1% -> 1% of each run, Pallas kernels for 26% -> 22%
where the time goes in v7:
time: 68.2 us; the launch traced here: 67.5 us
  waiting for transfers between devices  27.2 us (40%)
  starting transfers between devices  18.8 us (28%)
  Pallas kernels  15.3 us (22%)
  between operations  3.07 us (5%)
  local copies, waits for them, and re-layouts  1.98 us (3%)
  other arithmetic  1.09 us (2%)
    ppermute x6, waiting for transfers between devices, along(): return lax.ppermute(x, 'sample', moves)  14 us
    pallas_call x4, Pallas kernels, run_pairs(): pl.pallas_call(functools.partial(pairs_kernel, stage, names, [len(b) for...  12.3 us
    ppermute x4, waiting for transfers between devices, over(): return lax.ppermute(x, 'sample', moves)  11.3 us
    ppermute x6, starting transfers between devices, along(): return lax.ppermute(x, 'sample', moves)  8.98 us
    ppermute x4, starting transfers between devices, over(): return lax.ppermute(x, 'sample', moves)  8.25 us
    ppermute x6, waiting for transfers between devices, swap(): return lax.ppermute(x, 'sample', [(i, i ^ 1) for i in range(2 * N * N)])  1.91 us
    ppermute x6, starting transfers between devices, swap(): return lax.ppermute(x, 'sample', [(i, i ^ 1) for i in range(2 * N * N)])  1.6 us
    pallas_call x1, Pallas kernels, run_first(): pl.pallas_call(first_kernel, out_shape=jax.ShapeDtypeStruct((ROWS, 128),...  1.42 us
  transfers between devices with their start and end apart: 16, of which 6 were waited for; matrix products, arithmetic and copies ran while one was open for 1% of the time, Pallas kernels for 22%

profile of v7, /device:TPU:0, one launch (start us, length us, event | category | flops | bytes accessed | tf_op | source)
XLA Modules:
  0.0 67.5 jit_solution(3872860632472305731)
XLA Ops:
  1.3 0.0 copy-start
  1.3 1.2 %copy-done = bf16[1,512,1024]{2,1,0:T(8,128)(2,1)S(1)} copy-done((bf16[1,512,1024]{2,1,0:T(8,128)(2,1)S(1)}, bf16[1,512,1024]{2,1,0:T(8,128)(2,1)}, u32[]{:S(2)}) %copy-start) | copy-done | bytes 1048600
  2.5 0.6 unit.1.own_ref.refs_1_.refs_2_.refs_4_
  3.1 4.2 %collective-permute-start.2 = (bf16[528,1024]{1,0:T(8,128)(2,1)S(1)}, bf16[528,1024]{1,0:T(8,128)(2,1)S(1)}, u32[]{:S(2)}, u32[]{:S(2)}) collective-permute-start(bf16[528,1024]{1,0:T(8,128)(2,1)S(1)} %unit.1.own_ref.refs_1_.refs_2_.refs_4_), channel_id=1, source_target_pairs={{0,6},{1,25},{8,14},{3,27},{16,22},{5,29},{24,30},{7,31},{2,4},{9,... | collective-permute-start | bytes 3244040 | tf_op jit(solution)/shard_map/ppermute | solution.py:44
  7.3 0.0 collective-permute-start.1
  7.3 0.7 %dynamic-slice_bitcast_fusion.tab_ref = s32[28]{0:T(128)S(1)} fusion(s32[32,28]{1,0:T(8,128)} %constant.15.clone, s32[]{:T(128)S(6)} %select_n.7), kind=kLoop, calls=%fused_computation.6 | loop fusion | bytes 228 | tf_op jit(solution)/shard_map/squeeze | solution.py:328
  8.0 0.0 collective-permute-start
  8.0 12.4 %collective-permute-done.2.refs_3_.refs_6_.refs_5_ = bf16[528,1024]{1,0:T(8,128)(2,1)S(1)} collective-permute-done((bf16[528,1024]{1,0:T(8,128)(2,1)S(1)}, bf16[528,1024]{1,0:T(8,128)(2,1)S(1)}, u32[]{:S(2)}, u32[]{:S(2)}) %collective-permute-start.2) | collective-permute-done | bytes 1081376 | tf_op jit(solution)/shard_map/ppermute | solution.py:44
  20.5 3.0 %collective-permute-start.3 = (bf16[528,1024]{1,0:T(8,128)(2,1)S(1)}, bf16[528,1024]{1,0:T(8,128)(2,1)S(1)}, u32[]{:S(2)}, u32[]{:S(2)}) collective-permute-start(bf16[528,1024]{1,0:T(8,128)(2,1)S(1)} %unit.1.own_ref.refs_1_.refs_2_.refs_4_), channel_id=1, source_target_pairs={{0,24},{1,7},{8,16},{3,5},{16,8},{5,3},{24,0},{7,1},{2,26},{9,15},... | collective-permute-start | bytes 3244040 | tf_op jit(solution)/shard_map/ppermute | solution.py:49
  23.5 0.0 collective-permute-done.1.refs_0_.refs_1_
  23.5 0.0 collective-permute-start.4
  23.5 0.0 collective-permute-start.5
  23.5 0.5 collective-permute-start.8
  24.0 0.0 collective-permute-done.sib_ref.refs_2_.refs_3_
  24.0 1.4 %pairs_0.1.before_ref = f32[16,128]{1,0:T(8,128)S(1)} custom-call(s32[1]{0:T(128)} %bitcast.1.here_ref, bf16[528,1024]{1,0:T(8,128)(2,1)S(1)} %unit.1.own_ref.refs_1_.refs_2_.refs_4_, bf16[528,1024]{1,0:T(8,128)(2,1)S(1)} %collective-permute-done.sib_ref.refs_2_.refs_3_), custom_call_target="tpu_custom_call" | custom-call | flops 1073741824 | bytes 1081344 | tf_op jit(solution)/shard_map/pairs_0/pallas_call | solution.py:199
  25.4 2.9 %pairs_1.1.before_ref = f32[16,128]{1,0:T(8,128)S(1)} custom-call(s32[28]{0:T(128)S(1)} %dynamic-slice_bitcast_fusion.tab_ref, f32[16,128]{1,0:T(8,128)S(1)} %pairs_0.1.before_ref, bf16[528,1024]{1,0:T(8,128)(2,1)S(1)} %collective-permute-done.1.refs_0_.refs_1_, bf16[528,1024]{1,0:T(8,128)(2,1)S(1)} %unit.1.own_ref.refs_1_.refs_2_.refs_4_, ...), custom_call_target="tpu_custom_call" | custom-call | flops 2684354560 | bytes 4194304 | tf_op jit(solution)/shard_map/pairs_1/pallas_call | solution.py:271
  28.3 8.5 %collective-permute-done.3.side_ref.refs_5_ = bf16[528,1024]{1,0:T(8,128)(2,1)S(1)} collective-permute-done((bf16[528,1024]{1,0:T(8,128)(2,1)S(1)}, bf16[528,1024]{1,0:T(8,128)(2,1)S(1)}, u32[]{:S(2)}, u32[]{:S(2)}) %collective-permute-start.3) | collective-permute-done | bytes 1081376 | tf_op jit(solution)/shard_map/ppermute | solution.py:49
  36.8 1.0 %pick.1 = bf16[528,1024]{1,0:T(8,128)(2,1)S(1)} custom-call(s32[28]{0:T(128)S(1)} %dynamic-slice_bitcast_fusion.tab_ref, bf16[528,1024]{1,0:T(8,128)(2,1)S(1)} %unit.1.own_ref.refs_1_.refs_2_.refs_4_, bf16[528,1024]{1,0:T(8,128)(2,1)S(1)} %collective-permute-done.3.side_ref.refs_5_), custom_call_target="tpu_custom_call" | custom-call | tf_op jit(solution)/shard_map/pick/pallas_call | solution.py:307
  37.9 0.4 collective-permute-start.10
  38.3 0.3 collective-permute-done.4.refs_0_.refs_1_
  38.6 0.0 collective-permute-done.5.refs_4_
  38.6 3.9 %pairs_2.1.before_ref = f32[16,128]{1,0:T(8,128)S(1)} custom-call(s32[28]{0:T(128)S(1)} %dynamic-slice_bitcast_fusion.tab_ref, f32[16,128]{1,0:T(8,128)S(1)} %pairs_1.1.before_ref, bf16[528,1024]{1,0:T(8,128)(2,1)S(1)} %collective-permute-done.4.refs_0_.refs_1_, bf16[528,1024]{1,0:T(8,128)(2,1)S(1)} %collective-permute-done.1.refs_0_.refs_1_, ...), custom_call_target="tpu_custom_call" | custom-call | flops 4294967296 | bytes 7340032 | tf_op jit(solution)/shard_map/pairs_2/pallas_call | solution.py:271
  42.6 0.1 collective-permute-start.7
  42.8 0.8 %collective-permute-start.6 = (bf16[256,1024]{1,0:T(8,128)(2,1)S(1)}, bf16[256,1024]{1,0:T(8,128)(2,1)S(1)}, u32[]{:S(2)}, u32[]{:S(2)}) collective-permute-start(bf16[256,1024]{1,0:T(8,128)(2,1)S(1)} %slice.30), channel_id=1, source_target_pairs={{0,1},{1,0},{2,3},{3,2},{4,5},{5,4},{6,7},{7,6},{8,9},{9,8},{10,11... | collective-permute-start | bytes 1572872 | tf_op jit(solution)/shard_map/ppermute | solution.py:53
  43.5 0.0 collective-permute-done.8.refs_4_
  43.5 1.9 %collective-permute-done.6.refs_2_ = bf16[256,1024]{1,0:T(8,128)(2,1)S(1)} collective-permute-done((bf16[256,1024]{1,0:T(8,128)(2,1)S(1)}, bf16[256,1024]{1,0:T(8,128)(2,1)S(1)}, u32[]{:S(2)}, u32[]{:S(2)}) %collective-permute-start.6) | collective-permute-done | bytes 524320 | tf_op jit(solution)/shard_map/ppermute | solution.py:53
  45.4 0.0 collective-permute-done.7.refs_3_
  45.4 2.4 %pairs_3.1 = (f32[16,128]{1,0:T(8,128)S(1)}, bf16[528,1024]{1,0:T(8,128)(2,1)S(1)}) custom-call(s32[28]{0:T(128)S(1)} %dynamic-slice_bitcast_fusion.tab_ref, f32[16,128]{1,0:T(8,128)S(1)} %pairs_2.1.before_ref, bf16[528,1024]{1,0:T(8,128)(2,1)S(1)} %collective-permute-done.4.refs_0_.refs_1_, bf16[528,1024]{1,0:T(8,128)(2,1)S(1)} %collective-permute-done.1.refs_0_.refs_1_, ...), custom_call_target="tpu_custom_call" | custom-call | tf_op jit(solution)/shard_map/pairs_3/pallas_call | solution.py:271
  47.8 0.3 collective-permute-start.9
  48.1 2.3 %collective-permute-start.11 = (f32[16,128]{1,0:T(8,128)S(1)}, f32[16,128]{1,0:T(8,128)S(1)}, u32[]{:S(2)}, u32[]{:S(2)}) collective-permute-start(f32[16,128]{1,0:T(8,128)S(1)} %pairs_2.1.before_ref), channel_id=1, source_target_pairs={{0,24},{1,7},{8,16},{3,5},{16,8},{5,3},{24,0},{7,1},{2,26},{9,15},... | collective-permute-start | bytes 24584 | tf_op jit(solution)/shard_map/ppermute | solution.py:49
  50.4 0.0 collective-permute-done.9.refs_0_
  50.4 2.7 %collective-permute-done.10.refs_3_ = bf16[528,1024]{1,0:T(8,128)(2,1)S(1)} collective-permute-done((bf16[528,1024]{1,0:T(8,128)(2,1)S(1)}, bf16[528,1024]{1,0:T(8,128)(2,1)S(1)}, u32[]{:S(2)}, u32[]{:S(2)}) %collective-permute-start.10) | collective-permute-done | bytes 1081376 | tf_op jit(solution)/shard_map/ppermute | solution.py:49
  53.1 3.1 %pairs_4.1 = (f32[8,128]{1,0:T(8,128)S(1)}, f32[8,128]{1,0:T(8,128)S(1)}, f32[8,128]{1,0:T(8,128)S(1)}, f32[8,128]{1,0:T(8,128)S(1)}, f32[8,128]{1,0:T(8,128)S(1)}) custom-call(s32[28]{0:T(128)S(1)} %dynamic-slice_bitcast_fusion.tab_ref, f32[16,128]{1,0:T(8,128)S(1)} %get-tuple-element.21.before_ref, f32[16,128]{1,0:T(8,128)S(1)} %collective-permute-done.9.refs_0_, ...), custom_call_target="tpu_custom_call" | custom-call | tf_op jit(solution)/shard_map/pairs_4/pallas_call | solution.py:271
  56.2 0.1 collective-permute-start.12
  56.3 3.3 %collective-permute-start.13 = (f32[8,128]{1,0:T(8,128)S(1)}, f32[8,128]{1,0:T(8,128)S(1)}, u32[]{:S(2)}, u32[]{:S(2)}) collective-permute-start(f32[8,128]{1,0:T(8,128)S(1)} %get-tuple-element.25), channel_id=1, source_target_pairs={{0,6},{1,25},{8,14},{3,27},{16,22},{5,29},{24,30},{7,31},{2,4},{9,... | collective-permute-start | bytes 12296 | tf_op jit(solution)/shard_map/ppermute | solution.py:44
  59.6 1.4 %collective-permute-start.14 = (f32[8,128]{1,0:T(8,128)S(1)}, f32[8,128]{1,0:T(8,128)S(1)}, u32[]{:S(2)}, u32[]{:S(2)}) collective-permute-start(f32[8,128]{1,0:T(8,128)S(1)} %get-tuple-element.26), channel_id=1, source_target_pairs={{0,4},{1,17},{8,12},{3,19},{16,20},{5,21},{24,28},{7,23},{2,6},{9,... | collective-permute-start | bytes 12296 | tf_op jit(solution)/shard_map/ppermute | solution.py:44
  61.0 2.5 %collective-permute-start.15 = (f32[8,128]{1,0:T(8,128)S(1)}, f32[8,128]{1,0:T(8,128)S(1)}, u32[]{:S(2)}, u32[]{:S(2)}) collective-permute-start(f32[8,128]{1,0:T(8,128)S(1)} %get-tuple-element.27), channel_id=1, source_target_pairs={{0,16},{1,5},{8,0},{3,1},{16,24},{5,7},{24,8},{7,3},{2,18},{9,13},... | collective-permute-start | bytes 12296 | tf_op jit(solution)/shard_map/ppermute | solution.py:49
  63.4 0.0 collective-permute-done.11
  63.4 0.0 collective-permute-done.12
  63.4 0.0 collective-permute-done.13
  63.4 1.3 %collective-permute-done.14 = f32[8,128]{1,0:T(8,128)S(1)} collective-permute-done((f32[8,128]{1,0:T(8,128)S(1)}, f32[8,128]{1,0:T(8,128)S(1)}, u32[]{:S(2)}, u32[]{:S(2)}) %collective-permute-start.14) | collective-permute-done | bytes 4128 | tf_op jit(solution)/shard_map/ppermute | solution.py:44
  64.7 0.0 collective-permute-done.15
  64.7 1.1 %fusion = (f32[]{:T(128)}, f32[1,32]{1,0:T(1,128)}) fusion(f32[1,128]{1,0:T(1,128)S(1)} %slice_add_fusion.1, s32[]{:T(128)} %axis_index.12), kind=kLoop, calls=%fused_computation.1 | loop fusion | flops 127 | bytes 392 | tf_op jit(solution)/shard_map/reduce_sum | solution.py:352
  (3 shorter events, 0.1 us)
Async XLA Ops:
  1.3 1.2 %copy-start = (bf16[1,512,1024]{2,1,0:T(8,128)(2,1)S(1)}, bf16[1,512,1024]{2,1,0:T(8,128)(2,1)}, u32[]{:S(2)}) copy-start(bf16[1,512,1024]{2,1,0:T(8,128)(2,1)} %emb_ref.1) | copy-start | bytes 3145732
  3.1 17.3 %collective-permute-start.2 = (bf16[528,1024]{1,0:T(8,128)(2,1)S(1)}, bf16[528,1024]{1,0:T(8,128)(2,1)S(1)}, u32[]{:S(2)}, u32[]{:S(2)}) collective-permute-start(bf16[528,1024]{1,0:T(8,128)(2,1)S(1)} %unit.1.own_ref.refs_1_.refs_2_.refs_4_), channel_id=1, source_target_pairs={{0,6},{1,25},{8,14},{3,27},{16,22},{5,29},{24,30},{7,31},{2,4},{9,... | collective-permute-start | bytes 3244040 | tf_op jit(solution)/shard_map/ppermute | solution.py:44
  7.3 16.1 %collective-permute-start.1 = (bf16[528,1024]{1,0:T(8,128)(2,1)S(1)}, bf16[528,1024]{1,0:T(8,128)(2,1)S(1)}, u32[]{:S(2)}, u32[]{:S(2)}) collective-permute-start(bf16[528,1024]{1,0:T(8,128)(2,1)S(1)} %unit.1.own_ref.refs_1_.refs_2_.refs_4_), channel_id=1, source_target_pairs={{0,2},{1,9},{8,10},{3,11},{16,18},{5,13},{24,26},{7,15},{2,0},{9,1... | collective-permute-start | bytes 3244040 | tf_op jit(solution)/shard_map/ppermute | solution.py:44
  8.0 16.0 %collective-permute-start = (bf16[528,1024]{1,0:T(8,128)(2,1)S(1)}, bf16[528,1024]{1,0:T(8,128)(2,1)S(1)}, u32[]{:S(2)}, u32[]{:S(2)}) collective-permute-start(bf16[528,1024]{1,0:T(8,128)(2,1)S(1)} %unit.1.own_ref.refs_1_.refs_2_.refs_4_), channel_id=1, source_target_pairs={{0,1},{1,0},{2,3},{3,2},{4,5},{5,4},{6,7},{7,6},{8,9},{9,8},{10,11... | collective-permute-start | bytes 3244040 | tf_op jit(solution)/shard_map/ppermute | solution.py:53
  20.5 16.4 %collective-permute-start.3 = (bf16[528,1024]{1,0:T(8,128)(2,1)S(1)}, bf16[528,1024]{1,0:T(8,128)(2,1)S(1)}, u32[]{:S(2)}, u32[]{:S(2)}) collective-permute-start(bf16[528,1024]{1,0:T(8,128)(2,1)S(1)} %unit.1.own_ref.refs_1_.refs_2_.refs_4_), channel_id=1, source_target_pairs={{0,24},{1,7},{8,16},{3,5},{16,8},{5,3},{24,0},{7,1},{2,26},{9,15},... | collective-permute-start | bytes 3244040 | tf_op jit(solution)/shard_map/ppermute | solution.py:49
  23.5 15.2 %collective-permute-start.4 = (bf16[528,1024]{1,0:T(8,128)(2,1)S(1)}, bf16[528,1024]{1,0:T(8,128)(2,1)S(1)}, u32[]{:S(2)}, u32[]{:S(2)}) collective-permute-start(bf16[528,1024]{1,0:T(8,128)(2,1)S(1)} %collective-permute-done.2.refs_3_.refs_6_.refs_5_), channel_id=1, source_target_pairs={{0,2},{1,9},{8,10},{3,11},{16,18},{5,13},{24,26},{7,15},{2,0},{9,1... | collective-permute-start | bytes 3244040 | tf_op jit(solution)/shard_map/ppermute | solution.py:44
  23.5 15.2 %collective-permute-start.5 = (bf16[528,1024]{1,0:T(8,128)(2,1)S(1)}, bf16[528,1024]{1,0:T(8,128)(2,1)S(1)}, u32[]{:S(2)}, u32[]{:S(2)}) collective-permute-start(bf16[528,1024]{1,0:T(8,128)(2,1)S(1)} %collective-permute-done.1.refs_0_.refs_1_), channel_id=1, source_target_pairs={{0,1},{1,0},{2,3},{3,2},{4,5},{5,4},{6,7},{7,6},{8,9},{9,8},{10,11... | collective-permute-start | bytes 3244040 | tf_op jit(solution)/shard_map/ppermute | solution.py:53
  23.5 20.0 %collective-permute-start.8 = (bf16[528,1024]{1,0:T(8,128)(2,1)S(1)}, bf16[528,1024]{1,0:T(8,128)(2,1)S(1)}, u32[]{:S(2)}, u32[]{:S(2)}) collective-permute-start(bf16[528,1024]{1,0:T(8,128)(2,1)S(1)} %collective-permute-done.2.refs_3_.refs_6_.refs_5_), channel_id=1, source_target_pairs={{0,1},{1,0},{2,3},{3,2},{4,5},{5,4},{6,7},{7,6},{8,9},{9,8},{10,11... | collective-permute-start | bytes 3244040 | tf_op jit(solution)/shard_map/ppermute | solution.py:53
  37.9 15.2 %collective-permute-start.10 = (bf16[528,1024]{1,0:T(8,128)(2,1)S(1)}, bf16[528,1024]{1,0:T(8,128)(2,1)S(1)}, u32[]{:S(2)}, u32[]{:S(2)}) collective-permute-start(bf16[528,1024]{1,0:T(8,128)(2,1)S(1)} %pick.1), channel_id=1, source_target_pairs={{0,8},{1,3},{8,0},{3,1},{16,24},{5,7},{24,16},{7,5},{2,10},{9,11},... | collective-permute-start | bytes 3244040 | tf_op jit(solution)/shard_map/ppermute | solution.py:49
  42.6 2.8 %collective-permute-start.7 = (bf16[272,1024]{1,0:T(8,128)(2,1)S(1)}, bf16[272,1024]{1,0:T(8,128)(2,1)S(1)}, u32[]{:S(2)}, u32[]{:S(2)}) collective-permute-start(bf16[272,1024]{1,0:T(8,128)(2,1)S(1)} %slice.31), channel_id=1, source_target_pairs={{0,1},{1,0},{2,3},{3,2},{4,5},{5,4},{6,7},{7,6},{8,9},{9,8},{10,11... | collective-permute-start | bytes 1671176 | tf_op jit(solution)/shard_map/ppermute | solution.py:53
  42.8 2.6 %collective-permute-start.6 = (bf16[256,1024]{1,0:T(8,128)(2,1)S(1)}, bf16[256,1024]{1,0:T(8,128)(2,1)S(1)}, u32[]{:S(2)}, u32[]{:S(2)}) collective-permute-start(bf16[256,1024]{1,0:T(8,128)(2,1)S(1)} %slice.30), channel_id=1, source_target_pairs={{0,1},{1,0},{2,3},{3,2},{4,5},{5,4},{6,7},{7,6},{8,9},{9,8},{10,11... | collective-permute-start | bytes 1572872 | tf_op jit(solution)/shard_map/ppermute | solution.py:53
  47.8 2.6 %collective-permute-start.9 = (f32[16,128]{1,0:T(8,128)S(1)}, f32[16,128]{1,0:T(8,128)S(1)}, u32[]{:S(2)}, u32[]{:S(2)}) collective-permute-start(f32[16,128]{1,0:T(8,128)S(1)} %get-tuple-element.21.before_ref), channel_id=1, source_target_pairs={{0,1},{1,0},{2,3},{3,2},{4,5},{5,4},{6,7},{7,6},{8,9},{9,8},{10,11... | collective-permute-start | bytes 24584 | tf_op jit(solution)/shard_map/ppermute | solution.py:53
  48.1 15.4 %collective-permute-start.11 = (f32[16,128]{1,0:T(8,128)S(1)}, f32[16,128]{1,0:T(8,128)S(1)}, u32[]{:S(2)}, u32[]{:S(2)}) collective-permute-start(f32[16,128]{1,0:T(8,128)S(1)} %pairs_2.1.before_ref), channel_id=1, source_target_pairs={{0,24},{1,7},{8,16},{3,5},{16,8},{5,3},{24,0},{7,1},{2,26},{9,15},... | collective-permute-start | bytes 24584 | tf_op jit(solution)/shard_map/ppermute | solution.py:49
  56.2 7.2 %collective-permute-start.12 = (f32[8,128]{1,0:T(8,128)S(1)}, f32[8,128]{1,0:T(8,128)S(1)}, u32[]{:S(2)}, u32[]{:S(2)}) collective-permute-start(f32[8,128]{1,0:T(8,128)S(1)} %get-tuple-element.24), channel_id=1, source_target_pairs={{0,2},{1,9},{8,10},{3,11},{16,18},{5,13},{24,26},{7,15},{2,0},{9,1... | collective-permute-start | bytes 12296 | tf_op jit(solution)/shard_map/ppermute | solution.py:44
  56.3 7.2 %collective-permute-start.13 = (f32[8,128]{1,0:T(8,128)S(1)}, f32[8,128]{1,0:T(8,128)S(1)}, u32[]{:S(2)}, u32[]{:S(2)}) collective-permute-start(f32[8,128]{1,0:T(8,128)S(1)} %get-tuple-element.25), channel_id=1, source_target_pairs={{0,6},{1,25},{8,14},{3,27},{16,22},{5,29},{24,30},{7,31},{2,4},{9,... | collective-permute-start | bytes 12296 | tf_op jit(solution)/shard_map/ppermute | solution.py:44
  59.6 5.1 %collective-permute-start.14 = (f32[8,128]{1,0:T(8,128)S(1)}, f32[8,128]{1,0:T(8,128)S(1)}, u32[]{:S(2)}, u32[]{:S(2)}) collective-permute-start(f32[8,128]{1,0:T(8,128)S(1)} %get-tuple-element.26), channel_id=1, source_target_pairs={{0,4},{1,17},{8,12},{3,19},{16,20},{5,21},{24,28},{7,23},{2,6},{9,... | collective-permute-start | bytes 12296 | tf_op jit(solution)/shard_map/ppermute | solution.py:44
  61.0 3.8 %collective-permute-start.15 = (f32[8,128]{1,0:T(8,128)S(1)}, f32[8,128]{1,0:T(8,128)S(1)}, u32[]{:S(2)}, u32[]{:S(2)}) collective-permute-start(f32[8,128]{1,0:T(8,128)S(1)} %get-tuple-element.27), channel_id=1, source_target_pairs={{0,16},{1,5},{8,0},{3,1},{16,24},{5,7},{24,8},{7,3},{2,18},{9,13},... | collective-permute-start | bytes 12296 | tf_op jit(solution)/shard_map/ppermute | solution.py:49

commit v8 on v7

--- a/solution.py
+++ b/solution.py
@@ -330,8 +330,8 @@
     blocks["near"] = along(blocks["own"], near)
     blocks["sib"] = swap(after(blocks["own"], table))
     scores = run_first(here[None], blocks["own"], blocks["sib"])
-    blocks["side"] = over(after(blocks["own"], blocks["wide"]), wide)
-    blocks["far"] = along(after(blocks["wide"], blocks["near"]), near)
+    blocks["side"] = over(after(blocks["own"], blocks["near"]), wide)
+    blocks["far"] = along(blocks["wide"], near)
     blocks["sib_near"] = swap(blocks["near"])
     blocks["sib_wide"] = swap(blocks["wide"])
     (scores,) = run_pairs(0, table, scores, blocks)

time: 68.2 us -> 67 us (0.982)
  waiting for transfers between devices: 27.2 us -> 22.3 us
  starting transfers between devices: 18.8 us -> 22.8 us
    ppermute x6, starting transfers between devices: 8.98 us -> 12.1 us  [along(): return lax.ppermute(x, 'sample', moves)]
    ppermute x4, waiting for transfers between devices: 11.3 us -> 8.35 us  [over(): return lax.ppermute(x, 'sample', moves)]
    ppermute x6, waiting for transfers between devices: 14 us -> 12.1 us  [along(): return lax.ppermute(x, 'sample', moves)]
    ppermute x4, starting transfers between devices: 8.25 us -> 9.09 us  [over(): return lax.ppermute(x, 'sample', moves)]
  transfers between devices with their start and end apart: 16 -> 16, of which waited for: 6 -> 7; matrix products, arithmetic and copies ran while one was open for 1% -> 1% of each run, Pallas kernels for 22% -> 22%
where the time goes in v8:
time: 67 us; the launch traced here: 66.6 us
  starting transfers between devices  22.8 us (34%)
  waiting for transfers between devices  22.3 us (33%)
  Pallas kernels  15.3 us (23%)
  between operations  3.06 us (5%)
  local copies, waits for them, and re-layouts  1.98 us (3%)
  other arithmetic  1.09 us (2%)
    pallas_call x4, Pallas kernels, run_pairs(): pl.pallas_call(functools.partial(pairs_kernel, stage, names, [len(b) for...  12.3 us
    ppermute x6, waiting for transfers between devices, along(): return lax.ppermute(x, 'sample', moves)  12.1 us
    ppermute x6, starting transfers between devices, along(): return lax.ppermute(x, 'sample', moves)  12.1 us
    ppermute x4, starting transfers between devices, over(): return lax.ppermute(x, 'sample', moves)  9.09 us
    ppermute x4, waiting for transfers between devices, over(): return lax.ppermute(x, 'sample', moves)  8.35 us
    ppermute x6, waiting for transfers between devices, swap(): return lax.ppermute(x, 'sample', [(i, i ^ 1) for i in range(2 * N * N)])  1.91 us
    ppermute x6, starting transfers between devices, swap(): return lax.ppermute(x, 'sample', [(i, i ^ 1) for i in range(2 * N * N)])  1.6 us
    pallas_call x1, Pallas kernels, run_first(): pl.pallas_call(first_kernel, out_shape=jax.ShapeDtypeStruct((ROWS, 128),...  1.42 us
  transfers between devices with their start and end apart: 16, of which 7 were waited for; matrix products, arithmetic and copies ran while one was open for 1% of the time, Pallas kernels for 22%

profile of v8, /device:TPU:0, one launch (start us, length us, event | category | flops | bytes accessed | tf_op | source)
XLA Modules:
  0.0 66.6 jit_solution(16058916852846550722)
XLA Ops:
  1.3 0.0 copy-start
  1.3 1.2 %copy-done = bf16[1,512,1024]{2,1,0:T(8,128)(2,1)S(1)} copy-done((bf16[1,512,1024]{2,1,0:T(8,128)(2,1)S(1)}, bf16[1,512,1024]{2,1,0:T(8,128)(2,1)}, u32[]{:S(2)}) %copy-start) | copy-done | bytes 1048600
  2.5 0.6 unit.1.own_ref.refs_1_.refs_2_.refs_4_
  3.1 2.1 %collective-permute-start.1 = (bf16[528,1024]{1,0:T(8,128)(2,1)S(1)}, bf16[528,1024]{1,0:T(8,128)(2,1)S(1)}, u32[]{:S(2)}, u32[]{:S(2)}) collective-permute-start(bf16[528,1024]{1,0:T(8,128)(2,1)S(1)} %unit.1.own_ref.refs_1_.refs_2_.refs_4_), channel_id=1, source_target_pairs={{0,2},{1,9},{8,10},{3,11},{16,18},{5,13},{24,26},{7,15},{2,0},{9,1... | collective-permute-start | bytes 3244040 | tf_op jit(solution)/shard_map/ppermute | solution.py:44
  5.2 2.5 %collective-permute-start.2 = (bf16[528,1024]{1,0:T(8,128)(2,1)S(1)}, bf16[528,1024]{1,0:T(8,128)(2,1)S(1)}, u32[]{:S(2)}, u32[]{:S(2)}) collective-permute-start(bf16[528,1024]{1,0:T(8,128)(2,1)S(1)} %unit.1.own_ref.refs_1_.refs_2_.refs_4_), channel_id=1, source_target_pairs={{0,6},{1,25},{8,14},{3,27},{16,22},{5,29},{24,30},{7,31},{2,4},{9,... | collective-permute-start | bytes 3244040 | tf_op jit(solution)/shard_map/ppermute | solution.py:44
  7.7 0.7 %dynamic-slice_bitcast_fusion.tab_ref = s32[28]{0:T(128)S(1)} fusion(s32[32,28]{1,0:T(8,128)} %constant.15.clone, s32[]{:T(128)S(6)} %select_n.7), kind=kLoop, calls=%fused_computation.6 | loop fusion | bytes 228 | tf_op jit(solution)/shard_map/squeeze | solution.py:328
  8.4 0.0 collective-permute-start
  8.4 9.9 %collective-permute-done.1.refs_0_.refs_1_ = bf16[528,1024]{1,0:T(8,128)(2,1)S(1)} collective-permute-done((bf16[528,1024]{1,0:T(8,128)(2,1)S(1)}, bf16[528,1024]{1,0:T(8,128)(2,1)S(1)}, u32[]{:S(2)}, u32[]{:S(2)}) %collective-permute-start.1) | collective-permute-done | bytes 1081376 | tf_op jit(solution)/shard_map/ppermute | solution.py:44
  18.4 3.1 %collective-permute-start.3 = (bf16[528,1024]{1,0:T(8,128)(2,1)S(1)}, bf16[528,1024]{1,0:T(8,128)(2,1)S(1)}, u32[]{:S(2)}, u32[]{:S(2)}) collective-permute-start(bf16[528,1024]{1,0:T(8,128)(2,1)S(1)} %unit.1.own_ref.refs_1_.refs_2_.refs_4_), channel_id=1, source_target_pairs={{0,24},{1,7},{8,16},{3,5},{16,8},{5,3},{24,0},{7,1},{2,26},{9,15},... | collective-permute-start | bytes 3244040 | tf_op jit(solution)/shard_map/ppermute | solution.py:49
  21.5 0.1 collective-permute-done.2.refs_3_.refs_6_.refs_5_
  21.6 1.8 %collective-permute-start.4 = (bf16[528,1024]{1,0:T(8,128)(2,1)S(1)}, bf16[528,1024]{1,0:T(8,128)(2,1)S(1)}, u32[]{:S(2)}, u32[]{:S(2)}) collective-permute-start(bf16[528,1024]{1,0:T(8,128)(2,1)S(1)} %collective-permute-done.2.refs_3_.refs_6_.refs_5_), channel_id=1, source_target_pairs={{0,2},{1,9},{8,10},{3,11},{16,18},{5,13},{24,26},{7,15},{2,0},{9,1... | collective-permute-start | bytes 3244040 | tf_op jit(solution)/shard_map/ppermute | solution.py:44
  23.4 0.0 collective-permute-start.5
  23.4 0.5 collective-permute-start.8
  23.9 0.0 collective-permute-done.sib_ref.refs_2_.refs_3_
  23.9 1.4 %pairs_0.1.before_ref = f32[16,128]{1,0:T(8,128)S(1)} custom-call(s32[1]{0:T(128)} %bitcast.1.here_ref, bf16[528,1024]{1,0:T(8,128)(2,1)S(1)} %unit.1.own_ref.refs_1_.refs_2_.refs_4_, bf16[528,1024]{1,0:T(8,128)(2,1)S(1)} %collective-permute-done.sib_ref.refs_2_.refs_3_), custom_call_target="tpu_custom_call" | custom-call | flops 1073741824 | bytes 1081344 | tf_op jit(solution)/shard_map/pairs_0/pallas_call | solution.py:199
  25.3 2.9 %pairs_1.1.before_ref = f32[16,128]{1,0:T(8,128)S(1)} custom-call(s32[28]{0:T(128)S(1)} %dynamic-slice_bitcast_fusion.tab_ref, f32[16,128]{1,0:T(8,128)S(1)} %pairs_0.1.before_ref, bf16[528,1024]{1,0:T(8,128)(2,1)S(1)} %collective-permute-done.1.refs_0_.refs_1_, bf16[528,1024]{1,0:T(8,128)(2,1)S(1)} %unit.1.own_ref.refs_1_.refs_2_.refs_4_, ...), custom_call_target="tpu_custom_call" | custom-call | flops 2684354560 | bytes 4194304 | tf_op jit(solution)/shard_map/pairs_1/pallas_call | solution.py:271
  28.2 6.5 %collective-permute-done.3.side_ref.refs_5_ = bf16[528,1024]{1,0:T(8,128)(2,1)S(1)} collective-permute-done((bf16[528,1024]{1,0:T(8,128)(2,1)S(1)}, bf16[528,1024]{1,0:T(8,128)(2,1)S(1)}, u32[]{:S(2)}, u32[]{:S(2)}) %collective-permute-start.3) | collective-permute-done | bytes 1081376 | tf_op jit(solution)/shard_map/ppermute | solution.py:49
  34.7 1.0 %pick.1 = bf16[528,1024]{1,0:T(8,128)(2,1)S(1)} custom-call(s32[28]{0:T(128)S(1)} %dynamic-slice_bitcast_fusion.tab_ref, bf16[528,1024]{1,0:T(8,128)(2,1)S(1)} %unit.1.own_ref.refs_1_.refs_2_.refs_4_, bf16[528,1024]{1,0:T(8,128)(2,1)S(1)} %collective-permute-done.3.side_ref.refs_5_), custom_call_target="tpu_custom_call" | custom-call | tf_op jit(solution)/shard_map/pick/pallas_call | solution.py:307
  35.8 0.5 collective-permute-start.10
  36.3 0.4 collective-permute-done.4.refs_0_.refs_1_
  36.7 0.0 collective-permute-done.5.refs_4_
  36.7 3.9 %pairs_2.1.before_ref = f32[16,128]{1,0:T(8,128)S(1)} custom-call(s32[28]{0:T(128)S(1)} %dynamic-slice_bitcast_fusion.tab_ref, f32[16,128]{1,0:T(8,128)S(1)} %pairs_1.1.before_ref, bf16[528,1024]{1,0:T(8,128)(2,1)S(1)} %collective-permute-done.4.refs_0_.refs_1_, bf16[528,1024]{1,0:T(8,128)(2,1)S(1)} %collective-permute-done.1.refs_0_.refs_1_, ...), custom_call_target="tpu_custom_call" | custom-call | flops 4294967296 | bytes 7340032 | tf_op jit(solution)/shard_map/pairs_2/pallas_call | solution.py:271
  40.7 0.1 collective-permute-start.7
  40.9 0.8 %collective-permute-start.6 = (bf16[256,1024]{1,0:T(8,128)(2,1)S(1)}, bf16[256,1024]{1,0:T(8,128)(2,1)S(1)}, u32[]{:S(2)}, u32[]{:S(2)}) collective-permute-start(bf16[256,1024]{1,0:T(8,128)(2,1)S(1)} %slice.30), channel_id=1, source_target_pairs={{0,1},{1,0},{2,3},{3,2},{4,5},{5,4},{6,7},{7,6},{8,9},{9,8},{10,11... | collective-permute-start | bytes 1572872 | tf_op jit(solution)/shard_map/ppermute | solution.py:53
  41.6 0.0 collective-permute-done.8.refs_4_
  41.6 1.9 %collective-permute-done.6.refs_2_ = bf16[256,1024]{1,0:T(8,128)(2,1)S(1)} collective-permute-done((bf16[256,1024]{1,0:T(8,128)(2,1)S(1)}, bf16[256,1024]{1,0:T(8,128)(2,1)S(1)}, u32[]{:S(2)}, u32[]{:S(2)}) %collective-permute-start.6) | collective-permute-done | bytes 524320 | tf_op jit(solution)/shard_map/ppermute | solution.py:53
  43.5 0.0 collective-permute-done.7.refs_3_
  43.5 2.4 %pairs_3.1 = (f32[16,128]{1,0:T(8,128)S(1)}, bf16[528,1024]{1,0:T(8,128)(2,1)S(1)}) custom-call(s32[28]{0:T(128)S(1)} %dynamic-slice_bitcast_fusion.tab_ref, f32[16,128]{1,0:T(8,128)S(1)} %pairs_2.1.before_ref, bf16[528,1024]{1,0:T(8,128)(2,1)S(1)} %collective-permute-done.4.refs_0_.refs_1_, bf16[528,1024]{1,0:T(8,128)(2,1)S(1)} %collective-permute-done.1.refs_0_.refs_1_, ...), custom_call_target="tpu_custom_call" | custom-call | tf_op jit(solution)/shard_map/pairs_3/pallas_call | solution.py:271
  45.9 0.3 collective-permute-start.9
  46.1 3.0 %collective-permute-start.11 = (f32[16,128]{1,0:T(8,128)S(1)}, f32[16,128]{1,0:T(8,128)S(1)}, u32[]{:S(2)}, u32[]{:S(2)}) collective-permute-start(f32[16,128]{1,0:T(8,128)S(1)} %pairs_2.1.before_ref), channel_id=1, source_target_pairs={{0,24},{1,7},{8,16},{3,5},{16,8},{5,3},{24,0},{7,1},{2,26},{9,15},... | collective-permute-start | bytes 24584 | tf_op jit(solution)/shard_map/ppermute | solution.py:49
  49.2 0.0 collective-permute-done.9.refs_0_
  49.2 1.8 %collective-permute-done.10.refs_3_ = bf16[528,1024]{1,0:T(8,128)(2,1)S(1)} collective-permute-done((bf16[528,1024]{1,0:T(8,128)(2,1)S(1)}, bf16[528,1024]{1,0:T(8,128)(2,1)S(1)}, u32[]{:S(2)}, u32[]{:S(2)}) %collective-permute-start.10) | collective-permute-done | bytes 1081376 | tf_op jit(solution)/shard_map/ppermute | solution.py:49
  51.0 3.1 %pairs_4.1 = (f32[8,128]{1,0:T(8,128)S(1)}, f32[8,128]{1,0:T(8,128)S(1)}, f32[8,128]{1,0:T(8,128)S(1)}, f32[8,128]{1,0:T(8,128)S(1)}, f32[8,128]{1,0:T(8,128)S(1)}) custom-call(s32[28]{0:T(128)S(1)} %dynamic-slice_bitcast_fusion.tab_ref, f32[16,128]{1,0:T(8,128)S(1)} %get-tuple-element.19.before_ref, f32[16,128]{1,0:T(8,128)S(1)} %collective-permute-done.9.refs_0_, ...), custom_call_target="tpu_custom_call" | custom-call | tf_op jit(solution)/shard_map/pairs_4/pallas_call | solution.py:271
  54.1 2.1 %collective-permute-start.12 = (f32[8,128]{1,0:T(8,128)S(1)}, f32[8,128]{1,0:T(8,128)S(1)}, u32[]{:S(2)}, u32[]{:S(2)}) collective-permute-start(f32[8,128]{1,0:T(8,128)S(1)} %get-tuple-element.22), channel_id=1, source_target_pairs={{0,2},{1,9},{8,10},{3,11},{16,18},{5,13},{24,26},{7,15},{2,0},{9,1... | collective-permute-start | bytes 12296 | tf_op jit(solution)/shard_map/ppermute | solution.py:44
  56.2 2.5 %collective-permute-start.13 = (f32[8,128]{1,0:T(8,128)S(1)}, f32[8,128]{1,0:T(8,128)S(1)}, u32[]{:S(2)}, u32[]{:S(2)}) collective-permute-start(f32[8,128]{1,0:T(8,128)S(1)} %get-tuple-element.23), channel_id=1, source_target_pairs={{0,6},{1,25},{8,14},{3,27},{16,22},{5,29},{24,30},{7,31},{2,4},{9,... | collective-permute-start | bytes 12296 | tf_op jit(solution)/shard_map/ppermute | solution.py:44
  58.7 1.1 %collective-permute-start.14 = (f32[8,128]{1,0:T(8,128)S(1)}, f32[8,128]{1,0:T(8,128)S(1)}, u32[]{:S(2)}, u32[]{:S(2)}) collective-permute-start(f32[8,128]{1,0:T(8,128)S(1)} %get-tuple-element.24), channel_id=1, source_target_pairs={{0,4},{1,17},{8,12},{3,19},{16,20},{5,21},{24,28},{7,23},{2,6},{9,... | collective-permute-start | bytes 12296 | tf_op jit(solution)/shard_map/ppermute | solution.py:44
  59.7 2.5 %collective-permute-start.15 = (f32[8,128]{1,0:T(8,128)S(1)}, f32[8,128]{1,0:T(8,128)S(1)}, u32[]{:S(2)}, u32[]{:S(2)}) collective-permute-start(f32[8,128]{1,0:T(8,128)S(1)} %get-tuple-element.25), channel_id=1, source_target_pairs={{0,16},{1,5},{8,0},{3,1},{16,24},{5,7},{24,8},{7,3},{2,18},{9,13},... | collective-permute-start | bytes 12296 | tf_op jit(solution)/shard_map/ppermute | solution.py:49
  62.2 0.0 collective-permute-done.11
  62.2 0.0 collective-permute-done.12
  62.2 0.0 collective-permute-done.13
  62.2 1.6 %collective-permute-done.14 = f32[8,128]{1,0:T(8,128)S(1)} collective-permute-done((f32[8,128]{1,0:T(8,128)S(1)}, f32[8,128]{1,0:T(8,128)S(1)}, u32[]{:S(2)}, u32[]{:S(2)}) %collective-permute-start.14) | collective-permute-done | bytes 4128 | tf_op jit(solution)/shard_map/ppermute | solution.py:44
  63.8 0.0 collective-permute-done.15
  63.8 1.1 %fusion = (f32[]{:T(128)}, f32[1,32]{1,0:T(1,128)}) fusion(f32[1,128]{1,0:T(1,128)S(1)} %slice_add_fusion.1, s32[]{:T(128)} %axis_index.12), kind=kLoop, calls=%fused_computation.1 | loop fusion | flops 127 | bytes 392 | tf_op jit(solution)/shard_map/reduce_sum | solution.py:352
  (3 shorter events, 0.1 us)
Async XLA Ops:
  1.3 1.2 %copy-start = (bf16[1,512,1024]{2,1,0:T(8,128)(2,1)S(1)}, bf16[1,512,1024]{2,1,0:T(8,128)(2,1)}, u32[]{:S(2)}) copy-start(bf16[1,512,1024]{2,1,0:T(8,128)(2,1)} %emb_ref.1) | copy-start | bytes 3145732
  3.1 15.2 %collective-permute-start.1 = (bf16[528,1024]{1,0:T(8,128)(2,1)S(1)}, bf16[528,1024]{1,0:T(8,128)(2,1)S(1)}, u32[]{:S(2)}, u32[]{:S(2)}) collective-permute-start(bf16[528,1024]{1,0:T(8,128)(2,1)S(1)} %unit.1.own_ref.refs_1_.refs_2_.refs_4_), channel_id=1, source_target_pairs={{0,2},{1,9},{8,10},{3,11},{16,18},{5,13},{24,26},{7,15},{2,0},{9,1... | collective-permute-start | bytes 3244040 | tf_op jit(solution)/shard_map/ppermute | solution.py:44
  5.2 16.4 %collective-permute-start.2 = (bf16[528,1024]{1,0:T(8,128)(2,1)S(1)}, bf16[528,1024]{1,0:T(8,128)(2,1)S(1)}, u32[]{:S(2)}, u32[]{:S(2)}) collective-permute-start(bf16[528,1024]{1,0:T(8,128)(2,1)S(1)} %unit.1.own_ref.refs_1_.refs_2_.refs_4_), channel_id=1, source_target_pairs={{0,6},{1,25},{8,14},{3,27},{16,22},{5,29},{24,30},{7,31},{2,4},{9,... | collective-permute-start | bytes 3244040 | tf_op jit(solution)/shard_map/ppermute | solution.py:44
  8.4 15.5 %collective-permute-start = (bf16[528,1024]{1,0:T(8,128)(2,1)S(1)}, bf16[528,1024]{1,0:T(8,128)(2,1)S(1)}, u32[]{:S(2)}, u32[]{:S(2)}) collective-permute-start(bf16[528,1024]{1,0:T(8,128)(2,1)S(1)} %unit.1.own_ref.refs_1_.refs_2_.refs_4_), channel_id=1, source_target_pairs={{0,1},{1,0},{2,3},{3,2},{4,5},{5,4},{6,7},{7,6},{8,9},{9,8},{10,11... | collective-permute-start | bytes 3244040 | tf_op jit(solution)/shard_map/ppermute | solution.py:53
  18.4 16.4 %collective-permute-start.3 = (bf16[528,1024]{1,0:T(8,128)(2,1)S(1)}, bf16[528,1024]{1,0:T(8,128)(2,1)S(1)}, u32[]{:S(2)}, u32[]{:S(2)}) collective-permute-start(bf16[528,1024]{1,0:T(8,128)(2,1)S(1)} %unit.1.own_ref.refs_1_.refs_2_.refs_4_), channel_id=1, source_target_pairs={{0,24},{1,7},{8,16},{3,5},{16,8},{5,3},{24,0},{7,1},{2,26},{9,15},... | collective-permute-start | bytes 3244040 | tf_op jit(solution)/shard_map/ppermute | solution.py:49
  21.6 15.2 %collective-permute-start.4 = (bf16[528,1024]{1,0:T(8,128)(2,1)S(1)}, bf16[528,1024]{1,0:T(8,128)(2,1)S(1)}, u32[]{:S(2)}, u32[]{:S(2)}) collective-permute-start(bf16[528,1024]{1,0:T(8,128)(2,1)S(1)} %collective-permute-done.2.refs_3_.refs_6_.refs_5_), channel_id=1, source_target_pairs={{0,2},{1,9},{8,10},{3,11},{16,18},{5,13},{24,26},{7,15},{2,0},{9,1... | collective-permute-start | bytes 3244040 | tf_op jit(solution)/shard_map/ppermute | solution.py:44
  23.4 13.3 %collective-permute-start.5 = (bf16[528,1024]{1,0:T(8,128)(2,1)S(1)}, bf16[528,1024]{1,0:T(8,128)(2,1)S(1)}, u32[]{:S(2)}, u32[]{:S(2)}) collective-permute-start(bf16[528,1024]{1,0:T(8,128)(2,1)S(1)} %collective-permute-done.1.refs_0_.refs_1_), channel_id=1, source_target_pairs={{0,1},{1,0},{2,3},{3,2},{4,5},{5,4},{6,7},{7,6},{8,9},{9,8},{10,11... | collective-permute-start | bytes 3244040 | tf_op jit(solution)/shard_map/ppermute | solution.py:53
  23.4 18.2 %collective-permute-start.8 = (bf16[528,1024]{1,0:T(8,128)(2,1)S(1)}, bf16[528,1024]{1,0:T(8,128)(2,1)S(1)}, u32[]{:S(2)}, u32[]{:S(2)}) collective-permute-start(bf16[528,1024]{1,0:T(8,128)(2,1)S(1)} %collective-permute-done.2.refs_3_.refs_6_.refs_5_), channel_id=1, source_target_pairs={{0,1},{1,0},{2,3},{3,2},{4,5},{5,4},{6,7},{7,6},{8,9},{9,8},{10,11... | collective-permute-start | bytes 3244040 | tf_op jit(solution)/shard_map/ppermute | solution.py:53
  35.8 15.2 %collective-permute-start.10 = (bf16[528,1024]{1,0:T(8,128)(2,1)S(1)}, bf16[528,1024]{1,0:T(8,128)(2,1)S(1)}, u32[]{:S(2)}, u32[]{:S(2)}) collective-permute-start(bf16[528,1024]{1,0:T(8,128)(2,1)S(1)} %pick.1), channel_id=1, source_target_pairs={{0,8},{1,3},{8,0},{3,1},{16,24},{5,7},{24,16},{7,5},{2,10},{9,11},... | collective-permute-start | bytes 3244040 | tf_op jit(solution)/shard_map/ppermute | solution.py:49
  40.7 2.8 %collective-permute-start.7 = (bf16[272,1024]{1,0:T(8,128)(2,1)S(1)}, bf16[272,1024]{1,0:T(8,128)(2,1)S(1)}, u32[]{:S(2)}, u32[]{:S(2)}) collective-permute-start(bf16[272,1024]{1,0:T(8,128)(2,1)S(1)} %slice.31), channel_id=1, source_target_pairs={{0,1},{1,0},{2,3},{3,2},{4,5},{5,4},{6,7},{7,6},{8,9},{9,8},{10,11... | collective-permute-start | bytes 1671176 | tf_op jit(solution)/shard_map/ppermute | solution.py:53
  40.9 2.6 %collective-permute-start.6 = (bf16[256,1024]{1,0:T(8,128)(2,1)S(1)}, bf16[256,1024]{1,0:T(8,128)(2,1)S(1)}, u32[]{:S(2)}, u32[]{:S(2)}) collective-permute-start(bf16[256,1024]{1,0:T(8,128)(2,1)S(1)} %slice.30), channel_id=1, source_target_pairs={{0,1},{1,0},{2,3},{3,2},{4,5},{5,4},{6,7},{7,6},{8,9},{9,8},{10,11... | collective-permute-start | bytes 1572872 | tf_op jit(solution)/shard_map/ppermute | solution.py:53
  45.9 3.3 %collective-permute-start.9 = (f32[16,128]{1,0:T(8,128)S(1)}, f32[16,128]{1,0:T(8,128)S(1)}, u32[]{:S(2)}, u32[]{:S(2)}) collective-permute-start(f32[16,128]{1,0:T(8,128)S(1)} %get-tuple-element.19.before_ref), channel_id=1, source_target_pairs={{0,1},{1,0},{2,3},{3,2},{4,5},{5,4},{6,7},{7,6},{8,9},{9,8},{10,11... | collective-permute-start | bytes 24584 | tf_op jit(solution)/shard_map/ppermute | solution.py:53
  46.1 16.0 %collective-permute-start.11 = (f32[16,128]{1,0:T(8,128)S(1)}, f32[16,128]{1,0:T(8,128)S(1)}, u32[]{:S(2)}, u32[]{:S(2)}) collective-permute-start(f32[16,128]{1,0:T(8,128)S(1)} %pairs_2.1.before_ref), channel_id=1, source_target_pairs={{0,24},{1,7},{8,16},{3,5},{16,8},{5,3},{24,0},{7,1},{2,26},{9,15},... | collective-permute-start | bytes 24584 | tf_op jit(solution)/shard_map/ppermute | solution.py:49
  54.1 8.1 %collective-permute-start.12 = (f32[8,128]{1,0:T(8,128)S(1)}, f32[8,128]{1,0:T(8,128)S(1)}, u32[]{:S(2)}, u32[]{:S(2)}) collective-permute-start(f32[8,128]{1,0:T(8,128)S(1)} %get-tuple-element.22), channel_id=1, source_target_pairs={{0,2},{1,9},{8,10},{3,11},{16,18},{5,13},{24,26},{7,15},{2,0},{9,1... | collective-permute-start | bytes 12296 | tf_op jit(solution)/shard_map/ppermute | solution.py:44
  56.2 6.1 %collective-permute-start.13 = (f32[8,128]{1,0:T(8,128)S(1)}, f32[8,128]{1,0:T(8,128)S(1)}, u32[]{:S(2)}, u32[]{:S(2)}) collective-permute-start(f32[8,128]{1,0:T(8,128)S(1)} %get-tuple-element.23), channel_id=1, source_target_pairs={{0,6},{1,25},{8,14},{3,27},{16,22},{5,29},{24,30},{7,31},{2,4},{9,... | collective-permute-start | bytes 12296 | tf_op jit(solution)/shard_map/ppermute | solution.py:44
  58.7 5.1 %collective-permute-start.14 = (f32[8,128]{1,0:T(8,128)S(1)}, f32[8,128]{1,0:T(8,128)S(1)}, u32[]{:S(2)}, u32[]{:S(2)}) collective-permute-start(f32[8,128]{1,0:T(8,128)S(1)} %get-tuple-element.24), channel_id=1, source_target_pairs={{0,4},{1,17},{8,12},{3,19},{16,20},{5,21},{24,28},{7,23},{2,6},{9,... | collective-permute-start | bytes 12296 | tf_op jit(solution)/shard_map/ppermute | solution.py:44
  59.7 4.1 %collective-permute-start.15 = (f32[8,128]{1,0:T(8,128)S(1)}, f32[8,128]{1,0:T(8,128)S(1)}, u32[]{:S(2)}, u32[]{:S(2)}) collective-permute-start(f32[8,128]{1,0:T(8,128)S(1)} %get-tuple-element.25), channel_id=1, source_target_pairs={{0,16},{1,5},{8,0},{3,1},{16,24},{5,7},{24,8},{7,3},{2,18},{9,13},... | collective-permute-start | bytes 12296 | tf_op jit(solution)/shard_map/ppermute | solution.py:49
